TPU v7x, 32 devices: a whole 2x2x4 slice. The times are simulated.
32 devices in a mesh: img: 8 (over y, x, core), head: 4 (over z).
Axes of the slice: x: 2, y: 2, z: 4, core: 2. Of those that a mesh axis runs over, the one named last changes fastest.
Arguments:
- tokens: bfloat16 [50176, 256], P(('img', 'head')), may hold values from -6 to 6
- image_sides: int32 [8, 32], P('img'), may hold values from 0 to 4, as said below
- qkv_weight: bfloat16 [3, 256, 256], P(None, None, 'head'), may hold values from -0.375 to 0.375
- proj_weight: bfloat16 [256, 256], P('head'), may hold values from -1.5 to 1.5
- proj_bias: float32 [256], replicated, may hold values from -3 to 3
- fc_in: bfloat16 [1024, 256], P(('img', 'head')), may hold values from -0.375 to 0.375
- fc_in_bias: float32 [1024], replicated, may hold values from -3 to 3
- fc_out: bfloat16 [1024, 256], P(('img', 'head')), may hold values from -0.375 to 0.375
- fc_out_bias: float32 [256], replicated, may hold values from -3 to 3
- norm_gains: float32 [2, 256], replicated, may hold values from 0.5 to 1.5
- norm_shifts: float32 [2, 256], replicated, may hold values from -2 to 2
- peg_weight: float32 [9, 256], replicated, may hold values from -2 to 2
- peg_bias: float32 [256], replicated, may hold values from -3 to 3
- out_grad: bfloat16 [50176, 256], P(('img', 'head')), may hold values from -6 to 6
Outputs:
- output: bfloat16 [50176, 256], P(('img', 'head'))
- d_tokens: float32 [50176, 256], P(('img', 'head'))
- d_qkv_weight: float32 [3, 256, 256], P(None, None, 'head')
- d_proj_weight: float32 [256, 256], P('head')
- d_proj_bias: float32 [256], replicated
- d_fc_in: float32 [1024, 256], P(('img', 'head'))
- d_fc_in_bias: float32 [1024], replicated
- d_fc_out: float32 [1024, 256], P(('img', 'head'))
- d_fc_out_bias: float32 [256], replicated
- d_norm_gains: float32 [2, 256], replicated
- d_norm_shifts: float32 [2, 256], replicated
- d_peg_weight: float32 [9, 256], replicated
- d_peg_bias: float32 [256], replicated
Inputs may be any that keep to these rules, and one draw needn't show every extreme that they name: `image_sides`: each row lists one group's images in slot order, each of side 2, 3 or 4 windows; a 0 marks an unused slot and only follows used ones. The squared sides of a row add up to at most 128, and in some row to exactly 128.
All inputs are finite; a program needn't handle non-finite values.
Results may differ from a plain program's by a relative error of at most 0.017.
Values may be sent and summed in bfloat16 or wider, within the bound.
A program may use at most 192 MiB of HBM per device.

v0:
```python
import jax
import jax.numpy as jnp
from jax import lax
from jax.sharding import PartitionSpec as P

HDIM = 32
WS = 7


def layout(side_table, windows):
    window_areas = side_table * side_table
    finish = jnp.cumsum(window_areas)
    starts = finish - window_areas
    window_ids = jnp.arange(windows, dtype=jnp.int32)
    holding = (
        (window_ids[:, None] >= starts[None, :]) & (window_ids[:, None] < finish[None, :])
    ).astype(jnp.int32)
    image_side = jnp.sum(holding * side_table[None, :], axis=1)
    image_start = jnp.sum(holding * starts[None, :], axis=1)
    grid_size = jnp.where(
        image_side == 2, 14, jnp.where(image_side == 3, 18, jnp.where(image_side == 4, 24, 0))
    ).astype(jnp.int32)
    place_id = window_ids - image_start
    across = jnp.maximum(image_side, 1)
    window_row = place_id // across
    window_col = place_id % across
    cell_ids = jnp.arange(WS * WS, dtype=jnp.int32)
    patch_row = window_row[:, None] * WS + cell_ids[None, :] // WS
    patch_col = window_col[:, None] * WS + cell_ids[None, :] % WS
    grid_limit = grid_size[:, None]
    valid_mask = (patch_row < grid_limit) & (patch_col < grid_limit)
    inside_list = []
    for shift_row in (-1, 0, 1):
        for shift_col in (-1, 0, 1):
            near_row = patch_row + shift_row
            near_col = patch_col + shift_col
            in_grid = (
                valid_mask
                & (near_row >= 0)
                & (near_row < grid_limit)
                & (near_col >= 0)
                & (near_col < grid_limit)
            )
            inside_list.append(in_grid.reshape(-1).astype(jnp.float32))
    return (valid_mask.reshape(-1).astype(jnp.float32), across, jnp.stack(inside_list))


def near_tiles(ext_rows, margin, windows, across):
    width = ext_rows.shape[-1]
    blocks = ext_rows.reshape(-1, WS, WS, width)
    select = across.reshape(windows, 1, 1, 1)

    def piece(step_row, step_col, row_cut, col_cut):

        def cut(offset):
            return blocks[margin + offset : margin + offset + windows, row_cut, col_cut]

        if step_row == 0:
            return cut(step_col)
        return jnp.where(
            select == 2,
            cut(2 * step_row + step_col),
            jnp.where(select == 3, cut(3 * step_row + step_col), cut(4 * step_row + step_col)),
        )

    row_specs = ((-1, slice(WS - 1, WS)), (0, slice(0, WS)), (1, slice(0, 1)))
    col_specs = ((-1, slice(WS - 1, WS)), (0, slice(0, WS)), (1, slice(0, 1)))
    bands = []
    for step_row, row_cut in row_specs:
        bands.append(
            jnp.concatenate(
                [piece(step_row, step_col, row_cut, col_cut) for step_col, col_cut in col_specs],
                axis=2,
            )
        )
    return jnp.concatenate(bands, axis=1)


def tap_rows(tiles, tap_id):
    shift_row = tap_id // 3 - 1
    shift_col = tap_id % 3 - 1
    width = tiles.shape[-1]
    return (
        tiles[:, 1 + shift_row : 1 + shift_row + WS, 1 + shift_col : 1 + shift_col + WS, :]
        .reshape(-1, width)
        .astype(jnp.float32)
    )


def norm_forward(values, gain_vec, shift_vec):
    centre = values - jnp.mean(values, axis=-1, keepdims=True)
    inverse = lax.rsqrt(jnp.mean(centre * centre, axis=-1, keepdims=True) + 1e-06)
    scaled = centre * inverse
    return (scaled * gain_vec + shift_vec, scaled, inverse)


def norm_backward(gradient, scaled, inverse, gain_vec):
    d_scaled = gradient * gain_vec
    d_values = inverse * (
        d_scaled
        - jnp.mean(d_scaled, axis=-1, keepdims=True)
        - scaled * jnp.mean(d_scaled * scaled, axis=-1, keepdims=True)
    )
    return (d_values, jnp.sum(gradient * scaled, axis=0), jnp.sum(gradient, axis=0))


def peg_forward(centre_rows, source_ext, margin, across, inside, valid_mask, peg_weight, peg_bias):
    windows = centre_rows.shape[0] // (WS * WS)
    tiles = near_tiles(source_ext, margin, windows, across)
    mixed_sum = centre_rows.astype(jnp.float32) + peg_bias
    for tap_id in range(9):
        mixed_sum = mixed_sum + inside[tap_id][:, None] * peg_weight[tap_id] * tap_rows(
            tiles, tap_id
        )
    return valid_mask[:, None] * mixed_sum


def peg_backward(d_mixed, d_extended, source_ext, margin, across, inside, peg_weight):
    windows = d_mixed.shape[0] // (WS * WS)
    source_tiles = near_tiles(source_ext, margin, windows, across)
    grad_tiles = near_tiles(d_extended, margin, windows, across)
    d_source = d_mixed
    tap_grads = []
    for tap_id in range(9):
        tap_grads.append(
            jnp.sum(inside[tap_id][:, None] * d_mixed * tap_rows(source_tiles, tap_id), axis=0)
        )
        mirror = 8 - tap_id
        d_source = d_source + inside[mirror][:, None] * peg_weight[tap_id] * tap_rows(
            grad_tiles, mirror
        )
    return (d_source, jnp.stack(tap_grads), jnp.sum(d_mixed, axis=0))


def gelu_exact(values):
    return jax.nn.gelu(values, approximate=False)


def split_parts(qkv_parts, row_count, col_count):
    windows = row_count // (WS * WS)
    return qkv_parts.reshape(3, windows, WS * WS, col_count // HDIM, HDIM)


def window_scores(shaped, key_bias):
    windows = shaped.shape[1]
    scores = jnp.einsum(
        "wqhe,wkhe->whqk", shaped[0], shaped[1], preferred_element_type=jnp.float32
    ) * HDIM ** (-0.5)
    return scores + key_bias.reshape(windows, 1, 1, WS * WS)


def attend(normed, weight, key_bias):
    row_count = normed.shape[0]
    col_count = weight.shape[2]
    projected = jnp.einsum("rd,tdc->trc", normed, weight, preferred_element_type=jnp.float32)
    qkv_parts = projected.astype(jnp.bfloat16)
    shaped = split_parts(qkv_parts, row_count, col_count)
    scores = window_scores(shaped, key_bias)
    top_score = jnp.max(scores, axis=-1, keepdims=True)
    exponent = jnp.exp(scores - top_score)
    row_total = jnp.sum(exponent, axis=-1, keepdims=True)
    log_total = top_score + jnp.log(row_total)
    prob_low = (exponent / row_total).astype(jnp.bfloat16)
    context = jnp.einsum("whqk,wkhe->wqhe", prob_low, shaped[2], preferred_element_type=jnp.float32)
    return (qkv_parts, context.reshape(row_count, col_count).astype(jnp.bfloat16), log_total)


def attend_back(normed, weight, qkv_parts, log_total, key_bias, d_context):
    row_count = normed.shape[0]
    col_count = weight.shape[2]
    shaped = split_parts(qkv_parts, row_count, col_count)
    probs_full = jnp.exp(window_scores(shaped, key_bias) - log_total)
    prob_low = probs_full.astype(jnp.bfloat16)
    d_shaped = d_context.reshape(shaped.shape[1:])
    d_value = jnp.einsum("whqk,wqhe->wkhe", prob_low, d_shaped, preferred_element_type=jnp.float32)
    d_prob = jnp.einsum("wqhe,wkhe->whqk", d_shaped, shaped[2], preferred_element_type=jnp.float32)
    d_score = probs_full * (d_prob - jnp.sum(d_prob * probs_full, axis=-1, keepdims=True))
    d_score = d_score.astype(jnp.bfloat16)
    d_query = jnp.einsum(
        "whqk,wkhe->wqhe", d_score, shaped[1], preferred_element_type=jnp.float32
    ) * HDIM ** (-0.5)
    d_key = jnp.einsum(
        "whqk,wqhe->wkhe", d_score, shaped[0], preferred_element_type=jnp.float32
    ) * HDIM ** (-0.5)
    d_parts = (
        jnp.stack([d_query, d_key, d_value]).reshape(3, row_count, col_count).astype(jnp.bfloat16)
    )
    d_weight = jnp.einsum("trc,rd->tdc", d_parts, normed, preferred_element_type=jnp.float32)
    d_normed = jnp.einsum("trc,tdc->rd", d_parts, weight, preferred_element_type=jnp.float32)
    return (d_weight, d_normed)


def on_device(
    tokens,
    image_sides,
    qkv_weight,
    proj_weight,
    proj_bias,
    fc_in,
    fc_in_bias,
    fc_out,
    fc_out_bias,
    norm_gains,
    norm_shifts,
    peg_weight,
    peg_bias,
    out_grad,
):
    own_rows = tokens.shape[0]
    first_row = lax.axis_index("head") * own_rows
    group_rows = own_rows * lax.axis_size("head")
    margin = 5
    reach = margin * WS * WS
    valid_mask, across, inside = layout(image_sides[0], group_rows // (WS * WS))
    own_valid = lax.dynamic_slice_in_dim(valid_mask, first_row, own_rows, 0)
    key_bias = (valid_mask - 1.0) * 1000000000.0
    fc_in_all, fc_out_all = (
        lax.all_gather(fc_in, ("img", "head"), axis=0, tiled=True),
        lax.all_gather(fc_out, ("img", "head"), axis=0, tiled=True),
    )
    gathered = lax.all_gather(tokens, "head", axis=0, tiled=True)
    padded_source = jnp.pad(gathered, ((reach, reach), (0, 0)))
    field_all = peg_forward(
        gathered, padded_source, margin, across, inside, valid_mask, peg_weight, peg_bias
    )
    normed, scaled_one, inverse_one = norm_forward(field_all, norm_gains[0], norm_shifts[0])
    normed = normed.astype(jnp.bfloat16)
    qkv_parts, context, log_total = attend(normed, qkv_weight, key_bias)
    branch = (
        lax.psum_scatter(
            jnp.dot(context, proj_weight, preferred_element_type=jnp.float32).astype(jnp.bfloat16),
            "head",
            scatter_dimension=0,
            tiled=True,
        ).astype(jnp.float32)
        + proj_bias
    )
    field = lax.dynamic_slice_in_dim(field_all, first_row, own_rows, 0)
    hidden_in = field + branch
    normed_two, scaled_two, inverse_two = norm_forward(hidden_in, norm_gains[1], norm_shifts[1])
    normed_two = normed_two.astype(jnp.bfloat16)
    pre_act = (
        jnp.einsum("rd,fd->rf", normed_two, fc_in_all, preferred_element_type=jnp.float32)
        + fc_in_bias
    )
    active, gelu_pull = jax.vjp(gelu_exact, pre_act)
    active = active.astype(jnp.bfloat16)
    result = jnp.dot(active, fc_out_all, preferred_element_type=jnp.float32) + fc_out_bias
    output = (own_valid[:, None] * (hidden_in + result)).astype(jnp.bfloat16)
    d_output = own_valid[:, None] * out_grad.astype(jnp.float32)
    d_result = d_output.astype(jnp.bfloat16)
    d_fc_out = jnp.einsum("rf,rd->fd", active, d_result, preferred_element_type=jnp.float32)
    d_fc_out_bias = jnp.sum(d_output, axis=0)
    d_active = jnp.einsum("rd,fd->rf", d_result, fc_out_all, preferred_element_type=jnp.float32)
    d_pre = gelu_pull(d_active)[0].astype(jnp.bfloat16)
    d_fc_in_bias = jnp.sum(d_pre.astype(jnp.float32), axis=0)
    d_fc_in = jnp.einsum("rf,rd->fd", d_pre, normed_two, preferred_element_type=jnp.float32)
    d_normed_two = jnp.dot(d_pre, fc_in_all, preferred_element_type=jnp.float32)
    d_hidden_norm, gain_two, shift_two = norm_backward(
        d_normed_two, scaled_two, inverse_two, norm_gains[1]
    )
    d_hidden = d_output + d_hidden_norm
    d_branch = d_hidden.astype(jnp.bfloat16)
    d_proj_bias = jnp.sum(d_branch.astype(jnp.float32), axis=0)
    d_branch_all = lax.all_gather(d_branch, "head", axis=0, tiled=True)
    d_proj = jnp.einsum("rc,rd->cd", context, d_branch_all, preferred_element_type=jnp.float32)
    d_context = jnp.einsum(
        "rd,cd->rc", d_branch_all, proj_weight, preferred_element_type=jnp.float32
    ).astype(jnp.bfloat16)
    d_qkv, d_normed = attend_back(normed, qkv_weight, qkv_parts, log_total, key_bias, d_context)
    d_field, gain_one, shift_one = norm_backward(d_normed, scaled_one, inverse_one, norm_gains[0])
    own_part = lax.dynamic_slice_in_dim(d_field, first_row, own_rows, 0) + d_hidden
    d_field_all = lax.dynamic_update_slice_in_dim(d_field, own_part, first_row, 0)
    d_mixed_all = valid_mask[:, None] * d_field_all
    d_padded = jnp.pad(d_mixed_all, ((reach, reach), (0, 0)))
    d_source, d_peg_weight, d_peg_bias = peg_backward(
        d_mixed_all, d_padded, padded_source, margin, across, inside, peg_weight
    )
    d_tokens = lax.psum_scatter(
        d_source.astype(jnp.bfloat16), "head", scatter_dimension=0, tiled=True
    ).astype(jnp.float32)
    d_qkv, d_proj = lax.psum((d_qkv, d_proj), "img")
    d_fc_in, d_fc_out = (
        lax.psum_scatter(d_fc_in, ("img", "head"), scatter_dimension=0, tiled=True),
        lax.psum_scatter(d_fc_out, ("img", "head"), scatter_dimension=0, tiled=True),
    )
    small_sums = lax.psum(
        (
            d_proj_bias,
            d_fc_in_bias,
            d_fc_out_bias,
            jnp.stack([gain_one, gain_two]),
            jnp.stack([shift_one, shift_two]),
            d_peg_weight,
            d_peg_bias,
        ),
        ("img", "head"),
    )
    return (
        output,
        d_tokens,
        d_qkv,
        d_proj,
        small_sums[0],
        d_fc_in,
        small_sums[1],
        d_fc_out,
        small_sums[2],
        small_sums[3],
        small_sums[4],
        small_sums[5],
        small_sums[6],
    )


def solution(mesh):
    placed = (
        P(("img", "head"), None),
        P("img", None),
        P(None, None, "head"),
        P("head", None),
        P(),
        P(("img", "head"), None),
        P(),
        P(("img", "head"), None),
        P(),
        P(),
        P(),
        P(),
        P(),
        P(("img", "head"), None),
    )
    return jax.shard_map(
        on_device,
        mesh=mesh,
        in_specs=placed,
        out_specs=(
            P(("img", "head"), None),
            P(("img", "head"), None),
            P(None, None, "head"),
            P("head", None),
            P(),
            P(("img", "head"), None),
            P(),
            P(("img", "head"), None),
            P(),
            P(),
            P(),
            P(),
            P(),
        ),
        check_vma=False,
    )
```

profile of v0, /device:TPU:0, one launch (start us, length us, event | category | flops | bytes accessed | tf_op | source)
XLA Modules:
  0.0 1224.1 jit_solution(10091184480915722815)
XLA Ops:
  19.0 57.9 %all-gather.3.cloned.1.call-done = bf16[6272,256]{1,0:T(8,128)(2,1)} async-done(((bf16[1568,256]{1,0:T(8,128)(2,1)}), bf16[6272,256]{1,0:T(8,128)(2,1)}) %all-gather.3.cloned.1.call-update) | async-done | bytes 3211280 | tf_op jit(solution)/shard_map/all_gather | solution.py:221
  104.6 10.1 fusion.28
  122.5 8.0 reshape.736
  130.5 12.7 %maximum_maximum_fusion.2 = (bf16[128,8,9,256]{3,2,1,0:T(8,128)(2,1)}, bf16[128,8,9,256]{3,2,1,0:T(8,128)(2,1)}) fusion(bf16[128,7,1,256]{3,2,1,0:T(2,128)(2,1)S(1)} %copy-done.20, bf16[128,7,7,256]{3,2,1,0:T(8,128)(2,1)} %slice.299, bf16[128,7,1,256]{3,2,1,0:T(2,128)(2,1)S(1)} %copy-done.19, bf16[128,1,1,256]{3,2,1,0:T(2,128)(2,1)S(1)} %copy-done.30, ...), kind=kLoop, calls=%fused_computation.9 | loop fusion | flops 56623104 | bytes 14745600 | tf_op jit(solution)/shard_map/concatenate | solution.py:76
  143.2 23.7 %slice_convert_fusion.2 = (f32[128,7,7,256]{3,2,1,0:T(8,128)}, f32[128,7,7,256]{3,2,1,0:T(8,128)}, f32[128,7,7,256]{3,2,1,0:T(8,128)}, f32[128,7,7,256]{3,2,1,0:...) fusion(bf16[128,8,9,256]{3,2,1,0:T(8,128)(2,1)} %get-tuple-element.93, ...), kind=kLoop, calls=%fused_computation.76 | loop fusion | flops 9633792 | bytes 57802752 | tf_op jit(solution)/shard_map/convert_element_type | solution.py:86
  166.9 7.8 reshape.737
  182.5 7.8 reshape.738
  206.1 7.8 reshape.732
  214.1 20.0 %fusion.69 = (f32[6272]{0:T(1024)S(1)}, f32[6272,256]{1,0:T(8,128)S(1)}) fusion(f32[6272,256]{1,0:T(8,128)} %reshape.739, f32[256]{0:T(256)S(1)} %bitcast.133, f32[6272]{0:T(1024)S(1)} %copy-done.47, f32[6272,256]{1,0:T(8,128)} %reshape.738, f32[256]{0:T(256)S(1)} %bitcast.135, f32[6272]{0:T(1024)S(1)} %copy-done.50, f32[6272,256]{1,0:T(8,128)} %reshape.737, ...), kind=kLoop, calls=%fused_computation.206 | loop fusion | flops 49768320 | bytes 61300224 | tf_op jit(solution)/shard_map/reduce_sum | solution.py:91
  263.9 8.8 fusion.80
  287.8 79.3 %all_gather.13 = bf16[1024,256]{1,0:T(8,128)(2,1)S(1)} all-gather(bf16[32,256]{1,0:T(8,128)(2,1)S(1)} %copy-done.71), channel_id=1, replica_groups=mesh['img'=8,'head'=4] {'img','head'}, dimensions={0}, use_global_device_ids=true | all-gather | bytes 540672 | tf_op jit(solution)/shard_map/all_gather | solution.py:218
  367.2 68.3 %all_gather.14 = bf16[1024,256]{1,0:T(8,128)(2,1)S(1)} all-gather(bf16[32,256]{1,0:T(8,128)(2,1)S(1)} %copy-done.72), channel_id=1, replica_groups=mesh['img'=8,'head'=4] {'img','head'}, dimensions={0}, use_global_device_ids=true | all-gather | bytes 540672 | tf_op jit(solution)/shard_map/all_gather | solution.py:219
  438.3 16.6 %multiply_convert_fusion.1 = (bf16[1568,1024]{1,0:T(8,128)(2,1)}, f32[1568,1024]{1,0:T(8,128)S(1)}, f32[1568,1024]{1,0:T(8,128)S(1)}) fusion(f32[1024]{0:T(1024)S(1)} %copy-done.114, bf16[1024,256]{1,0:T(8,128)(2,1)S(1)} %all_gather.13, f32[1568,256]{1,0:T(8,128)S(1)} %get-tuple-element.48, f32[256]{0:T(256)S(1)} %bitcast.154, f32[256]{0:T(256)S(1)} %bitcast.149, ...), kind=kOutput, calls=%fused_computation.52 | convolution fusion | flops 930062336 | bytes 18204928 | tf_op jit(solution)/shard_map/rd,fd->rf/dot_general | solution.py:243
  464.8 61.7 %all-gather.5.cloned.1.call-done = bf16[6272,256]{1,0:T(8,128)(2,1)} async-done(((bf16[1568,256]{1,0:T(8,128)(2,1)}), bf16[6272,256]{1,0:T(8,128)(2,1)}) %all-gather.5.cloned.1.call-update) | async-done | bytes 3211280 | tf_op jit(solution)/shard_map/all_gather | solution.py:265
  545.7 12.6 %multiply_reduce_fusion = (f32[128,2,49]{2,1,0:T(2,128)S(1)}, f32[128,2,49,49]{2,3,1,0:T(8,128)}) fusion(f32[128,2,49,49]{2,3,1,0:T(8,128)S(1)} %bitcast.108, f32[128,2,49]{2,1,0:T(2,128)S(1)} %bitcast.114, bf16[128,49,2,32]{1,0,3,2:T(8,128)(2,1)S(1)} %copy-done.17, bf16[128,49,2,32]{1,0,3,2:T(8,128)(2,1)S(1)} %copy-done.10), kind=kOutput, calls=%fused_computation.15 | convolution fusion | flops 41169408 | bytes 6623232 | tf_op jit(solution)/shard_map/wqhe,wkhe->whqk/dot_general | solution.py:176
  596.2 12.1 multiply_reduce_fusion.9
  608.5 8.3 subtract_multiply_fusion
  619.8 17.2 %fusion.66 = (f32[256]{0:T(256)S(1)}, f32[256]{0:T(256)S(1)}, f32[256]{0:T(256)S(1)}, f32[256]{0:T(256)}, f32[256]{0:T(256)}, /*index=5*/f32[256]{0:T(256)}, f32...) fusion(f32[6272,256]{1,0:T(8,128)} %reshape.739, f32[6272]{0:T(1024)S(1)} %copy-done.48, ...), kind=kLoop, calls=%fused_computation.204 | loop fusion | flops 43349760 | bytes 61249024 | tf_op jit(solution)/shard_map/reduce_sum | solution.py:132
  642.9 8.6 reshape.723
  676.7 12.2 pad_maximum_fusion.1
  688.9 7.8 reshape.727
  704.5 18.8 %maximum_maximum_fusion = (f32[128,8,9,256]{3,2,1,0:T(8,128)}, f32[128,8,9,256]{3,2,1,0:T(8,128)}) fusion(f32[128,1,1,256]{3,2,1,0:T(1,128)S(1)} %get-tuple-element.83, f32[128,1,7,256]{3,2,1,0:T(8,128)S(1)} %get-tuple-element.86, f32[128,1,1,256]{3,2,1,0:T(1,128)S(1)} %get-tuple-element.82, f32[128,7,1,256]{3,2,1,0:T(1,128)S(1)} %get-tuple-element.89, ...), kind=kLoop, calls=%fused_computation | loop fusion | flops 23592960 | bytes 29491200 | tf_op jit(solution)/shard_map/concatenate | solution.py:76
  723.3 17.6 %fusion.72 = (f32[128,7,7,256]{3,2,1,0:T(8,128)}, f32[128,7,7,256]{3,2,1,0:T(8,128)}, f32[128,7,7,256]{3,2,1,0:T(8,128)}) fusion(f32[128,8,9,256]{3,2,1,0:T(8,128)} %get-tuple-element.74), kind=kLoop, calls=%fused_computation.208 | loop fusion | bytes 38535168 | tf_op jit(solution)/shard_map/slice | solution.py:84
  740.9 7.8 reshape.724
  764.3 17.7 %fusion.73 = (f32[128,7,7,256]{3,2,1,0:T(8,128)}, f32[128,7,7,256]{3,2,1,0:T(8,128)}, f32[128,7,7,256]{3,2,1,0:T(8,128)}) fusion(f32[128,8,9,256]{3,2,1,0:T(8,128)} %get-tuple-element.75), kind=kLoop, calls=%fused_computation.209 | loop fusion | bytes 38535168 | tf_op jit(solution)/shard_map/slice | solution.py:84
  782.0 7.8 reshape.729
  797.8 7.9 reshape.730
  805.8 20.0 %fusion.6 = bf16[6272,256]{1,0:T(8,128)(2,1)} fusion(f32[6272,256]{1,0:T(8,128)} %copy-done.2, f32[6272,256]{1,0:T(8,128)} %reshape.731, f32[6272,256]{1,0:T(8,128)} %reshape.730, f32[6272,256]{1,0:T(8,128)} %reshape.729, f32[6272,256]{1,0:T(8,128)} %reshape.728, f32[6272,256]{1,0:T(8,128)} %reshape.727, f32[6272,256]{1,0:T(8,128)} %reshape.726, ...), kind=kLoop, calls=%fused_computation.26 | loop fusion | flops 44957696 | bytes 61249024 | tf_op jit(solution)/shard_map/convert_element_type | solution.py:280
  849.6 43.1 %all-reduce.2 = (f32[256]{0:T(256)}, f32[1024]{0:T(1024)}, f32[256]{0:T(256)}, f32[2,256]{1,0:T(2,128)}, f32[2,256]{1,0:T(2,128)}, /*index=5*/f32[9,256]{1,0:T(8,128)}, f32[256]{0:T(256)}) all-reduce(f32[256]{0:T(256)S(1)} %copy-done.94, f32[1024]{0:T(1024)S(1)} %copy-done.105, ...), channel_id=1, replica_groups=mesh['img'=8,'head'=4] {'img','head'}, use_global_device_ids=true, to_apply=%region_19.20 | all-reduce | flops 5120 | bytes 40960 | tf_op jit(solution)/shard_map/psum | solution.py:287
  895.1 129.9 %reduce-scatter.11.cloned.1.call-done = f32[32,256]{1,0:T(8,128)} async-done(((f32[1024,256]{1,0:T(8,128)}), f32[32,256]{1,0:T(8,128)}) %reduce-scatter.11.cloned.1.call-update) | async-done | bytes 32784 | tf_op jit(solution)/shard_map/reduce_scatter | solution.py:285
  1025.0 134.6 %reduce-scatter.9.cloned.1.call-done = f32[32,256]{1,0:T(8,128)} async-done(((f32[1024,256]{1,0:T(8,128)}), f32[32,256]{1,0:T(8,128)}) %reduce-scatter.9.cloned.1.call-update) | async-done | bytes 32784 | tf_op jit(solution)/shard_map/reduce_scatter | solution.py:284
  1159.7 54.1 %all-reduce.6.cloned.1.call-done = (f32[3,256,64]{1,2,0:T(8,128)}, f32[64,256]{1,0:T(8,128)}) async-done(((f32[3,256,64]{1,2,0:T(8,128)}, f32[64,256]{1,0:T(8,128)}), (f32[3,256,64]{1,2,0:T(8,128)}, f32[64,256]{1,0:T(8,128)})) %all-reduce.6.cloned.1.call-update) | async-done | bytes 262160 | tf_op jit(solution)/shard_map/psum | solution.py:282
  (359 shorter events, 279.1 us)
Async XLA Ops:
  7.2 232.4 %copy-start = (bf16[3,256,64]{1,2,0:T(8,128)(2,1)S(1)}, bf16[3,256,64]{1,2,0:T(8,128)(2,1)}, u32[]{:S(2)}) copy-start(bf16[3,256,64]{1,2,0:T(8,128)(2,1)} %param.16) | copy-start | bytes 294916
  7.2 69.7 %all-gather.3.cloned.1.call-start = ((), (), s32[]{:S(2)}) async-start(), calls=%async_computation.4 | async-start | bytes 4014080 | tf_op jit(solution)/shard_map/all_gather | solution.py:221
  7.9 427.6 %reduce-scatter.5.cloned.1.call-start = ((), (), s32[]{:S(2)}) async-start(), calls=%async_computation.5 | async-start | bytes 4014080 | tf_op jit(solution)/shard_map/reduce_scatter | solution.py:230
  18.2 195.7 %copy-start.33 = (f32[6272]{0:T(1024)}, f32[6272]{0:T(1024)S(1)}, u32[]{:S(2)}) copy-start(f32[6272]{0:T(1024)S(1)} %get-tuple-element.59) | copy-start | bytes 75268
  18.3 195.7 %copy-start.35 = (f32[6272]{0:T(1024)}, f32[6272]{0:T(1024)S(1)}, u32[]{:S(2)}) copy-start(f32[6272]{0:T(1024)S(1)} %get-tuple-element.110) | copy-start | bytes 75268
  18.3 195.6 %copy-start.38 = (f32[6272]{0:T(1024)}, f32[6272]{0:T(1024)S(1)}, u32[]{:S(2)}) copy-start(f32[6272]{0:T(1024)S(1)} %get-tuple-element.64) | copy-start | bytes 75268
  18.3 195.6 %copy-start.41 = (f32[6272]{0:T(1024)}, f32[6272]{0:T(1024)S(1)}, u32[]{:S(2)}) copy-start(f32[6272]{0:T(1024)S(1)} %get-tuple-element.108) | copy-start | bytes 75268
  87.9 14.0 %copy-start.4 = (bf16[6272,256]{1,0:T(8,128)(2,1)S(1)}, bf16[6272,256]{1,0:T(8,128)(2,1)}, u32[]{:S(2)}) copy-start(bf16[6272,256]{1,0:T(8,128)(2,1)} %all-gather.3.cloned.1.call-done) | copy-start | bytes 9633796
  234.2 361.9 %copy-start.58 = (f32[6272]{0:T(1024)}, f32[6272]{0:T(1024)S(1)}, u32[]{:S(2)}) copy-start(f32[6272]{0:T(1024)S(1)} %broadcast_multiply_fusion.3) | copy-start | bytes 75268
  242.7 21.2 %copy-start.61 = (f32[128,49]{1,0:T(8,128)S(1)}, f32[128,49]{1,0:T(8,128)}, u32[]{:S(2)}) copy-start(f32[128,49]{1,0:T(8,128)} %add_multiply_fusion) | copy-start | bytes 75268
  257.1 15.6 %copy-start.11 = (bf16[128,49,2,32]{1,0,3,2:T(8,128)(2,1)}, bf16[128,49,2,32]{1,0,3,2:T(8,128)(2,1)S(1)}, u32[]{:S(2)}) copy-start(bf16[128,49,2,32]{1,0,3,2:T(8,128)(2,1)S(1)} %squeeze.8) | copy-start | bytes 2408452
  281.1 86.0 %copy-start.72 = (bf16[32,256]{1,0:T(8,128)(2,1)S(1)}, bf16[32,256]{1,0:T(8,128)(2,1)}, u32[]{:S(2)}) copy-start(bf16[32,256]{1,0:T(8,128)(2,1)} %param.21) | copy-start | bytes 49156
  282.5 153.0 %copy-start.107 = (f32[256]{0:T(256)S(1)}, f32[256]{0:T(256)}, u32[]{:S(2)}) copy-start(f32[256]{0:T(256)} %param.18) | copy-start | bytes 3076
  284.9 153.3 %copy-start.21 = (bf16[6272,64]{0,1:T(8,128)(2,1)}, bf16[6272,64]{0,1:T(8,128)(2,1)S(1)}, u32[]{:S(2)}) copy-start(bf16[6272,64]{0,1:T(8,128)(2,1)S(1)} %convert_element_type.246) | copy-start | bytes 2408452
  284.9 153.4 %copy-start.102 = (f32[1,256]{1,0:T(1,128)S(1)}, f32[1,256]{1,0:T(1,128)}, u32[]{:S(2)}) copy-start(f32[1,256]{1,0:T(1,128)} %get-tuple-element.128) | copy-start | bytes 3076
  284.9 153.4 %copy-start.108 = (f32[1,256]{1,0:T(1,128)S(1)}, f32[1,256]{1,0:T(1,128)}, u32[]{:S(2)}) copy-start(f32[1,256]{1,0:T(1,128)} %get-tuple-element.130) | copy-start | bytes 3076
  284.9 153.4 %copy-start.114 = (f32[1024]{0:T(1024)S(1)}, f32[1024]{0:T(1024)}, u32[]{:S(2)}) copy-start(f32[1024]{0:T(1024)} %param.20) | copy-start | bytes 12292
  287.7 238.8 %all-gather.5.cloned.1.call-start = ((), (), s32[]{:S(2)}) async-start(), calls=%async_computation.6 | async-start | bytes 4014080 | tf_op jit(solution)/shard_map/all_gather | solution.py:265
  287.8 173.4 %copy-start.67 = (f32[1568]{0:T(1024)}, f32[1568]{0:T(1024)S(1)}, u32[]{:S(2)}) copy-start(f32[1568]{0:T(1024)S(1)} %dynamic_slice.9) | copy-start | bytes 18820
  435.5 19.4 %copy-start.32 = (bf16[1024,256]{1,0:T(8,128)(2,1)}, bf16[1024,256]{1,0:T(8,128)(2,1)S(1)}, u32[]{:S(2)}) copy-start(bf16[1024,256]{1,0:T(8,128)(2,1)S(1)} %all_gather.14) | copy-start | bytes 1572868
  437.7 23.6 %copy-start.14 = (f32[1568,256]{1,0:T(8,128)}, f32[1568,256]{1,0:T(8,128)S(1)}, u32[]{:S(2)}) copy-start(f32[1568,256]{1,0:T(8,128)S(1)} %get-tuple-element.48) | copy-start | bytes 4816900
  437.7 23.6 %copy-start.65 = (f32[1568]{0:T(1024)}, f32[1568]{0:T(1024)S(1)}, u32[]{:S(2)}) copy-start(f32[1568]{0:T(1024)S(1)} %broadcast_multiply_fusion.6) | copy-start | bytes 18820
  438.3 23.0 %copy-start.69 = (f32[1568]{0:T(1024)}, f32[1568]{0:T(1024)S(1)}, u32[]{:S(2)}) copy-start(f32[1568]{0:T(1024)S(1)} %add_rsqrt_fusion.1) | copy-start | bytes 18820
  438.3 16.6 %copy-start.28 = (bf16[1568,256]{1,0:T(8,128)(2,1)S(1)}, bf16[1568,256]{1,0:T(8,128)(2,1)}, u32[]{:S(2)}) copy-start(bf16[1568,256]{1,0:T(8,128)(2,1)} %param.27) | copy-start | bytes 2408452
  464.7 428.0 %reduce-scatter.7.cloned.1.call-start = ((), (), s32[]{:S(2)}) async-start(), calls=%async_computation.7 | async-start | bytes 4014080 | tf_op jit(solution)/shard_map/reduce_scatter | solution.py:279
  530.4 15.3 %slice-start = ((s8[7340032]{0:T(1024)(128)(4,1)}), s8[3145728]{0:T(1024)(128)(4,1)S(1)}, s32[]{:S(2)}) async-start(s8[7340032]{0:T(1024)(128)(4,1)} %bitcast.107), calls=%async_computation.11 | async-start | bytes 6291456
  589.0 19.3 %slice-start.2 = ((s8[6422528]{0:T(1024)(128)(4,1)}), s8[2228224]{0:T(1024)(128)(4,1)S(1)}, s32[]{:S(2)}) async-start(s8[6422528]{0:T(1024)(128)(4,1)} %bitcast.109), calls=%async_computation.13 | async-start | bytes 4456448
  805.8 20.2 %copy-start.29 = (bf16[1568,256]{1,0:T(8,128)(2,1)S(1)}, bf16[1568,256]{1,0:T(8,128)(2,1)}, u32[]{:S(2)}) copy-start(bf16[1568,256]{1,0:T(8,128)(2,1)} %param.27) | copy-start | bytes 2408452
  805.8 20.2 %copy-start.68 = (f32[1568]{0:T(1024)S(1)}, f32[1568]{0:T(1024)}, u32[]{:S(2)}) copy-start(f32[1568]{0:T(1024)} %copy-done.67) | copy-start | bytes 18820
  825.9 199.1 %reduce-scatter.11.cloned.1.call-start = ((), (), s32[]{:S(2)}) async-start(), calls=%async_computation.9 | async-start | bytes 1081344 | tf_op jit(solution)/shard_map/reduce_scatter | solution.py:285
  830.5 329.1 %reduce-scatter.9.cloned.1.call-start = ((), (), s32[]{:S(2)}) async-start(), calls=%async_computation.8 | async-start | bytes 1081344 | tf_op jit(solution)/shard_map/reduce_scatter | solution.py:284
  835.4 378.4 %all-reduce.6.cloned.1.call-start = ((), (), s32[]{:S(2)}) async-start(), calls=%async_computation.10 | async-start | bytes 524288 | tf_op jit(solution)/shard_map/psum | solution.py:282
  (96 other events, 706.1 us)
Sparse Core Ops, SparseCore 0:
  9.6 67.2 all-gather.2
  287.8 67.9 reduce-scatter.4
  464.8 61.6 all-gather.4
  826.0 60.9 reduce-scatter.6
  889.7 135.2 reduce-scatter.10
  1027.8 131.8 reduce-scatter.8
  1163.3 50.3 all-reduce.5
where the time goes:
time: 1240 us; the launch traced here: 1220 us
  waiting for transfers between devices  439 us (35%)
  local copies, waits for them, and re-layouts  274 us (22%)
  other arithmetic  200 us (16%)
  blocking collectives  191 us (15%)
  matrix products  103 us (8%)
  between operations  16.3 us (1%)
    reduce_scatter x1, waiting for transfers between devices, on_device(): lax.psum_scatter(d_fc_in, ('img', 'head'), scatter_dimension=0, tiled=True)  135 us
    reduce_scatter x1, waiting for transfers between devices, on_device(): lax.psum_scatter(d_fc_out, ('img', 'head'), scatter_dimension=0, tiled=True)  130 us
    all_gather x1, blocking collectives, on_device(): lax.all_gather(fc_in, ('img', 'head'), axis=0, tiled=True)  79.3 us
    all_gather x1, blocking collectives, on_device(): lax.all_gather(fc_out, ('img', 'head'), axis=0, tiled=True)  68.3 us
    convert_element_type x8, local copies, waits for them, and re-layouts, tap_rows(): return tiles[:, 1 + shift_row:1 + shift_row + WS, 1 + shift_col:1 + shift...  62.7 us
    reshape x8, local copies, waits for them, and re-layouts, tap_rows(): return tiles[:, 1 + shift_row:1 + shift_row + WS, 1 + shift_col:1 + shift...  62.5 us
    all_gather x1, waiting for transfers between devices, on_device(): d_branch_all = lax.all_gather(d_branch, 'head', axis=0, tiled=True)  61.7 us
    all_gather x1, waiting for transfers between devices, on_device(): gathered = lax.all_gather(tokens, 'head', axis=0, tiled=True)  57.9 us
  transfers between devices with their start and end apart: 7, of which 5 were waited for; matrix products, arithmetic and copies ran while one was open for 3% of the time, Pallas kernels for 0%

commit v1 on v0

v1 whole, which is shorter than its diff:
```python
import functools

import jax
import jax.numpy as jnp
from jax import lax
from jax.experimental import pallas as pl
from jax.experimental.pallas import tpu as pltpu
from jax.sharding import PartitionSpec as P

F32 = jnp.float32
BF16 = jnp.bfloat16
MESH = pl.DeviceIdType.MESH

HDIM = 32
WS = 7
CELLS = WS * WS
SLOT = WS * 8
TALL = 64
MARGIN = 5
HALO = 256
EDGE = 6
OFFSET = 8
BLOCK = 4
SMALL = 32
VMEM_LIMIT = 56 * 1024 * 1024


def nn(left, right):
    return lax.dot_general(left, right, (((1,), (0,)), ((), ())), preferred_element_type=F32)


def nt(left, right):
    return lax.dot_general(left, right, (((1,), (1,)), ((), ())), preferred_element_type=F32)


def tn(left, right):
    return lax.dot_general(left, right, (((0,), (0,)), ((), ())), preferred_element_type=F32)


def iota(shape, axis):
    return lax.broadcasted_iota(jnp.int32, shape, axis)


def identity(size):
    return jnp.where(iota((size, size), 0) == iota((size, size), 1), 1.0, 0.0).astype(BF16)


def scan_windows(sides_ref, info_ref, windows):
    slots = sides_ref.shape[-1]

    def clear(index, carry):
        for kind in range(3):
            info_ref[kind, index] = 0
            info_ref[kind, OFFSET + windows + index] = 0
        return carry

    lax.fori_loop(0, OFFSET, clear, 0)

    def body(window, carry):
        slot, row, col = carry
        side = jnp.where(slot < slots, sides_ref[0, jnp.minimum(slot, slots - 1)], 0)
        info_ref[0, OFFSET + window] = side
        info_ref[1, OFFSET + window] = row
        info_ref[2, OFFSET + window] = col
        end_col = col + 1 >= side
        end_row = row + 1 >= side
        next_slot = jnp.where(end_col & end_row, slot + 1, slot)
        next_row = jnp.where(end_col, jnp.where(end_row, 0, row + 1), row)
        next_col = jnp.where(end_col, 0, col + 1)
        return (next_slot, next_row, next_col)

    zero = jnp.int32(0)
    lax.fori_loop(0, windows, body, (zero, zero, zero))


def window_of(info_ref, window):
    side = info_ref[0, OFFSET + window]
    row = info_ref[1, OFFSET + window]
    col = info_ref[2, OFFSET + window]
    limit = jnp.where(side == 2, 14, jnp.where(side == 3, 18, jnp.where(side == 4, 24, 0)))
    high = jnp.minimum(limit - WS * row, WS)
    wide = jnp.minimum(limit - WS * col, WS)
    return side, row, col, high, wide


def expand(rows_ref, start, high, wide):
    base = pl.multiple_of((start // 16) * 16, 16)
    shift = start - base
    place = iota((SLOT, TALL), 0)
    patch_row, patch_col = place >> 3, place & 7
    hit = (
        (iota((SLOT, TALL), 1) == WS * patch_row + patch_col + shift)
        & (patch_col < wide)
        & (patch_row < high)
    )
    return nn(jnp.where(hit, 1.0, 0.0).astype(BF16), rows_ref[pl.ds(base, TALL), :])


def contract_mask(step, rows):
    first = rows * step
    window = first // CELLS
    shift = first - CELLS * window
    source = iota((rows, BLOCK * SLOT), 1)
    hit = (iota((rows, BLOCK * SLOT), 0) + shift == WS * (source >> 3) + (source & 7)) & (
        (source & 7) < WS
    )
    return window, jnp.where(hit, 1.0, 0.0).astype(BF16)


def near(ext_ref, place, side, row, col):
    lane_col = iota((1, 8, ext_ref.shape[-1]), 1)
    first = jnp.where(col > 0, 0, 8)
    last = jnp.where(col < side - 1, WS - 1, 8)

    def triple(window, rows):
        own = ext_ref[window, rows]
        left = pltpu.roll(ext_ref[window - 1, rows], 2, 1)
        right = pltpu.roll(ext_ref[window + 1, rows], 6, 1)
        return (
            jnp.where(lane_col == first, left, pltpu.roll(own, 1, 1)),
            own,
            jnp.where(lane_col == last, right, pltpu.roll(own, 7, 1)),
        )

    above_on = jnp.where(row > 0, 1.0, 0.0)
    below_on = jnp.where(row < side - 1, 1.0, 0.0)
    above = triple(place - side, slice(WS - 1, WS))
    middle = triple(place, slice(0, WS))
    below = triple(place + side, slice(0, 1))
    return [
        jnp.concatenate([up * above_on, mid, down * below_on], axis=0)
        for up, mid, down in zip(above, middle, below)
    ]


def valid_cells(high, wide, width):
    shape = (WS, 8, width)
    return (iota(shape, 0) < high) & (iota(shape, 1) < wide)


def fold(values):
    rows, width = values.shape
    return jnp.sum(values.reshape(rows // 8, 8, width), axis=0)


def normalize(values):
    centre = values - jnp.mean(values, axis=-1, keepdims=True)
    inverse = lax.rsqrt(jnp.mean(centre * centre, axis=-1, keepdims=True) + 1e-06)
    return centre * inverse, inverse


def normalize_back(gradient, scaled, inverse, gain):
    d_scaled = gradient * gain
    mean_one = jnp.mean(d_scaled, axis=-1, keepdims=True)
    mean_two = jnp.mean(d_scaled * scaled, axis=-1, keepdims=True)
    return inverse * (d_scaled - mean_one - scaled * mean_two)


def stack_heads(values):
    head = iota(values.shape, 1) // HDIM
    zero = jnp.zeros_like(values)
    return jnp.concatenate([jnp.where(head == g, values, zero) for g in range(128 // HDIM)], axis=0)


def pick_heads(stacked):
    head = iota((TALL, 128), 1) // HDIM
    taken = stacked[0:TALL]
    for g in range(1, 128 // HDIM):
        taken = jnp.where(head == g, stacked[TALL * g : TALL * (g + 1)], taken)
    return taken


def to_tall(rows):
    return jnp.concatenate([rows, jnp.zeros((TALL - SLOT, rows.shape[1]), F32)], axis=0).astype(
        BF16
    )


def gelu_parts(values):
    cdf = 0.5 + 0.5 * lax.erf(values * (0.5**0.5))
    density = jnp.exp(-0.5 * values * values) * 0.3989422804014327
    return values * cdf, cdf + values * density


def rows_at(index, size):
    return pl.ds(pl.multiple_of(index * size, size), size)


def front(first, tokens_ref, og_ref, info_ref, ext_ref, dout_ref, windows):
    def source(place, carry):
        _, _, _, high, wide = window_of(info_ref, first + place - MARGIN)
        start = HALO - MARGIN * CELLS + CELLS * place
        ext_ref[place] = expand(tokens_ref, start, high, wide).reshape(WS, 8, -1)
        return carry

    lax.fori_loop(0, windows + 2 * MARGIN, source, 0, unroll=2)

    def cotangent(window, carry):
        _, _, _, high, wide = window_of(info_ref, first + window)
        dout_ref[rows_at(window, SLOT), :] = expand(og_ref, CELLS * window, high, wide)
        return carry

    lax.fori_loop(0, windows, cotangent, 0, unroll=2)


def field_pass(first, info_ref, ext_ref, peg_ref, peg_bias_ref, gain_ref, shift_ref, field_ref, scaled_ref, inverse_ref, normed_ref, windows):
    def pair(step, carry):
        normed = []
        for sub in range(2):
            window = 2 * step + sub
            side, row, col, high, wide = window_of(info_ref, first + window)
            bands = near(ext_ref, window + MARGIN, side, row, col)
            total = bands[1][1 : 1 + WS] + peg_bias_ref[...]
            for a in range(3):
                for b in range(3):
                    tap = 3 * a + b
                    total = total + bands[b][a : a + WS] * peg_ref[tap : tap + 1, :]
            total = jnp.where(valid_cells(high, wide, total.shape[-1]), total, 0.0)
            field = total.reshape(SLOT, -1)
            scaled, inverse = normalize(field)
            place = rows_at(window, SLOT)
            field_ref[place, :] = field
            scaled_ref[place, :] = scaled
            inverse_ref[place, :] = inverse
            normed.append(scaled * gain_ref[0:1, :] + shift_ref[0:1, :])
        normed_ref[rows_at(step, 2 * SLOT), :] = jnp.concatenate(normed, axis=0).astype(BF16)
        return carry

    lax.fori_loop(0, windows // 2, pair, 0)


def attend(qkv, high, wide, probs_ref, window):
    width = qkv.shape[1] // 3
    key = iota((TALL, 256), 0)
    usable = ((key >> 3) < high) & ((key & 7) < wide)
    halves = []
    for half in range(width // 128):
        query, keys, value = (
            qkv[:, width * t + 128 * half : width * t + 128 * (half + 1)] for t in range(3)
        )
        scores = jnp.where(usable, nt(keys, stack_heads(query)), -1e30)
        top = jnp.max(scores, axis=0, keepdims=True)
        exponent = jnp.exp((scores - top) * HDIM**-0.5)
        probs = exponent * (1.0 / jnp.sum(exponent, axis=0, keepdims=True))
        probs_ref[window, :, 256 * half : 256 * (half + 1)] = probs
        halves.append(pick_heads(tn(probs.astype(BF16), value)))
    return jnp.concatenate(halves, axis=1)


def attend_back(qkv, d_context, probs_ref, window):
    width = qkv.shape[1] // 3
    d_query, d_key, d_value = [], [], []
    for half in range(width // 128):
        query, keys, value = (
            qkv[:, width * t + 128 * half : width * t + 128 * (half + 1)] for t in range(3)
        )
        d_stack = stack_heads(d_context[:, 128 * half : 128 * (half + 1)])
        probs = probs_ref[window, :, 256 * half : 256 * (half + 1)]
        d_value.append(nn(probs.astype(BF16), d_stack))
        d_probs = nt(value, d_stack)
        inner = jnp.sum(d_probs * probs, axis=0, keepdims=True)
        d_score = (probs * (d_probs - inner)).astype(BF16)
        d_key.append(nn(d_score, stack_heads(query)) * HDIM**-0.5)
        d_query.append(pick_heads(tn(d_score, keys)) * HDIM**-0.5)
    return jnp.concatenate(d_query + d_key + d_value, axis=1)


def forward_block(first, refs, step):
    (info_ref, dout_ref, field_ref, normed_ref, wt_ref, proj_ref, proj_bias_ref, fc_ref, fc_in_bias_ref, fc_out_bias_ref,
     gain_ref, shift_ref, qkv_ref, probs_ref, context_ref, hidden_ref, result_ref, g_fc_ref, g_proj_ref, sums_ref, bias_ref) = refs
    rows = BLOCK * SLOT
    place = rows_at(step, rows)
    projected = nt(normed_ref[place, :], wt_ref[...])
    context = []
    for sub in range(BLOCK):
        window = BLOCK * step + sub
        _, _, _, high, wide = window_of(info_ref, first + window)
        qkv = to_tall(projected[SLOT * sub : SLOT * (sub + 1)])
        qkv_ref[window] = qkv
        context.append(attend(qkv, high, wide, probs_ref, window)[0:SLOT])
    context = jnp.concatenate(context, axis=0).astype(BF16)
    context_ref[place, :] = context
    hidden = field_ref[place, :] + nn(context, proj_ref[...]) + proj_bias_ref[...]
    scaled, inverse = normalize(hidden)
    normed = (scaled * gain_ref[1:2, :] + shift_ref[1:2, :]).astype(BF16)
    d_output = dout_ref[place, :]
    d_low = d_output.astype(BF16)
    normed_t = normed.T
    d_low_t = d_low.T
    ones = jnp.ones((8, rows), BF16)
    result = hidden + fc_out_bias_ref[...]
    d_normed = jnp.zeros_like(hidden)
    width = 256
    for chunk in range(fc_ref.shape[1] // width):
        cols = slice(width * chunk, width * (chunk + 1))
        w_in, w_out = fc_ref[0, cols, :], fc_ref[1, cols, :]
        pre = nt(normed, w_in) + fc_in_bias_ref[:, cols]
        active, slope = gelu_parts(pre)
        active = active.astype(BF16)
        d_pre = (nt(d_low, w_out) * slope).astype(BF16)
        result = result + nn(active, w_out)
        d_normed = d_normed + nn(d_pre, w_in)
        g_fc_ref[0, :, cols] += nn(normed_t, d_pre)
        g_fc_ref[1, :, cols] += nn(d_low_t, active)
        bias_ref[:, cols] += nn(ones, d_pre)
    result_ref[place, :] = result
    d_hidden = d_output + normalize_back(d_normed, scaled, inverse, gain_ref[1:2, :])
    hidden_ref[place, :] = d_hidden
    d_branch = d_hidden.astype(BF16)
    g_proj_ref[...] += nn(context.T, d_branch)
    sums_ref[0] += fold(d_branch.astype(F32))
    sums_ref[1] += fold(d_output)
    sums_ref[3] += fold(d_normed * scaled)
    sums_ref[5] += fold(d_normed)


def backward_block(first, refs, step):
    (info_ref, hidden_ref, proj_ref, qkv_ref, probs_ref, wt_ref, normed_ref, scaled_ref, inverse_ref, gain_ref,
     g_qkv_ref, sums_ref, mixed_ref) = refs
    rows = BLOCK * SLOT
    place = rows_at(step, rows)
    d_hidden = hidden_ref[place, :]
    d_context = nt(d_hidden.astype(BF16), proj_ref[...])
    d_qkv = []
    for sub in range(BLOCK):
        window = BLOCK * step + sub
        d_qkv.append(
            attend_back(
                qkv_ref[window],
                to_tall(d_context[SLOT * sub : SLOT * (sub + 1)]),
                probs_ref,
                window,
            )[0:SLOT]
        )
    d_qkv = jnp.concatenate(d_qkv, axis=0).astype(BF16)
    d_normed = nn(d_qkv, wt_ref[...])
    g_qkv_ref[...] += nn(normed_ref[place, :].T, d_qkv)
    scaled = scaled_ref[place, :]
    sums_ref[2] += fold(d_normed * scaled)
    sums_ref[4] += fold(d_normed)
    d_field = d_hidden + normalize_back(d_normed, scaled, inverse_ref[place, :], gain_ref[0:1, :])
    for sub in range(BLOCK):
        window = BLOCK * step + sub
        _, _, _, high, wide = window_of(info_ref, first + window)
        cells = d_field[SLOT * sub : SLOT * (sub + 1)].reshape(WS, 8, -1)
        mixed_ref[window] = jnp.where(valid_cells(high, wide, cells.shape[-1]), cells, 0.0)


def shrink(first, info_ref, padded_ref, dense_ref, exact):
    rows = 112

    def body(step, carry):
        window, hit = contract_mask(step, rows)
        values = padded_ref[pl.ds(pl.multiple_of(SLOT * window, 8), BLOCK * SLOT), :]
        high = values.astype(BF16)
        dense = nn(hit, high)
        if exact:
            dense = dense + nn(hit, (values - high.astype(F32)).astype(BF16))
        dense_ref[rows_at(step, rows), :] = dense.astype(dense_ref.dtype)
        return carry

    lax.fori_loop(0, dense_ref.shape[0] // rows, body, 0)


def compute_kernel(heads, sides_ref, tokens_ref, og_ref, wt_ref, proj_ref, fc_ref, proj_bias_ref, fc_in_bias_ref, fc_out_bias_ref,
                   gain_ref, shift_ref, peg_ref, peg_bias_ref,
                   output_ref, mixed_ref, ext_ref, g_fc_out_ref, g_at_ref, small_ref,
                   info_ref, dout_ref, field_ref, scaled_ref, inverse_ref, normed_ref, qkv_ref, probs_ref, context_ref, hidden_ref,
                   result_ref, g_fc_ref, g_proj_ref, g_qkv_ref, sums_ref, bias_ref):
    windows = mixed_ref.shape[0]
    first = lax.axis_index("head") * windows
    scan_windows(sides_ref, info_ref, heads * windows)
    front(first, tokens_ref, og_ref, info_ref, ext_ref, dout_ref, windows)
    for ref in (g_fc_ref, g_proj_ref, g_qkv_ref, sums_ref, bias_ref):
        ref[...] = jnp.zeros_like(ref)
    result_ref[windows * SLOT :, :] = jnp.zeros((result_ref.shape[0] - windows * SLOT, result_ref.shape[1]), F32)
    field_pass(first, info_ref, ext_ref, peg_ref, peg_bias_ref, gain_ref, shift_ref, field_ref, scaled_ref, inverse_ref, normed_ref, windows)
    forward_refs = (info_ref, dout_ref, field_ref, normed_ref, wt_ref, proj_ref, proj_bias_ref, fc_ref, fc_in_bias_ref, fc_out_bias_ref,
                    gain_ref, shift_ref, qkv_ref, probs_ref, context_ref, hidden_ref, result_ref, g_fc_ref, g_proj_ref, sums_ref, bias_ref)
    backward_refs = (info_ref, hidden_ref, proj_ref, qkv_ref, probs_ref, wt_ref, normed_ref, scaled_ref, inverse_ref, gain_ref,
                     g_qkv_ref, sums_ref, mixed_ref)

    def forward(step, carry):
        forward_block(first, forward_refs, step)
        return carry

    lax.fori_loop(0, windows // BLOCK, forward, 0)

    def mask_result(window, carry):
        _, _, _, high, wide = window_of(info_ref, first + window)
        place = rows_at(window, SLOT)
        cells = result_ref[place, :].reshape(WS, 8, -1)
        result_ref[place, :] = jnp.where(valid_cells(high, wide, cells.shape[-1]), cells, 0.0).reshape(SLOT, -1)
        return carry

    lax.fori_loop(0, windows, mask_result, 0)
    shrink(first, info_ref, result_ref, output_ref, False)

    def backward(step, carry):
        backward_block(first, backward_refs, step)
        return carry

    lax.fori_loop(0, windows // BLOCK, backward, 0)

    eye = identity(256)
    for kind in range(2):
        for chunk in range(g_fc_out_ref.shape[1] // 256):
            cols = slice(256 * chunk, 256 * (chunk + 1))
            g_fc_out_ref[kind, cols, :] = nt(eye, g_fc_ref[kind, :, cols].astype(BF16)).astype(BF16)
    for kind in range(3):
        cols = slice(256 * kind, 256 * (kind + 1))
        g_at_ref[kind] = nt(eye, g_qkv_ref[:, cols].astype(BF16)).astype(BF16)
    g_at_ref[3] = g_proj_ref[...].astype(BF16)
    small_ref[...] = jnp.zeros_like(small_ref)
    total = jnp.sum(sums_ref[...], axis=1)
    small_ref[0:1, :] = total[0:1]
    for chunk in range(4):
        small_ref[1 + chunk : 2 + chunk, :] = bias_ref[0:1, 256 * chunk : 256 * (chunk + 1)]
    small_ref[5:6, :] = total[1:2]
    small_ref[6:10, :] = total[2:6]


def peg_back(first, info_ref, ext_ref, mixed_ref, peg_ref, taps_ref, source_ref, windows):
    def body(window, carry):
        side, row, col, high, wide = window_of(info_ref, first + window)
        bands = near(ext_ref, window + MARGIN, side, row, col)
        grads = near(mixed_ref, window + MARGIN, side, row, col)
        own = grads[1][1 : 1 + WS]
        total = own
        for a in range(3):
            for b in range(3):
                tap = 3 * a + b
                taps_ref[tap] += jnp.sum(own * bands[b][a : a + WS], axis=0)
                total = total + grads[2 - b][2 - a : 2 - a + WS] * peg_ref[tap : tap + 1, :]
        taps_ref[9] += jnp.sum(own, axis=0)
        total = jnp.where(valid_cells(high, wide, total.shape[-1]), total, 0.0)
        source_ref[rows_at(window, SLOT), :] = total.reshape(SLOT, -1)
        return carry

    lax.fori_loop(0, windows, body, 0)


def peg_kernel(heads, sides_ref, ext_ref, mixed_ref, peg_ref, d_tokens_ref, taps_out_ref, info_ref, taps_ref, source_ref):
    windows = ext_ref.shape[0] - 2 * MARGIN
    first = lax.axis_index("head") * windows
    scan_windows(sides_ref, info_ref, heads * windows)
    taps_ref[...] = jnp.zeros_like(taps_ref)
    source_ref[windows * SLOT :, :] = jnp.zeros((source_ref.shape[0] - windows * SLOT, source_ref.shape[1]), F32)
    peg_back(first, info_ref, ext_ref, mixed_ref, peg_ref, taps_ref, source_ref, windows)
    taps_out_ref[...] = jnp.sum(taps_ref[...], axis=1)
    shrink(first, info_ref, source_ref, d_tokens_ref, True)


def vmem():
    return pl.BlockSpec(memory_space=pltpu.VMEM)


def smem():
    return pl.BlockSpec(memory_space=pltpu.SMEM)


def on_device(tokens, image_sides, qkv_weight, proj_weight, proj_bias, fc_in, fc_in_bias, fc_out, fc_out_bias,
              norm_gains, norm_shifts, peg_weight, peg_bias, out_grad):
    own_rows, width = tokens.shape
    windows = own_rows // CELLS
    heads = lax.axis_size("head")
    hidden = fc_in_bias.shape[0]
    padded = windows * SLOT
    extra = (windows + BLOCK) * SLOT
    me = lax.axis_index("head")

    gathered = lax.all_gather(tokens, "head", axis=0, tiled=True)
    gathered = jnp.pad(gathered, ((HALO, HALO), (0, 0)))
    tokens_ext = lax.dynamic_slice_in_dim(gathered, me * own_rows, own_rows + 2 * HALO, 0)
    qkv_t = jnp.swapaxes(qkv_weight, 1, 2)
    wt = lax.all_gather(qkv_t, "head", axis=1, tiled=True).reshape(-1, width)
    proj = lax.all_gather(proj_weight, "head", axis=0, tiled=True)
    fc = jnp.stack([
        lax.all_gather(fc_in, ("img", "head"), axis=0, tiled=True),
        lax.all_gather(fc_out, ("img", "head"), axis=0, tiled=True),
    ])

    shape = jax.ShapeDtypeStruct
    output, mixed, ext, g_fc, g_at, small = pl.pallas_call(
        functools.partial(compute_kernel, heads),
        out_shape=(
            shape((own_rows, width), BF16),
            shape((windows, WS, 8, width), F32),
            shape((windows + 2 * MARGIN, WS, 8, width), F32),
            shape((2, hidden, width), BF16),
            shape((4, width, width), BF16),
            shape((SMALL, width), F32),
        ),
        in_specs=[smem()] + [vmem()] * 12,
        out_specs=(vmem(),) * 6,
        scratch_shapes=[
            pltpu.SMEM((3, heads * windows + 2 * OFFSET), jnp.int32),
            pltpu.VMEM((padded, width), F32),
            pltpu.VMEM((padded, width), F32),
            pltpu.VMEM((padded, width), F32),
            pltpu.VMEM((padded, 1), F32),
            pltpu.VMEM((padded, width), BF16),
            pltpu.VMEM((windows, TALL, 3 * width), BF16),
            pltpu.VMEM((windows, TALL, 2 * width), F32),
            pltpu.VMEM((padded, width), BF16),
            pltpu.VMEM((padded, width), F32),
            pltpu.VMEM((extra, width), F32),
            pltpu.VMEM((2, width, hidden), F32),
            pltpu.VMEM((width, width), F32),
            pltpu.VMEM((width, 3 * width), F32),
            pltpu.VMEM((6, 8, width), F32),
            pltpu.VMEM((8, hidden), F32),
        ],
        compiler_params=pltpu.CompilerParams(vmem_limit_bytes=VMEM_LIMIT),
        name="block",
    )(image_sides, tokens_ext, out_grad, wt, proj, fc, proj_bias[None], fc_in_bias[None], fc_out_bias[None],
      norm_gains, norm_shifts, peg_weight, peg_bias[None])

    before = [(i, i + 1) for i in range(heads - 1)]
    after = [(i + 1, i) for i in range(heads - 1)]
    left = lax.ppermute(mixed[windows - MARGIN :].astype(BF16), "head", before).astype(F32)
    right = lax.ppermute(mixed[:MARGIN].astype(BF16), "head", after).astype(F32)
    mixed_ext = jnp.concatenate([left, mixed, right], axis=0)

    d_tokens, taps = pl.pallas_call(
        functools.partial(peg_kernel, heads),
        out_shape=(shape((own_rows, width), F32), shape((10, width), F32)),
        in_specs=[smem()] + [vmem()] * 3,
        out_specs=(vmem(),) * 2,
        scratch_shapes=[
            pltpu.SMEM((3, heads * windows + 2 * OFFSET), jnp.int32),
            pltpu.VMEM((10, 8, width), F32),
            pltpu.VMEM((extra, width), F32),
        ],
        compiler_params=pltpu.CompilerParams(vmem_limit_bytes=VMEM_LIMIT),
        name="peg_back",
    )(image_sides, ext, mixed_ext, peg_weight)

    small = small.at[10:20].set(taps)
    small = lax.psum(small, ("img", "head"))
    d_fc_in = lax.psum_scatter(g_fc[0].astype(F32), ("img", "head"), scatter_dimension=0, tiled=True)
    d_fc_out = lax.psum_scatter(g_fc[1].astype(F32), ("img", "head"), scatter_dimension=0, tiled=True)
    g_at = lax.psum(lax.psum_scatter(g_at.astype(F32), "head", scatter_dimension=1, tiled=True), "img")
    return (
        output,
        d_tokens,
        jnp.swapaxes(g_at[:3], 1, 2),
        g_at[3],
        small[0],
        d_fc_in,
        small[1:5].reshape(-1),
        d_fc_out,
        small[5],
        small[6:8],
        small[8:10],
        small[10:19],
        small[19],
    )


def solution(mesh):
    rows = P(("img", "head"), None)
    placed = (rows, P("img", None), P(None, None, "head"), P("head", None), P(), rows, P(), rows, P(), P(), P(), P(), P(), rows)
    return jax.shard_map(
        on_device,
        mesh=mesh,
        in_specs=placed,
        out_specs=(rows, rows, P(None, None, "head"), P("head", None), P(), rows, P(), rows, P(), P(), P(), P(), P()),
        check_vma=False,
    )
```

time: 1240 us -> 613 us (0.49); the launches traced: 1220 us -> 613 us
  local copies, waits for them, and re-layouts: 274 us -> 8.7 us
  other arithmetic: 200 us -> 6.53 us
  waiting for transfers between devices: 439 us -> 289 us
  matrix products: 103 us -> 0 us
  Pallas kernels: 0 us -> 73.8 us
  blocking collectives: 191 us -> 218 us
    dot_general x16 -> x0, matrix products: 101 us -> none  [the longest x1 16.6 us: on_device(): jnp.einsum('rd,fd->rf', normed_two, fc_in_all, preferred_element_type=jnp...]
    reshape x11 -> x0, local copies, waits for them, and re-layouts: 85.2 us -> none  [the longest x8 62.5 us: tap_rows(): return tiles[:, 1 + shift_row:1 + shift_row + WS, 1 + shift_col:1 + shift...]
    pallas_call x0 -> x2, Pallas kernels: none -> 73.8 us  [the longest x1 62.2 us: on_device(): pl.pallas_call(functools.partial(compute_kernel, heads), out_shape=(shape...]
    convert_element_type x10 -> x0, local copies, waits for them, and re-layouts: 66.4 us -> none  [the longest x8 62.7 us: tap_rows(): return tiles[:, 1 + shift_row:1 + shift_row + WS, 1 + shift_col:1 + shift...]
    convert_element_type x12 -> x4, other arithmetic: 68.6 us -> 3.74 us  [the longest x1 2.19 us: on_device(): g_at.astype(F32)]
    slice x10 -> x4, local copies, waits for them, and re-layouts: 63.6 us -> 1.79 us  [the longest x1 0.61 us: on_device(): small[10:19]]
    all_gather x1 -> x0, waiting for transfers between devices: 61.7 us -> none  [on_device(): d_branch_all = lax.all_gather(d_branch, 'head', axis=0, tiled=True)]
    all_gather x1, waiting for transfers between devices: 57.9 us -> 0.01 us  [on_device(): gathered = lax.all_gather(tokens, 'head', axis=0, tiled=True)]
  transfers between devices with their start and end apart: 7 -> 7, of which waited for: 5 -> 5; matrix products, arithmetic and copies ran while one was open for 3% -> 2% of each run, Pallas kernels for 0% -> 2%
where the time goes in v1:
time: 613 us
  waiting for transfers between devices  289 us (47%)
  blocking collectives  218 us (36%)
  Pallas kernels  73.8 us (12%)
  between operations  13.9 us (2%)
  local copies, waits for them, and re-layouts  8.7 us (1%)
  other arithmetic  6.53 us (1%)
    reduce_scatter x1, waiting for transfers between devices, on_device(): lax.psum_scatter(g_fc[0].astype(F32), ('img', 'head'), scatter_dimension=...  135 us
    reduce_scatter x1, waiting for transfers between devices, on_device(): lax.psum_scatter(g_fc[1].astype(F32), ('img', 'head'), scatter_dimension=...  122 us
    all_gather x1, blocking collectives, on_device(): lax.all_gather(fc_in, ('img', 'head'), axis=0, tiled=True)  76 us
    all_gather x1, blocking collectives, on_device(): lax.all_gather(fc_out, ('img', 'head'), axis=0, tiled=True)  69 us
    pallas_call x1, Pallas kernels, on_device(): pl.pallas_call(functools.partial(compute_kernel, heads), out_shape=(shape...  62.2 us
    psum x1, blocking collectives, on_device(): small = lax.psum(small, ('img', 'head'))  40.6 us
    reduce_scatter x1, waiting for transfers between devices, on_device(): lax.psum_scatter(g_at.astype(F32), 'head', scatter_dimension=1, tiled=True)  24.9 us
    all_gather x1, blocking collectives, on_device(): proj = lax.all_gather(proj_weight, 'head', axis=0, tiled=True)  17 us
  transfers between devices with their start and end apart: 7, of which 5 were waited for; matrix products, arithmetic and copies ran while one was open for 2% of the time, Pallas kernels for 2%

profile of v1, /device:TPU:0, one launch (start us, length us, event | category | flops | bytes accessed | tf_op | source)
XLA Modules:
  0.0 612.7 jit_solution(5235541645974620835)
XLA Ops:
  7.2 0.7 all-gather.2.cloned.1.call-update
  8.0 17.0 %all_gather.17.proj_ref = bf16[256,256]{1,0:T(8,128)(2,1)} all-gather(bf16[64,256]{1,0:T(8,128)(2,1)} %param.19), channel_id=1, replica_groups=mesh['img'=8,'head'=4] {'head'}, dimensions={0}, use_global_device_ids=true | all-gather | bytes 163840 | tf_op jit(solution)/shard_map/all_gather | solution.py:477
  25.0 76.0 %all_gather.18 = bf16[1024,256]{1,0:T(8,128)(2,1)S(1)} all-gather(bf16[32,256]{1,0:T(8,128)(2,1)} %param.21), channel_id=1, replica_groups=mesh['img'=8,'head'=4] {'img','head'}, dimensions={0}, use_global_device_ids=true | all-gather | bytes 540672 | tf_op jit(solution)/shard_map/all_gather | solution.py:479
  101.0 69.0 %all_gather.19 = bf16[1024,256]{1,0:T(8,128)(2,1)S(1)} all-gather(bf16[32,256]{1,0:T(8,128)(2,1)} %param.23), channel_id=1, replica_groups=mesh['img'=8,'head'=4] {'img','head'}, dimensions={0}, use_global_device_ids=true | all-gather | bytes 540672 | tf_op jit(solution)/shard_map/all_gather | solution.py:480
  170.0 1.1 pad_maximum_fusion.1.fc_ref
  171.1 15.7 %all_gather.16 = bf16[3,256,256]{2,1,0:T(8,128)(2,1)} all-gather(bf16[3,64,256]{2,1,0:T(8,128)(2,1)S(1)} %bitcast.27), channel_id=1, replica_groups=mesh['img'=8,'head'=4] {'head'}, dimensions={1}, use_global_device_ids=true | all-gather | bytes 491520 | tf_op jit(solution)/shard_map/all_gather | solution.py:476
  186.9 2.3 pad_dynamic-slice_fusion.tokens_ref
  189.1 62.2 %block.1 = (bf16[1568,256]{1,0:T(8,128)(2,1)}, f32[32,7,8,256]{3,2,1,0:T(8,128)}, f32[42,7,8,256]{3,2,1,0:T(8,128)}, bf16[2,1024,256]{2,1,0:T(8,128)(2,1)}, bf16...) custom-call(s32[1,32]{1,0:T(1,128)} %sides_ref.3, bf16[2080,256]{1,0:T(8,128)(2,1)} %pad_dynamic-slice_fusion.tokens_ref, ...), custom_call_target="tpu_custom_call" | custom-call | tf_op jit(solution)/shard_map/block/pallas_call | solution.py:484
  251.3 2.2 convert_element_type.27
  253.5 0.0 all-reduce.3.cloned.1.call-start
  253.6 24.9 %reduce-scatter.4.cloned.1.call-done = f32[4,64,256]{2,1,0:T(8,128)} async-done(((f32[4,256,256]{2,1,0:T(8,128)}), f32[4,64,256]{2,1,0:T(8,128)}) %reduce-scatter.4.cloned.1.call-update) | async-done | bytes 262160 | tf_op jit(solution)/shard_map/reduce_scatter | solution.py:543
  278.6 1.5 bitcast_convert_fusion
  280.1 0.0 reduce-scatter.6.cloned.1.call-start
  280.2 0.5 reduce-scatter.6.cloned.1.call-update
  280.7 0.1 copy-done
  280.8 0.1 convert.6
  281.0 1.3 collective-permute-start
  282.3 1.3 collective-permute-start.1
  283.6 1.8 collective-permute-done
  285.4 4.5 collective-permute-done.1
  289.9 1.6 pad_maximum_fusion.mixed_ref
  291.5 11.6 %peg_back.1 = (f32[1568,256]{1,0:T(8,128)}, f32[10,256]{1,0:T(8,128)}) custom-call(s32[1,32]{1,0:T(1,128)} %sides_ref.3, f32[42,7,8,256]{3,2,1,0:T(8,128)} %get-tuple-element.34.ext_ref, f32[42,7,8,256]{3,2,1,0:T(8,128)} %pad_maximum_fusion.mixed_ref, f32[9,256]{1,0:T(8,128)} %peg_ref.3), custom_call_target="tpu_custom_call" | custom-call | tf_op jit(solution)/shard_map/peg_back/pallas_call | solution.py:525
  303.1 0.8 scatter.4
  303.9 40.6 %psum.15 = f32[32,256]{1,0:T(8,128)S(1)} all-reduce(f32[32,256]{1,0:T(8,128)S(1)} %scatter.4), channel_id=1, replica_groups=mesh['img'=8,'head'=4] {'img','head'}, use_global_device_ids=true, to_apply=%region_2.3 | all-reduce | flops 8192 | bytes 65536 | tf_op jit(solution)/shard_map/psum | solution.py:540
  344.5 0.6 slice.80
  345.1 0.6 copy.27
  345.7 0.6 fusion.1
  346.3 0.6 fusion.2
  346.9 1.5 slice_bitcast_fusion.1
  348.4 1.6 slice_bitcast_fusion
  350.0 121.5 %reduce-scatter.8.cloned.1.call-done = f32[32,256]{1,0:T(8,128)} async-done(((f32[1024,256]{1,0:T(8,128)}), f32[32,256]{1,0:T(8,128)}) %reduce-scatter.8.cloned.1.call-update) | async-done | bytes 32784 | tf_op jit(solution)/shard_map/reduce_scatter | solution.py:542
  471.5 134.6 %reduce-scatter.6.cloned.1.call-done = f32[32,256]{1,0:T(8,128)} async-done(((f32[1024,256]{1,0:T(8,128)}), f32[32,256]{1,0:T(8,128)}) %reduce-scatter.6.cloned.1.call-update) | async-done | bytes 32784 | tf_op jit(solution)/shard_map/reduce_scatter | solution.py:541
  (19 shorter events, 0.2 us)
Async XLA Ops:
  7.2 163.9 %copy-start.2 = (bf16[3,256,64]{1,2,0:T(8,128)(2,1)S(1)}, bf16[3,256,64]{1,2,0:T(8,128)(2,1)}, u32[]{:S(2)}) copy-start(bf16[3,256,64]{1,2,0:T(8,128)(2,1)} %param.18) | copy-start | bytes 294916
  7.2 179.7 %all-gather.2.cloned.1.call-start = ((), (), s32[]{:S(2)}) async-start(), calls=%async_computation.3 | async-start | bytes 4014080 | tf_op jit(solution)/shard_map/all_gather | solution.py:472
  7.9 270.6 %reduce-scatter.4.cloned.1.call-start = ((), (), s32[]{:S(2)}) async-start(), calls=%async_computation.4 | async-start | bytes 1310720 | tf_op jit(solution)/shard_map/reduce_scatter | solution.py:543
  251.3 27.2 %copy-start.1 = (bf16[2,1024,256]{2,1,0:T(8,128)(2,1)S(1)}, bf16[2,1024,256]{2,1,0:T(8,128)(2,1)}, u32[]{:S(2)}) copy-start(bf16[2,1024,256]{2,1,0:T(8,128)(2,1)} %get-tuple-element.40) | copy-start | bytes 3145732
  253.5 93.4 %all-reduce.3.cloned.1.call-start = ((), (), s32[]{:S(2)}) async-start(), calls=%async_computation.5 | async-start | bytes 524288 | tf_op jit(solution)/shard_map/psum | solution.py:543
  278.5 193.0 %reduce-scatter.8.cloned.1.call-start = ((), (), s32[]{:S(2)}) async-start(), calls=%async_computation.7 | async-start | bytes 1081344 | tf_op jit(solution)/shard_map/reduce_scatter | solution.py:542
  278.6 2.3 copy-start
  280.1 326.0 %reduce-scatter.6.cloned.1.call-start = ((), (), s32[]{:S(2)}) async-start(), calls=%async_computation.6 | async-start | bytes 1081344 | tf_op jit(solution)/shard_map/reduce_scatter | solution.py:541
  281.0 4.4 collective-permute-start
  282.3 7.6 %collective-permute-start.1 = (bf16[5,7,8,256]{3,2,1,0:T(8,128)(2,1)S(1)}, bf16[5,7,8,256]{3,2,1,0:T(8,128)(2,1)S(1)}, u32[]{:S(2)}, u32[]{:S(2)}) collective-permute-start(bf16[5,7,8,256]{3,2,1,0:T(8,128)(2,1)S(1)} %get-tuple-element.44), channel_id=1, source_target_pairs={{1,0},{2,1},{3,2},{5,4},{6,5},{7,6},{9,8},{10,9},{11,10},{13,12},{... | collective-permute-start | bytes 430088 | tf_op jit(solution)/shard_map/ppermute | solution.py:522
  291.5 11.6 %copy-start.3 = (f32[32,256]{1,0:T(8,128)S(1)}, f32[32,256]{1,0:T(8,128)}, u32[]{:S(2)}) copy-start(f32[32,256]{1,0:T(8,128)} %get-tuple-element.38) | copy-start | bytes 98308
Sparse Core Ops, SparseCore 0:
  9.6 76.1 all-gather.1
  253.7 24.7 reduce-scatter.3
  281.8 52.2 all-reduce.2
  336.8 134.6 reduce-scatter.7
  474.3 131.8 reduce-scatter.5

commit v2 on v1

v2 whole, which is shorter than its diff:
```python
import functools
from types import SimpleNamespace

import jax
import jax.numpy as jnp
from jax import lax
from jax.experimental import pallas as pl
from jax.experimental.pallas import tpu as pltpu
from jax.sharding import PartitionSpec as P

F32 = jnp.float32
BF16 = jnp.bfloat16
MESH = pl.DeviceIdType.MESH

HDIM = 32
WS = 7
CELLS = WS * WS
SLOT = WS * 8
TALL = 64
MARGIN = 5
HALO = 256
EDGE = 6
OFFSET = 8
BLOCK = 4
SMALL = 32
VMEM_LIMIT = 56 * 1024 * 1024


def nn(left, right):
    return lax.dot_general(left, right, (((1,), (0,)), ((), ())), preferred_element_type=F32)


def nt(left, right):
    return lax.dot_general(left, right, (((1,), (1,)), ((), ())), preferred_element_type=F32)


def tn(left, right):
    return lax.dot_general(left, right, (((0,), (0,)), ((), ())), preferred_element_type=F32)


def iota(shape, axis):
    return lax.broadcasted_iota(jnp.int32, shape, axis)


def identity(size):
    return jnp.where(iota((size, size), 0) == iota((size, size), 1), 1.0, 0.0).astype(BF16)


def scan_windows(sides_ref, info_ref, windows):
    slots = sides_ref.shape[-1]

    def clear(index, carry):
        for kind in range(3):
            info_ref[kind, index] = 0
            info_ref[kind, OFFSET + windows + index] = 0
        return carry

    lax.fori_loop(0, OFFSET, clear, 0)

    def body(window, carry):
        slot, row, col = carry
        side = jnp.where(slot < slots, sides_ref[0, jnp.minimum(slot, slots - 1)], 0)
        info_ref[0, OFFSET + window] = side
        info_ref[1, OFFSET + window] = row
        info_ref[2, OFFSET + window] = col
        end_col = col + 1 >= side
        end_row = row + 1 >= side
        next_slot = jnp.where(end_col & end_row, slot + 1, slot)
        next_row = jnp.where(end_col, jnp.where(end_row, 0, row + 1), row)
        next_col = jnp.where(end_col, 0, col + 1)
        return (next_slot, next_row, next_col)

    zero = jnp.int32(0)
    lax.fori_loop(0, windows, body, (zero, zero, zero))


def window_of(info_ref, window):
    side = info_ref[0, OFFSET + window]
    row = info_ref[1, OFFSET + window]
    col = info_ref[2, OFFSET + window]
    limit = jnp.where(side == 2, 14, jnp.where(side == 3, 18, jnp.where(side == 4, 24, 0)))
    high = jnp.minimum(limit - WS * row, WS)
    wide = jnp.minimum(limit - WS * col, WS)
    return side, row, col, high, wide


def expand(rows_ref, start, high, wide):
    base = pl.multiple_of((start // 16) * 16, 16)
    shift = start - base
    place = iota((SLOT, TALL), 0)
    patch_row, patch_col = place >> 3, place & 7
    hit = (
        (iota((SLOT, TALL), 1) == WS * patch_row + patch_col + shift)
        & (patch_col < wide)
        & (patch_row < high)
    )
    return nn(jnp.where(hit, 1.0, 0.0).astype(BF16), rows_ref[pl.ds(base, TALL), :])


def contract_mask(step, rows):
    first = rows * step
    window = first // CELLS
    shift = first - CELLS * window
    source = iota((rows, BLOCK * SLOT), 1)
    hit = (iota((rows, BLOCK * SLOT), 0) + shift == WS * (source >> 3) + (source & 7)) & (
        (source & 7) < WS
    )
    return window, jnp.where(hit, 1.0, 0.0).astype(BF16)


def near(ext_ref, place, side, row, col):
    lane_col = iota((1, 8, ext_ref.shape[-1]), 1)
    first = jnp.where(col > 0, 0, 8)
    last = jnp.where(col < side - 1, WS - 1, 8)

    def triple(window, rows):
        own = ext_ref[window, rows]
        left = pltpu.roll(ext_ref[window - 1, rows], 2, 1)
        right = pltpu.roll(ext_ref[window + 1, rows], 6, 1)
        return (
            jnp.where(lane_col == first, left, pltpu.roll(own, 1, 1)),
            own,
            jnp.where(lane_col == last, right, pltpu.roll(own, 7, 1)),
        )

    above_on = jnp.where(row > 0, 1.0, 0.0)
    below_on = jnp.where(row < side - 1, 1.0, 0.0)
    above = triple(place - side, slice(WS - 1, WS))
    middle = triple(place, slice(0, WS))
    below = triple(place + side, slice(0, 1))
    return [
        jnp.concatenate([up * above_on, mid, down * below_on], axis=0)
        for up, mid, down in zip(above, middle, below)
    ]


def valid_cells(high, wide, width):
    shape = (WS, 8, width)
    return (iota(shape, 0) < high) & (iota(shape, 1) < wide)


def fold(values):
    rows, width = values.shape
    return jnp.sum(values.reshape(rows // 8, 8, width), axis=0)


def normalize(values):
    centre = values - jnp.mean(values, axis=-1, keepdims=True)
    inverse = lax.rsqrt(jnp.mean(centre * centre, axis=-1, keepdims=True) + 1e-06)
    return centre * inverse, inverse


def normalize_back(gradient, scaled, inverse, gain):
    d_scaled = gradient * gain
    mean_one = jnp.mean(d_scaled, axis=-1, keepdims=True)
    mean_two = jnp.mean(d_scaled * scaled, axis=-1, keepdims=True)
    return inverse * (d_scaled - mean_one - scaled * mean_two)


def stack_heads(values):
    head = iota(values.shape, 1) // HDIM
    zero = jnp.zeros_like(values)
    return jnp.concatenate([jnp.where(head == g, values, zero) for g in range(128 // HDIM)], axis=0)


def pick_heads(stacked):
    head = iota((TALL, 128), 1) // HDIM
    taken = stacked[0:TALL]
    for g in range(1, 128 // HDIM):
        taken = jnp.where(head == g, stacked[TALL * g : TALL * (g + 1)], taken)
    return taken


def to_tall(rows):
    return jnp.concatenate([rows, jnp.zeros((TALL - SLOT, rows.shape[1]), F32)], axis=0).astype(
        BF16
    )


def gelu_parts(values):
    cdf = 0.5 + 0.5 * lax.erf(values * (0.5**0.5))
    density = jnp.exp(-0.5 * values * values) * 0.3989422804014327
    return values * cdf, cdf + values * density


def rows_at(index, size):
    return pl.ds(pl.multiple_of(index * size, size), size)


def take_tokens(first, r, places):
    def source(place, carry):
        _, _, _, high, wide = window_of(r.info, first + place - MARGIN)
        start = HALO - MARGIN * CELLS + CELLS * place
        r.ext[place] = expand(r.rows, start, high, wide).reshape(WS, 8, -1)
        return carry

    lax.fori_loop(places[0], places[1], source, 0)


def take_cotangent(first, r):
    def cotangent(window, carry):
        _, _, _, high, wide = window_of(r.info, first + window)
        r.dout[rows_at(window, SLOT), :] = expand(r.og, CELLS * window, high, wide)
        return carry

    lax.fori_loop(0, r.windows, cotangent, 0, unroll=2)


def field_pass(first, r):
    def pair(step, carry):
        normed = []
        for sub in range(2):
            window = 2 * step + sub
            side, row, col, high, wide = window_of(r.info, first + window)
            bands = near(r.ext, window + MARGIN, side, row, col)
            total = bands[1][1 : 1 + WS] + r.peg_bias[...]
            for a in range(3):
                for b in range(3):
                    tap = 3 * a + b
                    total = total + bands[b][a : a + WS] * r.peg[tap : tap + 1, :]
            total = jnp.where(valid_cells(high, wide, total.shape[-1]), total, 0.0)
            field = total.reshape(SLOT, -1)
            scaled, inverse = normalize(field)
            place = rows_at(window, SLOT)
            r.field[place, :] = field
            r.scaled[place, :] = scaled
            r.inverse[place, :] = inverse
            normed.append(scaled * r.gain[0:1, :] + r.shift[0:1, :])
        r.normed[rows_at(step, 2 * SLOT), :] = jnp.concatenate(normed, axis=0).astype(BF16)
        return carry

    lax.fori_loop(0, r.windows // 2, pair, 0)


def attend(qkv, high, wide, probs_ref, window):
    width = qkv.shape[1] // 3
    key = iota((TALL, 256), 0)
    usable = ((key >> 3) < high) & ((key & 7) < wide)
    halves = []
    for half in range(width // 128):
        query, keys, value = (
            qkv[:, width * t + 128 * half : width * t + 128 * (half + 1)] for t in range(3)
        )
        scores = jnp.where(usable, nt(keys, stack_heads(query)), -1e30)
        top = jnp.max(scores, axis=0, keepdims=True)
        exponent = jnp.exp((scores - top) * HDIM**-0.5)
        probs = exponent * (1.0 / jnp.sum(exponent, axis=0, keepdims=True))
        probs_ref[window, :, 256 * half : 256 * (half + 1)] = probs
        halves.append(pick_heads(tn(probs.astype(BF16), value)))
    return jnp.concatenate(halves, axis=1)


def attend_back(qkv, d_context, probs_ref, window):
    width = qkv.shape[1] // 3
    d_query, d_key, d_value = [], [], []
    for half in range(width // 128):
        query, keys, value = (
            qkv[:, width * t + 128 * half : width * t + 128 * (half + 1)] for t in range(3)
        )
        d_stack = stack_heads(d_context[:, 128 * half : 128 * (half + 1)])
        probs = probs_ref[window, :, 256 * half : 256 * (half + 1)]
        d_value.append(nn(probs.astype(BF16), d_stack))
        d_probs = nt(value, d_stack)
        inner = jnp.sum(d_probs * probs, axis=0, keepdims=True)
        d_score = (probs * (d_probs - inner)).astype(BF16)
        d_key.append(nn(d_score, stack_heads(query)) * HDIM**-0.5)
        d_query.append(pick_heads(tn(d_score, keys)) * HDIM**-0.5)
    return jnp.concatenate(d_query + d_key + d_value, axis=1)


def qkv_weights(r):
    heads, halves = r.at_w.shape[:2]
    return jnp.concatenate(
        [r.at_w[z, half, kind] for kind in range(3) for z in range(heads) for half in range(halves)], axis=0
    )


def proj_weights(r):
    heads, halves = r.at_w.shape[:2]
    return jnp.concatenate([r.at_w[z, half, 3] for z in range(heads) for half in range(halves)], axis=0)


def feed_weights(r, chunk, kind):
    cores, _, heads = r.fc_w.shape[:3]
    return jnp.concatenate(
        [r.fc_w[core, chunk, z, kind] for core in range(cores) for z in range(heads)], axis=0
    )


def attention_block(first, r, step):
    rows = BLOCK * SLOT
    place = rows_at(step, rows)
    width = r.field.shape[1]
    projected = nt(r.normed[place, :], qkv_weights(r))
    context = []
    for sub in range(BLOCK):
        window = BLOCK * step + sub
        _, _, _, high, wide = window_of(r.info, first + window)
        qkv = to_tall(projected[SLOT * sub : SLOT * (sub + 1)])
        r.qkv[window] = qkv
        context.append(attend(qkv, high, wide, r.probs, window)[0:SLOT])
    context = jnp.concatenate(context, axis=0).astype(BF16)
    r.context[place, :] = context
    r.field[place, :] += nn(context, proj_weights(r)) + r.proj_bias[...]


def feed_block(first, r, step):
    rows = BLOCK * SLOT
    place = rows_at(step, rows)
    width = r.field.shape[1]
    hidden = r.field[place, :]
    scaled, inverse = normalize(hidden)
    normed = (scaled * r.gain[1:2, :] + r.shift[1:2, :]).astype(BF16)
    d_output = r.dout[place, :]
    d_low = d_output.astype(BF16)
    normed_t = normed.T
    d_low_t = d_low.T
    ones = jnp.ones((8, rows), BF16)
    result = hidden + r.fc_out_bias[...]
    d_normed = jnp.zeros_like(hidden)
    for chunk in range(r.fc_w.shape[1]):
        w_in, w_out = feed_weights(r, chunk, 0), feed_weights(r, chunk, 1)
        cols = slice(w_in.shape[0] * chunk, w_in.shape[0] * (chunk + 1))
        pre = nt(normed, w_in) + r.fc_in_bias[:, cols]
        active, slope = gelu_parts(pre)
        active = active.astype(BF16)
        d_pre = (nt(d_low, w_out) * slope).astype(BF16)
        result = result + nn(active, w_out)
        d_normed = d_normed + nn(d_pre, w_in)
        r.g_fc_t[0, :, cols] += nn(normed_t, d_pre)
        r.g_fc_t[1, :, cols] += nn(d_low_t, active)
        r.bias[:, cols] += nn(ones, d_pre)
    for sub in range(BLOCK):
        _, _, _, high, wide = window_of(r.info, first + BLOCK * step + sub)
        cells = result[SLOT * sub : SLOT * (sub + 1)].reshape(WS, 8, -1)
        cells = jnp.where(valid_cells(high, wide, width), cells, 0.0)
        r.result[rows_at(BLOCK * step + sub, SLOT), :] = cells.reshape(SLOT, -1)
    d_hidden = d_output + normalize_back(d_normed, scaled, inverse, r.gain[1:2, :])
    r.hidden[place, :] = d_hidden
    d_branch = d_hidden.astype(BF16)
    r.g_proj[...] += nn(r.context[place, :].T, d_branch)
    r.sums[0] += fold(d_branch.astype(F32))
    r.sums[1] += fold(d_output)
    r.sums[3] += fold(d_normed * scaled)
    r.sums[5] += fold(d_normed)


def backward_block(first, r, step):
    rows = BLOCK * SLOT
    place = rows_at(step, rows)
    width = r.field.shape[1]
    d_hidden = r.hidden[place, :]
    d_context = nt(d_hidden.astype(BF16), proj_weights(r))
    d_qkv = []
    for sub in range(BLOCK):
        window = BLOCK * step + sub
        d_window = to_tall(d_context[SLOT * sub : SLOT * (sub + 1)])
        d_qkv.append(attend_back(r.qkv[window], d_window, r.probs, window)[0:SLOT])
    d_qkv = jnp.concatenate(d_qkv, axis=0).astype(BF16)
    d_normed = nn(d_qkv, qkv_weights(r))
    r.g_qkv[...] += nn(r.normed[place, :].T, d_qkv)
    scaled = r.scaled[place, :]
    r.sums[2] += fold(d_normed * scaled)
    r.sums[4] += fold(d_normed)
    d_field = d_hidden + normalize_back(d_normed, scaled, r.inverse[place, :], r.gain[0:1, :])
    for sub in range(BLOCK):
        window = BLOCK * step + sub
        side, row, col, high, wide = window_of(r.info, first + window)
        own = d_field[SLOT * sub : SLOT * (sub + 1)].reshape(WS, 8, -1)
        own = jnp.where(valid_cells(high, wide, width), own, 0.0)
        r.mixed[window + MARGIN] = own
        bands = near(r.ext, window + MARGIN, side, row, col)
        for a in range(3):
            for b in range(3):
                r.sums[6 + 3 * a + b] += jnp.sum(own * bands[b][a : a + WS], axis=0)
        r.sums[15] += jnp.sum(own, axis=0)


def token_pass(first, r, start, stop):
    def body(window, carry):
        side, row, col, high, wide = window_of(r.info, first + window)
        grads = near(r.mixed, window + MARGIN, side, row, col)
        total = grads[1][1 : 1 + WS]
        for a in range(3):
            for b in range(3):
                tap = 3 * a + b
                total = total + grads[2 - b][2 - a : 2 - a + WS] * r.peg[tap : tap + 1, :]
        total = jnp.where(valid_cells(high, wide, total.shape[-1]), total, 0.0)
        r.source[rows_at(window, SLOT), :] = total.reshape(SLOT, -1)
        return carry

    lax.fori_loop(start, stop, body, 0)


def shrink(padded_ref, dense_ref, exact):
    rows = 112

    def body(step, carry):
        window, hit = contract_mask(step, rows)
        values = padded_ref[pl.ds(pl.multiple_of(SLOT * window, 8), BLOCK * SLOT), :]
        high = values.astype(BF16)
        dense = nn(hit, high)
        if exact:
            dense = dense + nn(hit, (values - high.astype(F32)).astype(BF16))
        dense_ref[rows_at(step, rows), :] = dense.astype(dense_ref.dtype)
        return carry

    lax.fori_loop(0, dense_ref.shape[0] // rows, body, 0)


def clear(r):
    for ref in (r.g_fc_t, r.g_proj, r.g_qkv, r.sums, r.bias):
        ref[...] = jnp.zeros_like(ref)
    tail = r.windows * SLOT
    for ref in (r.result, r.source):
        ref[tail:, :] = jnp.zeros((ref.shape[0] - tail, ref.shape[1]), F32)


def turn_feed_gradients(r):
    eye = identity(256)
    cores, quads, heads, _, own, _ = r.g_fc.shape
    for kind in range(2):
        for chunk in range(quads):
            piece = r.g_fc_t[kind, :, 256 * chunk : 256 * (chunk + 1)].astype(BF16)
            turned = nt(eye, piece).astype(BF16)
            for core in range(cores):
                for z in range(heads):
                    place = own * (heads * core + z)
                    r.g_fc[core, chunk, z, kind] = turned[place : place + own]


def turn_attention_gradients(r):
    eye = identity(256)
    halves, _, heads, piece, _ = r.g_at.shape
    for kind in range(4):
        if kind < 3:
            turned = nt(eye, r.g_qkv[:, 256 * kind : 256 * (kind + 1)].astype(BF16)).astype(BF16)
        else:
            turned = r.g_proj[...].astype(BF16)
        for half in range(halves):
            for z in range(heads):
                place = piece * (halves * z + half)
                r.g_at[half, kind, z] = turned[place : place + piece]


def collect_small(r):
    total = jnp.sum(r.sums[...], axis=1)
    r.small[...] = jnp.zeros_like(r.small)
    r.small[0:1, :] = total[0:1]
    for chunk in range(4):
        r.small[1 + chunk : 2 + chunk, :] = r.bias[0:1, 256 * chunk : 256 * (chunk + 1)]
    r.small[5:6, :] = total[1:2]
    r.small[6:10, :] = total[2:6]
    r.small[10:20, :] = total[6:16]


def loop(start, stop, body):
    def step(index, carry):
        body(index)
        return carry

    lax.fori_loop(start, stop, step, 0)


COPIES = 50


def fused_kernel(names, *refs):
    r = SimpleNamespace(**dict(zip(names, refs)))
    r.windows = r.mixed.shape[0] - 2 * MARGIN
    blocks = r.windows // BLOCK
    own_rows = r.tokens.shape[0]
    heads = r.at_w.shape[0]
    quads = r.fc_w.shape[1]
    z, img = lax.axis_index("head"), lax.axis_index("img")
    yx, core = img // 2, img % 2
    other = 1 - core
    first = z * r.windows

    def flip(value, mask):
        low, high = value % 2, value // 2
        low = 1 - low if mask & 1 else low
        high = 1 - high if mask & 2 else high
        return 2 * high + low

    z_peer = {m: (img, flip(z, m)) for m in range(1, heads)}
    yx_peer = {m: (2 * flip(yx, m) + core, z) for m in range(1, quads)}
    sibling = (2 * yx + other, z)
    cross = {m: (2 * flip(yx, m) + other, z) for m in range(1, quads)}
    plane = [yx_peer[m] for m in yx_peer] + [sibling] + [cross[m] for m in cross]

    def copy(index, source, target, device):
        return pltpu.make_async_remote_copy(
            src_ref=source,
            dst_ref=target,
            send_sem=r.send.at[index],
            recv_sem=r.recv.at[index],
            device_id=device,
            device_id_type=MESH,
        )

    forth = copy(0, r.tokens.at[own_rows - HALO : own_rows], r.rows.at[0:HALO], (img, z + 1))
    back = copy(1, r.tokens.at[0:HALO], r.rows.at[HALO + own_rows :], (img, z - 1))
    at_z = [copy(1 + m, r.at_w.at[z, core], r.at_w.at[z, core], z_peer[m]) for m in z_peer]
    at_core = [copy(4 + m, r.at_w.at[flip(z, m), core], r.at_w.at[flip(z, m), core], sibling) for m in z_peer]
    fc_z = [copy(7 + m, r.fc_w.at[core, yx, z], r.fc_w.at[core, yx, z], z_peer[m]) for m in z_peer]
    fc_yx = [copy(10 + m, r.fc_w.at[core, yx], r.fc_w.at[core, yx], yx_peer[m]) for m in yx_peer]
    fc_core = copy(14, r.fc_w.at[core], r.fc_w.at[core], sibling)
    gf_core = copy(15, r.g_fc.at[other], r.gf_one, sibling)
    gf_yx = [copy(15 + m, r.gf_two.at[flip(yx, m)], r.gf_three.at[m - 1], yx_peer[m]) for m in yx_peer]
    gf_z = [copy(18 + m, r.gf_four.at[flip(z, m)], r.gf_five.at[m - 1], z_peer[m]) for m in z_peer]
    ga_core = copy(22, r.g_at.at[other], r.ga_one, sibling)
    ga_yx = [copy(22 + m, r.ga_two.at[flip(yx, m)], r.ga_three.at[m - 1], yx_peer[m]) for m in yx_peer]
    ga_z = [copy(25 + m, r.ga_four.at[flip(z, m)], r.ga_five.at[m - 1], z_peer[m]) for m in z_peer]
    ga_plane = [copy(29 + i, r.ga_all.at[yx, core], r.ga_all.at[yx, core], peer) for i, peer in enumerate(plane)]
    sm_plane = [copy(36 + i, r.small, r.small_plane.at[yx, core], peer) for i, peer in enumerate(plane)]
    sm_z = [copy(42 + m, r.small_sum, r.small_z.at[z], z_peer[m]) for m in z_peer]
    mix_forth = copy(46, r.edge_out.at[0], r.edge_in.at[0], (img, z + 1))
    mix_back = copy(47, r.edge_out.at[1], r.edge_in.at[1], (img, z - 1))

    eye = identity(r.qkv_w.shape[2])
    for kind in range(4):
        turned = nt(eye, r.qkv_w[kind]).astype(BF16) if kind < 3 else r.proj_w[...]
        for half in range(2):
            r.at_w[z, half, kind] = turned[half * (turned.shape[0] // 2) : (half + 1) * (turned.shape[0] // 2)]
    r.fc_w[core, yx, z, 0] = r.fc_in[...]
    r.fc_w[core, yx, z, 1] = r.fc_out[...]
    barrier = pltpu.get_barrier_semaphore()
    greeted = [z_peer[m] for m in z_peer] + plane
    for peer in greeted:
        pl.semaphore_signal(barrier, inc=1, device_id=peer, device_id_type=MESH)

    pl.semaphore_wait(barrier, len(greeted))

    @pl.when(z < heads - 1)
    def _():
        forth.start()

    @pl.when(z > 0)
    def _():
        back.start()

    for one in at_z + fc_z:
        one.start()

    scan_windows(r.sides, r.info, heads * r.windows)
    clear(r)
    r.rows[HALO : HALO + own_rows, :] = r.tokens[...]

    @pl.when(z == 0)
    def _():
        r.rows[0:HALO, :] = jnp.zeros((HALO, r.rows.shape[1]), BF16)

    @pl.when(z == heads - 1)
    def _():
        r.rows[HALO + own_rows :, :] = jnp.zeros((HALO, r.rows.shape[1]), BF16)

    take_cotangent(first, r)

    @pl.when(z > 0)
    def _():
        forth.wait_recv()

    @pl.when(z < heads - 1)
    def _():
        back.wait_recv()

    take_tokens(first, r, (0, 2 * MARGIN + r.windows))
    for one, two in zip(at_z, at_core):
        one.wait_recv()
        two.start()
    for one in fc_z:
        one.wait_recv()
    for one in fc_yx:
        one.start()
    field_pass(first, r)
    for one in at_core:
        one.wait_recv()

    loop(0, 1, lambda step: attention_block(first, r, step))
    for one in fc_yx:
        one.wait_recv()
    fc_core.start()
    loop(1, blocks, lambda step: attention_block(first, r, step))
    fc_core.wait_recv()
    loop(0, blocks, lambda step: feed_block(first, r, step))
    turn_feed_gradients(r)
    gf_core.start()

    def backward(start, stop):
        loop(start, stop, lambda step: backward_block(first, r, (step + blocks - 2) % blocks))

    backward(0, 2)
    gf_core.wait_recv()
    r.gf_two[...] = (r.g_fc[core].astype(F32) + r.gf_one[...].astype(F32)).astype(BF16)
    for one in gf_yx:
        one.start()
    backward(2, 4)
    edge = EDGE * SLOT
    last = r.mixed[MARGIN + r.windows - EDGE : MARGIN + r.windows]
    r.edge_out[0] = last.reshape(edge, -1).astype(BF16)
    r.edge_out[1] = r.mixed[MARGIN : MARGIN + EDGE].reshape(edge, -1).astype(BF16)

    @pl.when(z < heads - 1)
    def _():
        mix_forth.start()

    @pl.when(z > 0)
    def _():
        mix_back.start()

    backward(4, 5)
    for one in gf_yx:
        one.wait_recv()
    total = r.gf_two[yx].astype(F32)
    for m in range(quads - 1):
        total = total + r.gf_three[m].astype(F32)
    r.gf_four[...] = total.astype(BF16)
    for one in gf_z:
        one.start()
    backward(5, blocks)

    turn_attention_gradients(r)
    ga_core.start()
    collect_small(r)
    for one in sm_plane:
        one.start()
    for one in gf_z:
        one.wait_recv()
    total = r.gf_four[z].astype(F32)
    for m in range(heads - 1):
        total = total + r.gf_five[m].astype(F32)
    r.d_fc_in[...] = total[0]
    r.d_fc_out[...] = total[1]

    shape = (MARGIN, WS, 8, r.mixed.shape[-1])
    skip = (EDGE - MARGIN) * SLOT

    @pl.when(z > 0)
    def _():
        mix_forth.wait_recv()
        r.mixed[0:MARGIN] = r.edge_in[0].astype(F32)[skip:].reshape(shape)

    @pl.when(z == 0)
    def _():
        r.mixed[0:MARGIN] = jnp.zeros(shape, F32)

    @pl.when(z < heads - 1)
    def _():
        mix_back.wait_recv()
        r.mixed[MARGIN + r.windows :] = r.edge_in[1].astype(F32)[0 : MARGIN * SLOT].reshape(shape)

    @pl.when(z == heads - 1)
    def _():
        r.mixed[MARGIN + r.windows :] = jnp.zeros(shape, F32)

    shrink(r.result, r.output, False)
    ga_core.wait_recv()
    r.ga_two[...] = (r.g_at[core].astype(F32) + r.ga_one[...].astype(F32)).astype(BF16)
    for one in ga_yx:
        one.start()
    for one in sm_plane:
        one.wait_recv()
    r.small_plane[yx, core] = r.small[...]
    total = jnp.zeros(r.small.shape, F32)
    for a in range(quads):
        for b in range(2):
            total = total + r.small_plane[a, b]
    r.small_sum[...] = total
    for one in sm_z:
        one.start()
    token_pass(first, r, 0, r.windows // 2)
    for one in ga_yx:
        one.wait_recv()
    total = r.ga_two[yx].astype(F32)
    for m in range(quads - 1):
        total = total + r.ga_three[m].astype(F32)
    r.ga_four[...] = total.astype(BF16)
    for one in ga_z:
        one.start()
    token_pass(first, r, r.windows // 2, r.windows)
    for one in ga_z:
        one.wait_recv()
    total = r.ga_four[z].astype(F32)
    for m in range(heads - 1):
        total = total + r.ga_five[m].astype(F32)
    r.ga_all[yx, core] = total.astype(BF16)
    for one in ga_plane:
        one.start()
    shrink(r.source, r.d_tokens, True)
    for one in sm_z:
        one.wait_recv()
    r.small_z[z] = r.small_sum[...]
    total = jnp.zeros(r.small.shape, F32)
    for a in range(heads):
        total = total + r.small_z[a]
    r.d_proj_bias[...] = total[0:1]
    for chunk in range(4):
        r.d_fc_in_bias[:, 256 * chunk : 256 * (chunk + 1)] = total[1 + chunk : 2 + chunk]
    r.d_fc_out_bias[...] = total[5:6]
    r.d_gains[...] = total[6:8]
    r.d_shifts[...] = total[8:10]
    r.d_peg[...] = total[10:19]
    r.d_peg_bias[...] = total[19:20]
    for one in ga_plane:
        one.wait_recv()
    eye = identity(256)
    for kind in range(3):
        r.d_qkv[kind] = nt(eye, r.ga_all[kind].reshape(-1, 256))
    r.d_proj[...] = r.ga_all[3].reshape(-1, 256).astype(F32)

    for one in at_z + at_core + fc_z + fc_yx + [fc_core, gf_core] + gf_yx + gf_z + [ga_core] + ga_yx + ga_z + ga_plane + sm_plane + sm_z:
        one.wait_send()

    @pl.when(z < heads - 1)
    def _():
        forth.wait_send()
        mix_forth.wait_send()

    @pl.when(z > 0)
    def _():
        back.wait_send()
        mix_back.wait_send()


def local_kernel(names, *refs):
    r = SimpleNamespace(**dict(zip(names, refs)))
    r.windows = r.mixed.shape[0] - 2 * MARGIN
    blocks = r.windows // BLOCK
    first = lax.axis_index("head") * r.windows
    scan_windows(r.sides, r.info, r.at_w.shape[0] * r.windows)
    clear(r)
    take_cotangent(first, r)
    take_tokens(first, r, (0, r.windows + 2 * MARGIN))
    field_pass(first, r)
    loop(0, blocks, lambda step: attention_block(first, r, step))
    loop(0, blocks, lambda step: feed_block(first, r, step))
    turn_feed_gradients(r)
    loop(0, blocks, lambda step: backward_block(first, r, step))
    turn_attention_gradients(r)
    collect_small(r)
    shrink(r.result, r.output, False)
    for edge in (slice(0, MARGIN), slice(MARGIN + r.windows, 2 * MARGIN + r.windows)):
        r.mixed[edge] = jnp.zeros((MARGIN,) + r.mixed.shape[1:], F32)


def token_kernel(names, *refs):
    r = SimpleNamespace(**dict(zip(names, refs)))
    r.windows = r.mixed.shape[0] - 2 * MARGIN
    heads = (r.info.shape[1] - 2 * OFFSET) // r.windows
    first = lax.axis_index("head") * r.windows
    scan_windows(r.sides, r.info, heads * r.windows)
    tail = r.windows * SLOT
    r.source[tail:, :] = jnp.zeros((r.source.shape[0] - tail, r.source.shape[1]), F32)
    token_pass(first, r, 0, r.windows)
    shrink(r.source, r.d_tokens, True)


def vmem():
    return pl.BlockSpec(memory_space=pltpu.VMEM)


def smem():
    return pl.BlockSpec(memory_space=pltpu.SMEM)


def work_buffers(windows, heads, width, hidden):
    padded = windows * SLOT
    extra = (windows + BLOCK) * SLOT
    return {
        "info": pltpu.SMEM((3, heads * windows + 2 * OFFSET), jnp.int32),
        "dout": pltpu.VMEM((padded, width), F32),
        "field": pltpu.VMEM((padded, width), F32),
        "scaled": pltpu.VMEM((padded, width), F32),
        "inverse": pltpu.VMEM((padded, 1), F32),
        "normed": pltpu.VMEM((padded, width), BF16),
        "qkv": pltpu.VMEM((windows, TALL, 3 * width), BF16),
        "probs": pltpu.VMEM((windows, TALL, 2 * width), F32),
        "context": pltpu.VMEM((padded, width), BF16),
        "hidden": pltpu.VMEM((padded, width), F32),
        "result": pltpu.VMEM((extra, width), F32),
        "source": pltpu.VMEM((extra, width), F32),
        "g_fc_t": pltpu.VMEM((2, width, hidden), F32),
        "g_proj": pltpu.VMEM((width, width), F32),
        "g_qkv": pltpu.VMEM((width, 3 * width), F32),
        "sums": pltpu.VMEM((16, 8, width), F32),
        "bias": pltpu.VMEM((8, hidden), F32),
    }


def call(kernel, name, inputs, outputs, scratch, **params):
    names = list(inputs) + list(outputs) + list(scratch)
    results = pl.pallas_call(
        functools.partial(kernel, names),
        out_shape=tuple(outputs.values()),
        in_specs=[smem()] + [vmem()] * (len(inputs) - 1),
        out_specs=(vmem(),) * len(outputs),
        scratch_shapes=list(scratch.values()),
        compiler_params=pltpu.CompilerParams(vmem_limit_bytes=VMEM_LIMIT, **params),
        name=name,
    )(*inputs.values())
    return dict(zip(outputs, results))


def on_any_device(tokens, image_sides, qkv_weight, proj_weight, proj_bias, fc_in, fc_in_bias, fc_out, fc_out_bias,
                  norm_gains, norm_shifts, peg_weight, peg_bias, out_grad):
    own_rows, width = tokens.shape
    windows = own_rows // CELLS
    heads = lax.axis_size("head")
    hidden = fc_in_bias.shape[0]
    piece = width // heads // 2
    own = 256 // heads // 2
    shape = jax.ShapeDtypeStruct
    place = lax.axis_index("head") * own_rows
    around = jnp.pad(lax.all_gather(tokens, "head", axis=0, tiled=True), ((HALO, HALO), (0, 0)))
    turned = jnp.concatenate([jnp.swapaxes(qkv_weight, 1, 2), proj_weight[None]], axis=0)
    at_w = lax.all_gather(turned, "head", axis=1, tiled=True)
    fc_w = jnp.stack(
        [lax.all_gather(fc, ("img", "head"), axis=0, tiled=True) for fc in (fc_in, fc_out)]
    )
    edges = (windows + 2 * MARGIN, WS, 8, width)
    out = call(
        local_kernel,
        "block",
        {
            "sides": image_sides,
            "rows": lax.dynamic_slice_in_dim(around, place, own_rows + 2 * HALO, 0),
            "og": out_grad,
            "at_w": at_w.reshape(4, heads, 2, piece, width).transpose(1, 2, 0, 3, 4),
            "fc_w": fc_w.reshape(2, hidden // 256, 2, heads, own, width).transpose(2, 1, 3, 0, 4, 5),
            "proj_bias": proj_bias[None],
            "fc_in_bias": fc_in_bias[None],
            "fc_out_bias": fc_out_bias[None],
            "gain": norm_gains,
            "shift": norm_shifts,
            "peg": peg_weight,
            "peg_bias": peg_bias[None],
        },
        {
            "output": shape((own_rows, width), BF16),
            "mixed": shape(edges, F32),
            "g_fc": shape((2, hidden // 256, heads, 2, own, width), BF16),
            "g_at": shape((2, 4, heads, piece, width), BF16),
            "small": shape((SMALL, width), F32),
        },
        dict(work_buffers(windows, heads, width, hidden), ext=pltpu.VMEM(edges, F32)),
    )
    mixed = out["mixed"]
    last, start = windows, MARGIN
    forth = lax.ppermute(mixed[last : last + MARGIN].astype(BF16), "head", [(i, i + 1) for i in range(heads - 1)])
    back = lax.ppermute(mixed[start : start + MARGIN].astype(BF16), "head", [(i + 1, i) for i in range(heads - 1)])
    own = mixed[MARGIN : MARGIN + windows]
    mixed = jnp.concatenate([forth.astype(F32), own, back.astype(F32)], axis=0)
    d_tokens = call(
        token_kernel,
        "tokens",
        {"sides": image_sides, "mixed": mixed, "peg": peg_weight},
        {"d_tokens": shape((own_rows, width), F32)},
        {name: work_buffers(windows, heads, width, hidden)[name] for name in ("info", "source")},
    )["d_tokens"]
    everywhere = ("img", "head")
    d_fc_in, d_fc_out = (
        lax.psum_scatter(g.reshape(hidden, width).astype(F32), everywhere, scatter_dimension=0, tiled=True)
        for g in out["g_fc"].transpose(3, 1, 0, 2, 4, 5)
    )
    g_at = out["g_at"].transpose(1, 2, 0, 3, 4).reshape(4, width, width).astype(F32)
    g_at = lax.psum(lax.psum_scatter(g_at, "head", scatter_dimension=1, tiled=True), "img")
    small = lax.psum(out["small"], everywhere)
    return (out["output"], d_tokens, jnp.swapaxes(g_at[:3], 1, 2), g_at[3], small[0], d_fc_in, small[1:5].reshape(-1),
            d_fc_out, small[5], small[6:8], small[8:10], small[10:19], small[19])


def on_device(tokens, image_sides, qkv_weight, proj_weight, proj_bias, fc_in, fc_in_bias, fc_out, fc_out_bias,
              norm_gains, norm_shifts, peg_weight, peg_bias, out_grad):
    own_rows, width = tokens.shape
    windows = own_rows // CELLS
    heads = lax.axis_size("head")
    hidden = fc_in_bias.shape[0]
    quads = lax.axis_size("img") // 2
    own = fc_in.shape[0]
    if quads != 4 or heads != 4 or own % 16 != 0:
        return on_any_device(tokens, image_sides, qkv_weight, proj_weight, proj_bias, fc_in, fc_in_bias, fc_out,
                             fc_out_bias, norm_gains, norm_shifts, peg_weight, peg_bias, out_grad)
    piece = width // heads // 2
    shape = jax.ShapeDtypeStruct
    inputs = {
        "sides": image_sides,
        "tokens": tokens,
        "og": out_grad,
        "qkv_w": qkv_weight,
        "proj_w": proj_weight,
        "fc_in": fc_in,
        "fc_out": fc_out,
        "proj_bias": proj_bias[None],
        "fc_in_bias": fc_in_bias[None],
        "fc_out_bias": fc_out_bias[None],
        "gain": norm_gains,
        "shift": norm_shifts,
        "peg": peg_weight,
        "peg_bias": peg_bias[None],
    }
    outputs = {
        "output": shape((own_rows, width), BF16),
        "d_tokens": shape((own_rows, width), F32),
        "d_qkv": shape(qkv_weight.shape, F32),
        "d_proj": shape(proj_weight.shape, F32),
        "d_proj_bias": shape((1, width), F32),
        "d_fc_in": shape(fc_in.shape, F32),
        "d_fc_in_bias": shape((1, hidden), F32),
        "d_fc_out": shape(fc_out.shape, F32),
        "d_fc_out_bias": shape((1, width), F32),
        "d_gains": shape(norm_gains.shape, F32),
        "d_shifts": shape(norm_shifts.shape, F32),
        "d_peg": shape(peg_weight.shape, F32),
        "d_peg_bias": shape((1, width), F32),
    }
    scratch = work_buffers(windows, heads, width, hidden)
    scratch.update({
        "rows": pltpu.VMEM((own_rows + 2 * HALO, width), BF16),
        "ext": pltpu.VMEM((windows + 2 * MARGIN, WS, 8, width), F32),
        "mixed": pltpu.VMEM((windows + 2 * MARGIN, WS, 8, width), F32),
        "edge_out": pltpu.VMEM((2, EDGE * SLOT, width), BF16),
        "edge_in": pltpu.VMEM((2, EDGE * SLOT, width), BF16),
        "at_w": pltpu.VMEM((heads, 2, 4, piece, width), BF16),
        "fc_w": pltpu.VMEM((2, quads, heads, 2, own, width), BF16),
        "g_fc": pltpu.VMEM((2, quads, heads, 2, own, width), BF16),
        "gf_one": pltpu.VMEM((quads, heads, 2, own, width), BF16),
        "gf_two": pltpu.VMEM((quads, heads, 2, own, width), BF16),
        "gf_three": pltpu.VMEM((quads - 1, heads, 2, own, width), BF16),
        "gf_four": pltpu.VMEM((heads, 2, own, width), BF16),
        "gf_five": pltpu.VMEM((heads - 1, 2, own, width), BF16),
        "g_at": pltpu.VMEM((2, 4, heads, piece, width), BF16),
        "ga_one": pltpu.VMEM((4, heads, piece, width), BF16),
        "ga_two": pltpu.VMEM((4, heads, piece, width), BF16),
        "ga_three": pltpu.VMEM((quads - 1, heads, piece, width), BF16),
        "ga_four": pltpu.VMEM((heads, piece, width), BF16),
        "ga_five": pltpu.VMEM((heads - 1, piece, width), BF16),
        "ga_all": pltpu.VMEM((4, 2, piece, width), BF16),
        "small": pltpu.VMEM((SMALL, width), F32),
        "small_plane": pltpu.VMEM((quads, 2, SMALL, width), F32),
        "small_sum": pltpu.VMEM((SMALL, width), F32),
        "small_z": pltpu.VMEM((heads, SMALL, width), F32),
        "send": pltpu.SemaphoreType.DMA((COPIES,)),
        "recv": pltpu.SemaphoreType.DMA((COPIES,)),
    })
    out = call(fused_kernel, "block", inputs, outputs, scratch, collective_id=0, has_side_effects=True)
    for name in ("d_proj_bias", "d_fc_in_bias", "d_fc_out_bias", "d_peg_bias"):
        out[name] = out[name].reshape(-1)
    return tuple(out.values())


def solution(mesh):
    rows = P(("img", "head"), None)
    placed = (rows, P("img", None), P(None, None, "head"), P("head", None), P(), rows, P(), rows, P(), P(), P(), P(), P(), rows)
    return jax.shard_map(
        on_device,
        mesh=mesh,
        in_specs=placed,
        out_specs=(rows, rows, P(None, None, "head"), P("head", None), P(), rows, P(), rows, P(), P(), P(), P(), P()),
        check_vma=False,
    )
```

time: 613 us -> 102 us (0.17)
  waiting for transfers between devices: 289 us -> 0 us
  blocking collectives: 218 us -> 0 us
  Pallas kernels: 73.8 us -> 88.2 us
  between operations: 13.9 us -> 0.73 us
  other arithmetic: 6.53 us -> 0 us
    reduce_scatter x3 -> x0, waiting for transfers between devices: 281 us -> none  [the longest x1 135 us: on_device(): lax.psum_scatter(g_fc[0].astype(F32), ('img', 'head'), scatter_dimension=...]
    all_gather x4 -> x0, blocking collectives: 178 us -> none  [the longest x1 76 us: on_device(): lax.all_gather(fc_in, ('img', 'head'), axis=0, tiled=True)]
    psum x1 -> x0, blocking collectives: 40.6 us -> none  [on_device(): small = lax.psum(small, ('img', 'head'))]
    pallas_call x2 -> x1, Pallas kernels: 73.8 us -> 88.2 us  [call(): pl.pallas_call(functools.partial(kernel, names), out_shape=tuple(outputs....]
    unnamed x10 -> x36, local copies, waits for them, and re-layouts: 0.73 us -> 12.8 us
    ppermute x2 -> x0, waiting for transfers between devices: 6.31 us -> none  [the longest x1 4.52 us: on_device(): right = lax.ppermute(mixed[:MARGIN].astype(BF16), 'head', after).astype(F32)]
  transfers between devices with their start and end apart: 7 -> 0, of which waited for: 5 -> 0; matrix products, arithmetic and copies ran while one was open for 2% -> 0% of each run, Pallas kernels for 2% -> 0%
where the time goes in v2:
time: 102 us
  Pallas kernels  88.2 us (86%)
  local copies, waits for them, and re-layouts  12.8 us (13%)
    pallas_call x1, Pallas kernels, call(): pl.pallas_call(functools.partial(kernel, names), out_shape=tuple(outputs....  88.2 us
    unnamed x36, local copies, waits for them, and re-layouts  12.8 us

profile of v2, /device:TPU:0, one launch (start us, length us, event | category | flops | bytes accessed | tf_op | source)
XLA Modules:
  0.0 101.8 jit_solution(15755791553487134201)
XLA Ops:
  0.6 1.7 %copy.27.refs_3_ = bf16[3,256,64]{2,1,0:T(8,128)(2,1)} copy(bf16[3,256,64]{1,2,0:T(8,128)(2,1)} %param.16) | data formatting | bytes 196608 | tf_op args[2]
  2.4 88.2 %block.1 = (bf16[1568,256]{1,0:T(8,128)(2,1)}, f32[1568,256]{1,0:T(8,128)}, f32[3,256,64]{2,1,0:T(8,128)}, f32[64,256]{1,0:T(8,128)}, f32[1,256]{1,0:T(1,128)}, ...) custom-call(s32[1,32]{1,0:T(1,128)} %refs_0_.1, ...), custom_call_target="tpu_custom_call" | custom-call | tf_op jit(solution)/shard_map/block/pallas_call | solution.py:793
  90.6 0.0 copy-start
  90.6 1.9 %copy.28 = f32[3,256,64]{1,2,0:T(8,128)} copy(f32[3,256,64]{2,1,0:T(8,128)} %get-tuple-element.41) | data formatting | bytes 393216
  92.5 2.1 %copy.41 = bf16[1568,256]{1,0:T(8,128)(2,1)} copy(bf16[1568,256]{1,0:T(8,128)(2,1)} %get-tuple-element.65) | data formatting | bytes 1605632
  94.6 0.0 copy-done
  94.6 0.0 copy-start.5
  94.6 0.0 copy-start.2
  94.6 0.0 copy-start.9
  94.7 0.0 copy-start.7
  94.7 0.0 copy-start.6
  94.7 0.0 copy-start.4
  94.7 0.0 copy-start.8
  94.7 1.2 %copy.42 = f32[1568,256]{1,0:T(8,128)} copy(f32[1568,256]{1,0:T(8,128)S(1)} %copy-done) | data formatting | bytes 3211264
  95.8 0.0 copy-done.1
  95.9 0.6 copy.43
  96.5 0.0 copy-done.10
  96.5 0.6 copy.44
  97.0 0.0 copy-done.3
  97.0 0.6 copy.45
  97.7 0.0 copy-done.5
  97.7 0.6 copy.46
  98.3 0.0 copy-done.2
  98.3 0.6 copy.47
  98.9 0.0 copy-done.9
  98.9 0.6 copy.48
  99.4 0.0 copy-done.7
  99.4 0.6 copy.49
  100.0 0.0 copy-done.6
  100.0 0.6 copy.50
  100.6 0.6 copy.51
  101.2 0.6 copy.52
  (5 shorter events, 0.0 us)
Async XLA Ops:
  90.6 4.0 %copy-start = (f32[1568,256]{1,0:T(8,128)S(1)}, f32[1568,256]{1,0:T(8,128)}, u32[]{:S(2)}) copy-start(f32[1568,256]{1,0:T(8,128)} %get-tuple-element.66) | copy-start | bytes 4816900
  94.6 1.2 %copy-start.1 = (f32[64,256]{1,0:T(8,128)S(1)}, f32[64,256]{1,0:T(8,128)}, u32[]{:S(2)}) copy-start(f32[64,256]{1,0:T(8,128)} %get-tuple-element.68) | copy-start | bytes 196612
  94.6 1.9 %copy-start.10 = (f32[1,256]{1,0:T(1,128)S(1)}, f32[1,256]{1,0:T(1,128)}, u32[]{:S(2)}) copy-start(f32[1,256]{1,0:T(1,128)} %get-tuple-element.30) | copy-start | bytes 3076
  94.6 2.4 %copy-start.3 = (f32[32,256]{1,0:T(8,128)S(1)}, f32[32,256]{1,0:T(8,128)}, u32[]{:S(2)}) copy-start(f32[32,256]{1,0:T(8,128)} %get-tuple-element.70) | copy-start | bytes 98308
  94.6 3.0 %copy-start.5 = (f32[1,1024]{1,0:T(1,128)S(1)}, f32[1,1024]{1,0:T(1,128)}, u32[]{:S(2)}) copy-start(f32[1,1024]{1,0:T(1,128)} %get-tuple-element.32) | copy-start | bytes 12292
  94.6 3.6 %copy-start.2 = (f32[32,256]{1,0:T(8,128)S(1)}, f32[32,256]{1,0:T(8,128)}, u32[]{:S(2)}) copy-start(f32[32,256]{1,0:T(8,128)} %get-tuple-element.72) | copy-start | bytes 98308
  94.6 4.2 %copy-start.9 = (f32[1,256]{1,0:T(1,128)S(1)}, f32[1,256]{1,0:T(1,128)}, u32[]{:S(2)}) copy-start(f32[1,256]{1,0:T(1,128)} %get-tuple-element.34) | copy-start | bytes 3076
  94.7 4.8 %copy-start.7 = (f32[2,256]{1,0:T(2,128)S(1)}, f32[2,256]{1,0:T(2,128)}, u32[]{:S(2)}) copy-start(f32[2,256]{1,0:T(2,128)} %get-tuple-element.74) | copy-start | bytes 6148
  94.7 5.4 %copy-start.6 = (f32[2,256]{1,0:T(2,128)S(1)}, f32[2,256]{1,0:T(2,128)}, u32[]{:S(2)}) copy-start(f32[2,256]{1,0:T(2,128)} %get-tuple-element.75) | copy-start | bytes 6148
  94.7 5.9 %copy-start.4 = (f32[9,256]{1,0:T(8,128)S(1)}, f32[9,256]{1,0:T(8,128)}, u32[]{:S(2)}) copy-start(f32[9,256]{1,0:T(8,128)} %get-tuple-element.76) | copy-start | bytes 27652
  94.7 6.5 %copy-start.8 = (f32[1,256]{1,0:T(1,128)S(1)}, f32[1,256]{1,0:T(1,128)}, u32[]{:S(2)}) copy-start(f32[1,256]{1,0:T(1,128)} %get-tuple-element.38) | copy-start | bytes 3076

commit v3 on v2

v3 whole, which is shorter than its diff:
```python
import functools
from types import SimpleNamespace

import jax
import jax.numpy as jnp
from jax import lax
from jax.experimental import pallas as pl
from jax.experimental.pallas import tpu as pltpu
from jax.sharding import PartitionSpec as P

F32 = jnp.float32
BF16 = jnp.bfloat16
MESH = pl.DeviceIdType.MESH

HDIM = 32
WS = 7
CELLS = WS * WS
SLOT = WS * 8
TALL = 64
MARGIN = 5
HALO = 256
EDGE = 6
OFFSET = 8
BLOCK = 8
FEED = 8
SPAN = 4
SMALL = 32
VMEM_LIMIT = 56 * 1024 * 1024


def nn(left, right):
    return lax.dot_general(left, right, (((1,), (0,)), ((), ())), preferred_element_type=F32)


def nt(left, right):
    return lax.dot_general(left, right, (((1,), (1,)), ((), ())), preferred_element_type=F32)


def tn(left, right):
    return lax.dot_general(left, right, (((0,), (0,)), ((), ())), preferred_element_type=F32)


def iota(shape, axis):
    return lax.broadcasted_iota(jnp.int32, shape, axis)


def identity(size):
    return jnp.where(iota((size, size), 0) == iota((size, size), 1), 1.0, 0.0).astype(BF16)


def scan_windows(sides_ref, info_ref, windows):
    slots = sides_ref.shape[-1]

    def clear(index, carry):
        for kind in range(3):
            info_ref[kind, index] = 0
            info_ref[kind, OFFSET + windows + index] = 0
        return carry

    lax.fori_loop(0, OFFSET, clear, 0)

    def body(window, carry):
        slot, row, col = carry
        side = jnp.where(slot < slots, sides_ref[0, jnp.minimum(slot, slots - 1)], 0)
        info_ref[0, OFFSET + window] = side
        info_ref[1, OFFSET + window] = row
        info_ref[2, OFFSET + window] = col
        end_col = col + 1 >= side
        end_row = row + 1 >= side
        next_slot = jnp.where(end_col & end_row, slot + 1, slot)
        next_row = jnp.where(end_col, jnp.where(end_row, 0, row + 1), row)
        next_col = jnp.where(end_col, 0, col + 1)
        return (next_slot, next_row, next_col)

    zero = jnp.int32(0)
    lax.fori_loop(0, windows, body, (zero, zero, zero))


def window_of(info_ref, window):
    side = info_ref[0, OFFSET + window]
    row = info_ref[1, OFFSET + window]
    col = info_ref[2, OFFSET + window]
    limit = jnp.where(side == 2, 14, jnp.where(side == 3, 18, jnp.where(side == 4, 24, 0)))
    high = jnp.minimum(limit - WS * row, WS)
    wide = jnp.minimum(limit - WS * col, WS)
    return side, row, col, high, wide


def expand(rows_ref, starts, limits):
    place = iota((SLOT, TALL), 0)
    patch_row, patch_col = place >> 3, place & 7
    wanted = WS * patch_row + patch_col - iota((SLOT, TALL), 1)
    hits, bases = [], []
    for start, (high, wide) in zip(starts, limits):
        base = (start // 16) * 16
        base = base if isinstance(base, int) else pl.multiple_of(base, 16)
        hit = (wanted == base - start) & (patch_col < wide) & (patch_row < high)
        hits.append(jnp.where(hit, 1.0, 0.0).astype(BF16))
        bases.append(base)
    return [nn(hit, rows_ref[pl.ds(base, TALL), :]) for hit, base in zip(hits, bases)]


def contract_mask(step, rows):
    first = rows * step
    window = first // CELLS
    shift = first - CELLS * window
    source = iota((rows, SPAN * SLOT), 1)
    hit = (iota((rows, SPAN * SLOT), 0) + shift == WS * (source >> 3) + (source & 7)) & (
        (source & 7) < WS
    )
    return window, jnp.where(hit, 1.0, 0.0).astype(BF16)


def near(ext_ref, place, side, row, col):
    lane_col = iota((1, 8, ext_ref.shape[-1]), 1)
    first = jnp.where(col > 0, 0, 8)
    last = jnp.where(col < side - 1, WS - 1, 8)

    def triple(window, rows):
        own = ext_ref[window, rows]
        left = pltpu.roll(ext_ref[window - 1, rows], 2, 1)
        right = pltpu.roll(ext_ref[window + 1, rows], 6, 1)
        return (
            jnp.where(lane_col == first, left, pltpu.roll(own, 1, 1)),
            own,
            jnp.where(lane_col == last, right, pltpu.roll(own, 7, 1)),
        )

    above_on = jnp.where(row > 0, 1.0, 0.0)
    below_on = jnp.where(row < side - 1, 1.0, 0.0)
    above = triple(place - side, slice(WS - 1, WS))
    middle = triple(place, slice(0, WS))
    below = triple(place + side, slice(0, 1))
    return [
        jnp.concatenate([up * above_on, mid, down * below_on], axis=0)
        for up, mid, down in zip(above, middle, below)
    ]


def valid_cells(high, wide, width):
    shape = (WS, 8, width)
    return (iota(shape, 0) < high) & (iota(shape, 1) < wide)


def fold(values):
    rows, width = values.shape
    return jnp.sum(values.reshape(rows // 8, 8, width), axis=0)


def normalize(values):
    centre = values - jnp.mean(values, axis=-1, keepdims=True)
    inverse = lax.rsqrt(jnp.mean(centre * centre, axis=-1, keepdims=True) + 1e-06)
    return centre * inverse, inverse


def normalize_back(gradient, scaled, inverse, gain):
    d_scaled = gradient * gain
    mean_one = jnp.mean(d_scaled, axis=-1, keepdims=True)
    mean_two = jnp.mean(d_scaled * scaled, axis=-1, keepdims=True)
    return inverse * (d_scaled - mean_one - scaled * mean_two)


def stack_heads(values):
    head = iota(values.shape, 1) // HDIM
    zero = jnp.zeros_like(values)
    return jnp.concatenate([jnp.where(head == g, values, zero) for g in range(128 // HDIM)], axis=0)


def pick_heads(stacked):
    head = iota((TALL, 128), 1) // HDIM
    taken = stacked[0:TALL]
    for g in range(1, 128 // HDIM):
        taken = jnp.where(head == g, stacked[TALL * g : TALL * (g + 1)], taken)
    return taken


def to_tall(rows):
    return jnp.concatenate([rows, jnp.zeros((TALL - SLOT, rows.shape[1]), F32)], axis=0).astype(
        BF16
    )


def gelu_parts(values):
    cdf = 0.5 + 0.5 * lax.erf(values * (0.5**0.5))
    density = jnp.exp(-0.5 * values * values) * 0.3989422804014327
    return values * cdf, cdf + values * density


def rows_at(index, size):
    return pl.ds(pl.multiple_of(index * size, size), size)


def take_tokens(first, r):
    def source(step, carry):
        windows = [BLOCK * step + i for i in range(BLOCK)]
        limits = [window_of(r.info, first + window)[3:] for window in windows]
        starts = [CELLS * window for window in windows]
        for window, rows in zip(windows, expand(r.tokens, starts, limits)):
            r.ext[MARGIN + window] = rows.reshape(WS, 8, -1)
        return carry

    lax.fori_loop(0, r.windows // BLOCK, source, 0)


def take_margin(first, r, rows_ref, skip, place):
    windows = list(range(MARGIN))
    limits = [window_of(r.info, first + place - MARGIN + window)[3:] for window in windows]
    starts = [skip + CELLS * window for window in windows]
    for window, rows in zip(windows, expand(rows_ref, starts, limits)):
        r.ext[place + window] = rows.reshape(WS, 8, -1)


def take_cotangent(first, r):
    def cotangent(step, carry):
        windows = [BLOCK * step + i for i in range(BLOCK)]
        limits = [window_of(r.info, first + window)[3:] for window in windows]
        starts = [CELLS * window for window in windows]
        for window, rows in zip(windows, expand(r.og, starts, limits)):
            r.dout[rows_at(window, SLOT), :] = rows
        return carry

    lax.fori_loop(0, r.windows // BLOCK, cotangent, 0)


def field_pass(first, r, start, stop):
    count = 4

    def body(step, carry):
        totals = []
        for sub in range(count):
            window = count * step + sub
            side, row, col, high, wide = window_of(r.info, first + window)
            bands = near(r.ext, window + MARGIN, side, row, col)
            total = bands[1][1 : 1 + WS] + r.peg_bias[...]
            for a in range(3):
                for b in range(3):
                    tap = 3 * a + b
                    total = total + bands[b][a : a + WS] * r.peg[tap : tap + 1, :]
            total = jnp.where(valid_cells(high, wide, total.shape[-1]), total, 0.0)
            totals.append(total.reshape(SLOT, -1))
        field = jnp.concatenate(totals, axis=0)
        scaled, inverse = normalize(field)
        place = rows_at(step, count * SLOT)
        r.field[place, :] = field
        r.scaled[place, :] = scaled
        r.inverse[place, :] = inverse
        r.normed[place, :] = (scaled * r.gain[0:1, :] + r.shift[0:1, :]).astype(BF16)
        return carry

    lax.fori_loop(start // count, stop // count, body, 0)


def parts_of(qkv, half):
    width = qkv.shape[1] // 3
    return [qkv[:, width * t + 128 * half : width * t + 128 * (half + 1)] for t in range(3)]


def attend(qkvs, limits, probs_ref, windows):
    key = iota((TALL, 256), 0)
    key_row, key_col = key >> 3, key & 7
    usable = [(key_row < high) & (key_col < wide) for high, wide in limits]
    halves = range(qkvs[0].shape[1] // 3 // 128)
    pairs = [(i, half) for i in range(len(windows)) for half in halves]
    parts = [parts_of(qkvs[i], half) for i, half in pairs]
    scores = [nt(keys, stack_heads(query)) for query, keys, _ in parts]
    scores = [jnp.where(usable[i], score, -1e30) for (i, _), score in zip(pairs, scores)]
    tops = [jnp.max(score, axis=0, keepdims=True) for score in scores]
    exponents = [jnp.exp((score - top) * HDIM**-0.5) for score, top in zip(scores, tops)]
    shares = [1.0 / jnp.sum(exponent, axis=0, keepdims=True) for exponent in exponents]
    probs = [exponent * share for exponent, share in zip(exponents, shares)]
    for (i, half), prob in zip(pairs, probs):
        probs_ref[windows[i], :, 256 * half : 256 * (half + 1)] = prob
    context = [tn(prob.astype(BF16), value) for prob, (_, _, value) in zip(probs, parts)]
    context = [pick_heads(one) for one in context]
    return [
        jnp.concatenate([one for (j, _), one in zip(pairs, context) if j == i], axis=1)
        for i in range(len(windows))
    ]


def attend_back(qkvs, d_contexts, probs_ref, windows):
    halves = range(qkvs[0].shape[1] // 3 // 128)
    pairs = [(i, half) for i in range(len(windows)) for half in halves]
    parts = [parts_of(qkvs[i], half) for i, half in pairs]
    stacks = [stack_heads(d_contexts[i][:, 128 * half : 128 * (half + 1)]) for i, half in pairs]
    probs = [probs_ref[windows[i], :, 256 * half : 256 * (half + 1)] for i, half in pairs]
    d_probs = [nt(value, stack) for (_, _, value), stack in zip(parts, stacks)]
    d_value = [nn(prob.astype(BF16), stack) for prob, stack in zip(probs, stacks)]
    inner = [jnp.sum(d * prob, axis=0, keepdims=True) for d, prob in zip(d_probs, probs)]
    d_score = [(prob * (d - one)).astype(BF16) for prob, d, one in zip(probs, d_probs, inner)]
    d_key = [nn(d, stack_heads(query)) * HDIM**-0.5 for d, (query, _, _) in zip(d_score, parts)]
    d_query = [tn(d, keys) for d, (_, keys, _) in zip(d_score, parts)]
    d_query = [pick_heads(one) * HDIM**-0.5 for one in d_query]
    return [
        jnp.concatenate(
            [one for kind in (d_query, d_key, d_value) for (j, _), one in zip(pairs, kind) if j == i],
            axis=1,
        )
        for i in range(len(windows))
    ]


def qkv_weights(r):
    halves, _, heads = r.at_w.shape[:3]
    return jnp.concatenate(
        [r.at_w[half, kind, z] for kind in range(3) for z in range(heads) for half in range(halves)], axis=0
    )


def proj_weights(r):
    halves, _, heads = r.at_w.shape[:3]
    return jnp.concatenate([r.at_w[half, 3, z] for z in range(heads) for half in range(halves)], axis=0)


def feed_weights(r, slot, kind):
    cores, _, heads = r.fc_w.shape[:3]
    return jnp.concatenate(
        [r.fc_w[core, slot, z, kind] for core in range(cores) for z in range(heads)], axis=0
    )


def attention_block(first, r, step):
    rows = BLOCK * SLOT
    place = rows_at(step, rows)
    windows = [BLOCK * step + sub for sub in range(BLOCK)]
    limits = [window_of(r.info, first + window)[3:] for window in windows]
    projected = nt(r.normed[place, :], qkv_weights(r))
    qkvs = [to_tall(projected[SLOT * sub : SLOT * (sub + 1)]) for sub in range(BLOCK)]
    for window, qkv in zip(windows, qkvs):
        r.qkv[window] = qkv
    context = attend(qkvs, limits, r.probs, windows)
    context = jnp.concatenate([one[0:SLOT] for one in context], axis=0).astype(BF16)
    r.context[place, :] = context
    hidden = r.field[place, :] + nn(context, proj_weights(r)) + r.proj_bias[...]
    scaled, inverse = normalize(hidden)
    r.scaled_two[place, :] = scaled
    r.inverse_two[place, :] = inverse
    r.normed_two[place, :] = (scaled * r.gain[1:2, :] + r.shift[1:2, :]).astype(BF16)
    r.result[place, :] = hidden + r.fc_out_bias[...]


def feed_chunk(r, slot, chunk):
    rows = FEED * SLOT
    blocks = r.windows // FEED
    w_in, w_out = feed_weights(r, slot, 0), feed_weights(r, slot, 1)
    bias = r.fc_in_bias[chunk]
    places = [slice(rows * block, rows * (block + 1)) for block in range(blocks)]

    def ahead(block):
        place = places[block]
        return nt(r.normed_two[place, :], w_in), nt(r.dout[place, :].astype(BF16), w_out)

    waiting = ahead(0)
    d_bias = jnp.zeros((8, w_in.shape[0]), F32)
    for block in range(blocks):
        pre, d_active = waiting
        place = places[block]
        if block + 1 < blocks:
            waiting = ahead(block + 1)
        active, slope = gelu_parts(pre + bias)
        active = active.astype(BF16)
        d_pre = d_active * slope
        d_bias = d_bias + fold(d_pre)
        d_pre = d_pre.astype(BF16)
        r.active[place, :] = active
        r.d_pre[place, :] = d_pre
        r.result[place, :] += nn(active, w_out)
        d_normed = nn(d_pre, w_in)
        r.d_two[place, :] = d_normed if slot == 0 else r.d_two[place, :] + d_normed
    r.bias[chunk] = d_bias
    cores, _, heads, _, own, _ = r.g_fc.shape
    d_in = tn(r.d_pre[...], r.normed_two[...]).astype(BF16)
    d_out = tn(r.active[...], r.dout[...].astype(BF16)).astype(BF16)
    for core in range(cores):
        for z in range(heads):
            place = own * (heads * core + z)
            r.g_fc[core, slot, z, 0] = d_in[place : place + own]
            r.g_fc[core, slot, z, 1] = d_out[place : place + own]


def attention_back(first, r, step):
    rows = BLOCK * SLOT
    place = rows_at(step, rows)
    windows = [BLOCK * step + sub for sub in range(BLOCK)]
    d_output = r.dout[place, :]
    scaled = r.scaled_two[place, :]
    d_normed = r.d_two[place, :]
    d_hidden = d_output + normalize_back(d_normed, scaled, r.inverse_two[place, :], r.gain[1:2, :])
    r.hidden[place, :] = d_hidden
    d_branch = d_hidden.astype(BF16)
    d_context = nt(d_branch, proj_weights(r))
    d_context = [to_tall(d_context[SLOT * sub : SLOT * (sub + 1)]) for sub in range(BLOCK)]
    r.g_proj[...] += tn(r.context[place, :], d_branch)
    r.sums[0] += fold(d_branch.astype(F32))
    r.sums[1] += fold(d_output)
    r.sums[3] += fold(d_normed * scaled)
    r.sums[5] += fold(d_normed)
    d_qkv = attend_back([r.qkv[window] for window in windows], d_context, r.probs, windows)
    d_qkv = jnp.concatenate([one[0:SLOT] for one in d_qkv], axis=0).astype(BF16)
    r.d_parts[place, :] = d_qkv
    r.g_qkv[...] += tn(d_qkv, r.normed[place, :])


def field_back(first, r, step):
    rows = BLOCK * SLOT
    place = rows_at(step, rows)
    width = r.field.shape[1]
    d_normed = nn(r.d_parts[place, :], qkv_weights(r))
    scaled = r.scaled[place, :]
    r.sums[2] += fold(d_normed * scaled)
    r.sums[4] += fold(d_normed)
    d_norm = normalize_back(d_normed, scaled, r.inverse[place, :], r.gain[0:1, :])
    d_field = r.hidden[place, :] + d_norm
    taps = [jnp.zeros((8, width), F32) for _ in range(10)]
    for sub in range(BLOCK):
        window = BLOCK * step + sub
        side, row, col, high, wide = window_of(r.info, first + window)
        own = d_field[SLOT * sub : SLOT * (sub + 1)].reshape(WS, 8, -1)
        own = jnp.where(valid_cells(high, wide, width), own, 0.0)
        r.mixed[window + MARGIN] = own
        bands = near(r.ext, window + MARGIN, side, row, col)
        for a in range(3):
            for b in range(3):
                taps[3 * a + b] = taps[3 * a + b] + jnp.sum(own * bands[b][a : a + WS], axis=0)
        taps[9] = taps[9] + jnp.sum(own, axis=0)
    for tap in range(10):
        r.sums[6 + tap] += taps[tap]


def token_pass(first, r, start, stop):
    count = 4

    def body(step, carry):
        for sub in range(count):
            window = start + count * step + sub
            side, row, col, high, wide = window_of(r.info, first + window)
            grads = near(r.mixed, window + MARGIN, side, row, col)
            total = grads[1][1 : 1 + WS]
            for a in range(3):
                for b in range(3):
                    tap = 3 * a + b
                    total = total + grads[2 - b][2 - a : 2 - a + WS] * r.peg[tap : tap + 1, :]
            total = jnp.where(valid_cells(high, wide, total.shape[-1]), total, 0.0)
            r.source[rows_at(window, SLOT), :] = total.reshape(SLOT, -1)
        return carry

    lax.fori_loop(0, (stop - start) // count, body, 0)


def shrink(padded_ref, dense_ref, exact):
    rows, count = 112, 7

    def body(step, carry):
        steps = [count * step + i for i in range(count)]
        masks = [contract_mask(one, rows) for one in steps]
        values = [
            padded_ref[pl.ds(pl.multiple_of(SLOT * window, 8), SPAN * SLOT), :] for window, _ in masks
        ]
        highs = [value.astype(BF16) for value in values]
        dense = [nn(hit, high) for (_, hit), high in zip(masks, highs)]
        if exact:
            lows = [(value - high.astype(F32)).astype(BF16) for value, high in zip(values, highs)]
            dense = [one + nn(hit, low) for one, (_, hit), low in zip(dense, masks, lows)]
        for one, result in zip(steps, dense):
            dense_ref[rows_at(one, rows), :] = result.astype(dense_ref.dtype)
        return carry

    lax.fori_loop(0, dense_ref.shape[0] // rows // count, body, 0)


def clear(r):
    for ref in (r.g_proj, r.g_qkv, r.sums):
        ref[...] = jnp.zeros_like(ref)
    tail = r.windows * SLOT
    for ref in (r.result, r.source):
        ref[tail:, :] = jnp.zeros((ref.shape[0] - tail, ref.shape[1]), F32)


def mask_result(first, r):
    def body(step, carry):
        for sub in range(BLOCK):
            window = BLOCK * step + sub
            _, _, _, high, wide = window_of(r.info, first + window)
            place = rows_at(window, SLOT)
            cells = r.result[place, :].reshape(WS, 8, -1)
            cells = jnp.where(valid_cells(high, wide, cells.shape[-1]), cells, 0.0)
            r.result[place, :] = cells.reshape(SLOT, -1)
        return carry

    lax.fori_loop(0, r.windows // BLOCK, body, 0)


def turn_attention_gradients(r):
    halves, _, heads, piece, width = r.g_at.shape
    for kind in range(4):
        rows = r.g_qkv[width * kind : width * (kind + 1), :] if kind < 3 else r.g_proj[...]
        rows = rows.astype(BF16)
        for half in range(halves):
            for z in range(heads):
                place = piece * (halves * z + half)
                r.g_at[half, kind, z] = rows[place : place + piece]


def collect_small(r):
    total = jnp.sum(r.sums[...], axis=1)
    r.small[...] = jnp.zeros_like(r.small)
    r.small[0:1, :] = total[0:1]
    r.small[1:5, :] = jnp.sum(r.bias[...], axis=1)
    r.small[5:6, :] = total[1:2]
    r.small[6:10, :] = total[2:6]
    r.small[10:20, :] = total[6:16]


def loop(start, stop, body):
    def step(index, carry):
        body(index)
        return carry

    lax.fori_loop(start, stop, step, 0)


COPIES = 55


def fused_kernel(names, *refs):
    r = SimpleNamespace(**dict(zip(names, refs)))
    r.windows = r.mixed.shape[0] - 2 * MARGIN
    blocks = r.windows // BLOCK
    own_rows = r.tokens.shape[0]
    heads = r.at_w.shape[2]
    quads = r.fc_w.shape[1]
    piece = r.at_w.shape[3]
    z, img = lax.axis_index("head"), lax.axis_index("img")
    yx, core = img // 2, img % 2
    other = 1 - core
    first = z * r.windows

    def flip(value, mask):
        low, high = value % 2, value // 2
        low = 1 - low if mask & 1 else low
        high = 1 - high if mask & 2 else high
        return 2 * high + low

    z_peer = {m: (img, flip(z, m)) for m in range(1, heads)}
    yx_peer = {m: (2 * flip(yx, m) + core, z) for m in range(1, quads)}
    sibling = (2 * yx + other, z)
    cross = {m: (2 * flip(yx, m) + other, z) for m in range(1, quads)}
    plane = [yx_peer[m] for m in yx_peer] + [sibling] + [cross[m] for m in cross]
    numbers = iter(range(COPIES))

    def copy(source, target, device):
        index = next(numbers)
        return pltpu.make_async_remote_copy(
            src_ref=source,
            dst_ref=target,
            send_sem=r.send.at[index],
            recv_sem=r.recv.at[index],
            device_id=device,
            device_id_type=MESH,
        )

    forth = copy(r.tokens.at[own_rows - HALO : own_rows], r.halo_low, (img, z + 1))
    back = copy(r.tokens.at[0:HALO], r.halo_high, (img, z - 1))
    at_own = r.at_w.at[core, yx]
    at_z = [copy(at_own.at[z], at_own.at[z], z_peer[m]) for m in z_peer]
    at_yx = [copy(at_own, at_own, yx_peer[m]) for m in yx_peer]
    at_core = copy(r.at_w.at[core], r.at_w.at[core], sibling)
    fc_own = r.fc_w.at[core, 0]
    fc_z = [copy(fc_own.at[z], fc_own.at[z], z_peer[m]) for m in z_peer]
    fc_yx = [copy(fc_own, r.fc_w.at[core, m], yx_peer[m]) for m in yx_peer]
    fc_core = [copy(r.fc_w.at[core, m], r.fc_w.at[core, m], sibling) for m in range(quads)]
    gf_core = [copy(r.g_fc.at[other, m], r.gf_one.at[m], sibling) for m in range(quads)]
    gf_yx = [copy(r.gf_two.at[m], r.gf_three.at[m - 1], yx_peer[m]) for m in yx_peer]
    gf_z = [copy(r.gf_four.at[flip(z, m)], r.gf_five.at[m - 1], z_peer[m]) for m in z_peer]
    ga_core = copy(r.g_at.at[other], r.ga_one, sibling)
    ga_yx = [copy(r.ga_two.at[flip(yx, m)], r.ga_three.at[m - 1], yx_peer[m]) for m in yx_peer]
    ga_z = [copy(r.ga_four.at[flip(z, m)], r.ga_five.at[m - 1], z_peer[m]) for m in z_peer]
    ga_plane = [copy(r.ga_all.at[yx, core], r.ga_all.at[yx, core], peer) for peer in plane]
    sm_plane = [copy(r.small, r.small_plane.at[yx, core], peer) for peer in plane]
    sm_z = [copy(r.small_sum, r.small_z.at[z], z_peer[m]) for m in z_peer]
    mix_forth = copy(r.edge_out.at[0], r.edge_in.at[0], (img, z + 1))
    mix_back = copy(r.edge_out.at[1], r.edge_in.at[1], (img, z - 1))
    has_next, has_last = z < heads - 1, z > 0

    def start(copies):
        for one in copies:
            one.start()

    def arrive(copies):
        for one in copies:
            one.wait_recv()

    def total_of(own, others):
        total = own.astype(F32)
        for index in range(others.shape[0]):
            total = total + others[index].astype(F32)
        return total

    for kind in range(4):
        rows = r.qkv_w[kind] if kind < 3 else r.proj_w[...]
        for half in range(2):
            r.at_own[kind, half] = rows[piece * half : piece * (half + 1)]
    r.at_w[core, yx, z] = r.at_own[yx, core]
    r.fc_w[core, 0, z, 0] = r.fc_in[...]
    r.fc_w[core, 0, z, 1] = r.fc_out[...]
    barrier = pltpu.get_barrier_semaphore()
    greeted = [z_peer[m] for m in z_peer] + plane
    for peer in greeted:
        pl.semaphore_signal(barrier, inc=1, device_id=peer, device_id_type=MESH)
    scan_windows(r.sides, r.info, heads * r.windows)
    pl.semaphore_wait(barrier, len(greeted))
    start(at_z)

    @pl.when(has_next)
    def _():
        forth.start()

    @pl.when(has_last)
    def _():
        back.start()

    take_cotangent(first, r)
    start(fc_z)
    clear(r)
    take_tokens(first, r)
    arrive(at_z)
    start(at_yx)
    field_pass(first, r, BLOCK, r.windows - BLOCK)
    margin = (MARGIN,) + r.ext.shape[1:]

    @pl.when(has_last)
    def _():
        forth.wait_recv()
        take_margin(first, r, r.halo_low, HALO - MARGIN * CELLS, 0)

    @pl.when(z == 0)
    def _():
        r.ext[0:MARGIN] = jnp.zeros(margin, F32)

    @pl.when(has_next)
    def _():
        back.wait_recv()
        take_margin(first, r, r.halo_high, 0, MARGIN + r.windows)

    @pl.when(z == heads - 1)
    def _():
        r.ext[MARGIN + r.windows :] = jnp.zeros(margin, F32)

    arrive(fc_z)
    start(fc_yx)
    fc_core[0].start()
    field_pass(first, r, 0, BLOCK)
    field_pass(first, r, r.windows - BLOCK, r.windows)
    arrive(at_yx)
    at_core.start()
    at_core.wait_recv()
    loop(0, 2, lambda step: attention_block(first, r, step))
    for one, two in zip(fc_yx, fc_core[1:]):
        one.wait_recv()
        two.start()
    loop(2, blocks, lambda step: attention_block(first, r, step))

    def add_cores(m):
        gf_core[m].wait_recv()
        r.gf_two[m] = (r.g_fc[core, m].astype(F32) + r.gf_one[m].astype(F32)).astype(BF16)
        if m > 0:
            gf_yx[m - 1].start()

    for m in range(quads):
        fc_core[m].wait_recv()
        feed_chunk(r, m, flip(yx, m))
        gf_core[m].start()
        if m > 0:
            add_cores(m - 1)

    def attention(start, stop):
        loop(start, stop, lambda step: attention_back(first, r, step))

    attention(0, 1)
    add_cores(quads - 1)
    attention(1, 3)
    arrive(gf_yx)
    r.gf_four[...] = total_of(r.gf_two[0], r.gf_three).astype(BF16)
    start(gf_z)
    attention(3, blocks)
    turn_attention_gradients(r)
    ga_core.start()

    def field(start, stop):
        loop(start, stop, lambda step: field_back(first, r, (step + blocks - 1) % blocks))

    field(0, 2)
    edge = EDGE * SLOT
    last = r.mixed[MARGIN + r.windows - EDGE : MARGIN + r.windows]
    r.edge_out[0] = last.reshape(edge, -1).astype(BF16)
    r.edge_out[1] = r.mixed[MARGIN : MARGIN + EDGE].reshape(edge, -1).astype(BF16)

    @pl.when(has_next)
    def _():
        mix_forth.start()

    @pl.when(has_last)
    def _():
        mix_back.start()

    ga_core.wait_recv()
    r.ga_two[...] = (r.g_at[core].astype(F32) + r.ga_one[...].astype(F32)).astype(BF16)
    start(ga_yx)
    field(2, blocks)
    collect_small(r)
    start(sm_plane)
    mask_result(first, r)
    shrink(r.result, r.output, False)
    arrive(gf_z)
    total = total_of(r.gf_four[z], r.gf_five)
    r.d_fc_in[...] = total[0]
    r.d_fc_out[...] = total[1]
    token_pass(first, r, BLOCK, r.windows - BLOCK)
    arrive(ga_yx)
    r.ga_four[...] = total_of(r.ga_two[yx], r.ga_three).astype(BF16)
    start(ga_z)
    arrive(sm_plane)
    r.small_plane[yx, core] = r.small[...]
    total = jnp.zeros(r.small.shape, F32)
    for a in range(quads):
        for b in range(2):
            total = total + r.small_plane[a, b]
    r.small_sum[...] = total
    start(sm_z)
    skip = (EDGE - MARGIN) * SLOT

    @pl.when(has_last)
    def _():
        mix_forth.wait_recv()
        r.mixed[0:MARGIN] = r.edge_in[0].astype(F32)[skip:].reshape(margin)

    @pl.when(z == 0)
    def _():
        r.mixed[0:MARGIN] = jnp.zeros(margin, F32)

    @pl.when(has_next)
    def _():
        mix_back.wait_recv()
        r.mixed[MARGIN + r.windows :] = r.edge_in[1].astype(F32)[0 : MARGIN * SLOT].reshape(margin)

    @pl.when(z == heads - 1)
    def _():
        r.mixed[MARGIN + r.windows :] = jnp.zeros(margin, F32)

    token_pass(first, r, 0, BLOCK)
    token_pass(first, r, r.windows - BLOCK, r.windows)
    arrive(ga_z)
    r.ga_all[yx, core] = total_of(r.ga_four[z], r.ga_five).astype(BF16)
    start(ga_plane)
    shrink(r.source, r.d_tokens, True)
    arrive(sm_z)
    r.small_z[z] = r.small_sum[...]
    total = jnp.zeros(r.small.shape, F32)
    for a in range(heads):
        total = total + r.small_z[a]
    r.small_out[...] = total
    arrive(ga_plane)
    for kind in range(4):
        for half in range(2):
            rows = r.ga_all[kind, half].astype(F32)
            place = slice(piece * half, piece * (half + 1))
            if kind < 3:
                r.d_qkv[kind, place, :] = rows
            else:
                r.d_proj[place, :] = rows

    sent = at_z + at_yx + [at_core] + fc_z + fc_yx + fc_core + gf_core + gf_yx + gf_z + [ga_core] + ga_yx + ga_z
    for one in sent + ga_plane + sm_plane + sm_z:
        one.wait_send()

    @pl.when(has_next)
    def _():
        forth.wait_send()
        mix_forth.wait_send()

    @pl.when(has_last)
    def _():
        back.wait_send()
        mix_back.wait_send()


def local_kernel(names, *refs):
    r = SimpleNamespace(**dict(zip(names, refs)))
    r.windows = r.mixed.shape[0] - 2 * MARGIN
    blocks = r.windows // BLOCK
    first = lax.axis_index("head") * r.windows
    scan_windows(r.sides, r.info, r.at_w.shape[2] * r.windows)
    clear(r)
    take_cotangent(first, r)
    take_tokens(first, r)
    take_margin(first, r, r.halo_low, HALO - MARGIN * CELLS, 0)
    take_margin(first, r, r.halo_high, 0, MARGIN + r.windows)
    field_pass(first, r, 0, r.windows)
    loop(0, blocks, lambda step: attention_block(first, r, step))
    for chunk in range(r.fc_w.shape[1]):
        feed_chunk(r, chunk, chunk)
    loop(0, blocks, lambda step: attention_back(first, r, step))
    loop(0, blocks, lambda step: field_back(first, r, step))
    turn_attention_gradients(r)
    collect_small(r)
    mask_result(first, r)
    shrink(r.result, r.output, False)
    for edge in (slice(0, MARGIN), slice(MARGIN + r.windows, 2 * MARGIN + r.windows)):
        r.mixed[edge] = jnp.zeros((MARGIN,) + r.mixed.shape[1:], F32)


def token_kernel(names, *refs):
    r = SimpleNamespace(**dict(zip(names, refs)))
    r.windows = r.mixed.shape[0] - 2 * MARGIN
    heads = (r.info.shape[1] - 2 * OFFSET) // r.windows
    first = lax.axis_index("head") * r.windows
    scan_windows(r.sides, r.info, heads * r.windows)
    tail = r.windows * SLOT
    r.source[tail:, :] = jnp.zeros((r.source.shape[0] - tail, r.source.shape[1]), F32)
    token_pass(first, r, 0, r.windows)
    shrink(r.source, r.d_tokens, True)


def vmem():
    return pl.BlockSpec(memory_space=pltpu.VMEM)


def smem():
    return pl.BlockSpec(memory_space=pltpu.SMEM)


def work_buffers(windows, heads, width, hidden):
    padded = windows * SLOT
    extra = (windows + SPAN) * SLOT
    return {
        "info": pltpu.SMEM((3, heads * windows + 2 * OFFSET), jnp.int32),
        "dout": pltpu.VMEM((padded, width), F32),
        "field": pltpu.VMEM((padded, width), F32),
        "scaled": pltpu.VMEM((padded, width), F32),
        "inverse": pltpu.VMEM((padded, 1), F32),
        "normed": pltpu.VMEM((padded, width), BF16),
        "qkv": pltpu.VMEM((windows, TALL, 3 * width), BF16),
        "probs": pltpu.VMEM((windows, TALL, 2 * width), F32),
        "context": pltpu.VMEM((padded, width), BF16),
        "hidden": pltpu.VMEM((padded, width), F32),
        "result": pltpu.VMEM((extra, width), F32),
        "source": pltpu.VMEM((extra, width), F32),
        "scaled_two": pltpu.VMEM((padded, width), F32),
        "inverse_two": pltpu.VMEM((padded, 1), F32),
        "normed_two": pltpu.VMEM((padded, width), BF16),
        "d_two": pltpu.VMEM((padded, width), F32),
        "active": pltpu.VMEM((padded, 256), BF16),
        "d_pre": pltpu.VMEM((padded, 256), BF16),
        "d_parts": pltpu.VMEM((padded, 3 * width), BF16),
        "g_proj": pltpu.VMEM((width, width), F32),
        "g_qkv": pltpu.VMEM((3 * width, width), F32),
        "sums": pltpu.VMEM((16, 8, width), F32),
        "bias": pltpu.VMEM((hidden // 256, 8, 256), F32),
    }


def call(kernel, name, inputs, outputs, scratch, **params):
    names = list(inputs) + list(outputs) + list(scratch)
    results = pl.pallas_call(
        functools.partial(kernel, names),
        out_shape=tuple(outputs.values()),
        in_specs=[smem()] + [vmem()] * (len(inputs) - 1),
        out_specs=(vmem(),) * len(outputs),
        scratch_shapes=list(scratch.values()),
        compiler_params=pltpu.CompilerParams(vmem_limit_bytes=VMEM_LIMIT, **params),
        name=name,
    )(*inputs.values())
    return dict(zip(outputs, results))


def on_any_device(tokens, image_sides, qkv_weight, proj_weight, proj_bias, fc_in, fc_in_bias, fc_out, fc_out_bias,
                  norm_gains, norm_shifts, peg_weight, peg_bias, out_grad):
    own_rows, width = tokens.shape
    windows = own_rows // CELLS
    heads = lax.axis_size("head")
    hidden = fc_in_bias.shape[0]
    piece = width // heads // 2
    own = 256 // heads // 2
    shape = jax.ShapeDtypeStruct
    place = lax.axis_index("head") * own_rows
    around = jnp.pad(lax.all_gather(tokens, "head", axis=0, tiled=True), ((HALO, HALO), (0, 0)))
    halo = jnp.stack(
        [lax.dynamic_slice_in_dim(around, place + shift, HALO, 0) for shift in (0, own_rows + HALO)]
    )
    turned = jnp.concatenate([jnp.swapaxes(qkv_weight, 1, 2), proj_weight[None]], axis=0)
    at_w = lax.all_gather(turned, "head", axis=1, tiled=True)
    fc_w = jnp.stack(
        [lax.all_gather(fc, ("img", "head"), axis=0, tiled=True) for fc in (fc_in, fc_out)]
    )
    edges = (windows + 2 * MARGIN, WS, 8, width)
    out = call(
        local_kernel,
        "block",
        {
            "sides": image_sides,
            "tokens": tokens,
            "halo_low": halo[0],
            "halo_high": halo[1],
            "og": out_grad,
            "at_w": at_w.reshape(4, heads, 2, piece, width).transpose(2, 0, 1, 3, 4),
            "fc_w": fc_w.reshape(2, hidden // 256, 2, heads, own, width).transpose(2, 1, 3, 0, 4, 5),
            "proj_bias": proj_bias[None],
            "fc_in_bias": fc_in_bias.reshape(-1, 1, 256),
            "fc_out_bias": fc_out_bias[None],
            "gain": norm_gains,
            "shift": norm_shifts,
            "peg": peg_weight,
            "peg_bias": peg_bias[None],
        },
        {
            "output": shape((own_rows, width), BF16),
            "mixed": shape(edges, F32),
            "g_fc": shape((2, hidden // 256, heads, 2, own, width), BF16),
            "g_at": shape((2, 4, heads, piece, width), BF16),
            "small": shape((SMALL, width), F32),
        },
        dict(work_buffers(windows, heads, width, hidden), ext=pltpu.VMEM(edges, F32)),
    )
    mixed = out["mixed"]
    last, start = windows, MARGIN
    forth = lax.ppermute(mixed[last : last + MARGIN].astype(BF16), "head", [(i, i + 1) for i in range(heads - 1)])
    back = lax.ppermute(mixed[start : start + MARGIN].astype(BF16), "head", [(i + 1, i) for i in range(heads - 1)])
    own = mixed[MARGIN : MARGIN + windows]
    mixed = jnp.concatenate([forth.astype(F32), own, back.astype(F32)], axis=0)
    d_tokens = call(
        token_kernel,
        "tokens",
        {"sides": image_sides, "mixed": mixed, "peg": peg_weight},
        {"d_tokens": shape((own_rows, width), F32)},
        {name: work_buffers(windows, heads, width, hidden)[name] for name in ("info", "source")},
    )["d_tokens"]
    everywhere = ("img", "head")
    d_fc_in, d_fc_out = (
        lax.psum_scatter(g.reshape(hidden, width).astype(F32), everywhere, scatter_dimension=0, tiled=True)
        for g in out["g_fc"].transpose(3, 1, 0, 2, 4, 5)
    )
    g_at = out["g_at"].transpose(1, 2, 0, 3, 4).reshape(4, width, width).astype(F32)
    g_at = lax.psum(lax.psum_scatter(g_at, "head", scatter_dimension=1, tiled=True), "img")
    small = lax.psum(out["small"], everywhere)
    return (out["output"], d_tokens, jnp.swapaxes(g_at[:3], 1, 2), g_at[3], small[0], d_fc_in, small[1:5].reshape(-1),
            d_fc_out, small[5], small[6:8], small[8:10], small[10:19], small[19])


def on_device(tokens, image_sides, qkv_weight, proj_weight, proj_bias, fc_in, fc_in_bias, fc_out, fc_out_bias,
              norm_gains, norm_shifts, peg_weight, peg_bias, out_grad):
    own_rows, width = tokens.shape
    windows = own_rows // CELLS
    heads = lax.axis_size("head")
    hidden = fc_in_bias.shape[0]
    quads = lax.axis_size("img") // 2
    own = fc_in.shape[0]
    if quads != 4 or heads != 4 or own % 16 != 0:
        return on_any_device(tokens, image_sides, qkv_weight, proj_weight, proj_bias, fc_in, fc_in_bias, fc_out,
                             fc_out_bias, norm_gains, norm_shifts, peg_weight, peg_bias, out_grad)
    piece = width // heads // 2
    shape = jax.ShapeDtypeStruct
    inputs = {
        "sides": image_sides,
        "tokens": tokens,
        "og": out_grad,
        "qkv_w": jnp.swapaxes(qkv_weight, 1, 2),
        "proj_w": proj_weight,
        "fc_in": fc_in,
        "fc_out": fc_out,
        "proj_bias": proj_bias[None],
        "fc_in_bias": fc_in_bias.reshape(-1, 1, 256),
        "fc_out_bias": fc_out_bias[None],
        "gain": norm_gains,
        "shift": norm_shifts,
        "peg": peg_weight,
        "peg_bias": peg_bias[None],
    }
    large = {
        "output": shape((own_rows, width), BF16),
        "d_tokens": shape((own_rows, width), F32),
        "d_qkv": shape((3, width // heads, width), F32),
        "d_proj": shape(proj_weight.shape, F32),
        "d_fc_in": shape(fc_in.shape, F32),
        "d_fc_out": shape(fc_out.shape, F32),
    }
    scratch = work_buffers(windows, heads, width, hidden)
    scratch.update({
        "halo_low": pltpu.VMEM((HALO, width), BF16),
        "halo_high": pltpu.VMEM((HALO, width), BF16),
        "ext": pltpu.VMEM((windows + 2 * MARGIN, WS, 8, width), F32),
        "mixed": pltpu.VMEM((windows + 2 * MARGIN, WS, 8, width), F32),
        "edge_out": pltpu.VMEM((2, EDGE * SLOT, width), BF16),
        "edge_in": pltpu.VMEM((2, EDGE * SLOT, width), BF16),
        "at_w": pltpu.VMEM((2, 4, heads, piece, width), BF16),
        "at_own": pltpu.VMEM((4, 2, piece, width), BF16),
        "fc_w": pltpu.VMEM((2, quads, heads, 2, own, width), BF16),
        "g_fc": pltpu.VMEM((2, quads, heads, 2, own, width), BF16),
        "gf_one": pltpu.VMEM((quads, heads, 2, own, width), BF16),
        "gf_two": pltpu.VMEM((quads, heads, 2, own, width), BF16),
        "gf_three": pltpu.VMEM((quads - 1, heads, 2, own, width), BF16),
        "gf_four": pltpu.VMEM((heads, 2, own, width), BF16),
        "gf_five": pltpu.VMEM((heads - 1, 2, own, width), BF16),
        "g_at": pltpu.VMEM((2, 4, heads, piece, width), BF16),
        "ga_one": pltpu.VMEM((4, heads, piece, width), BF16),
        "ga_two": pltpu.VMEM((4, heads, piece, width), BF16),
        "ga_three": pltpu.VMEM((quads - 1, heads, piece, width), BF16),
        "ga_four": pltpu.VMEM((heads, piece, width), BF16),
        "ga_five": pltpu.VMEM((heads - 1, piece, width), BF16),
        "ga_all": pltpu.VMEM((4, 2, piece, width), BF16),
        "small_plane": pltpu.VMEM((quads, 2, SMALL, width), F32),
        "small_sum": pltpu.VMEM((SMALL, width), F32),
        "small_z": pltpu.VMEM((heads, SMALL, width), F32),
        "small": pltpu.VMEM((SMALL, width), F32),
        "send": pltpu.SemaphoreType.DMA((COPIES,)),
        "recv": pltpu.SemaphoreType.DMA((COPIES,)),
    })
    made = call(
        fused_kernel,
        "block",
        inputs,
        dict(large, small_out=shape((SMALL, width), F32)),
        scratch,
        collective_id=0,
        has_side_effects=True,
    )
    small = {
        "d_proj_bias": shape((1, width), F32),
        "d_fc_in_bias": shape((1, hidden), F32),
        "d_fc_out_bias": shape((1, width), F32),
        "d_gains": shape(norm_gains.shape, F32),
        "d_shifts": shape(norm_shifts.shape, F32),
        "d_peg": shape(peg_weight.shape, F32),
        "d_peg_bias": shape((1, width), F32),
    }
    count = len(large)

    def hand_out(*refs):
        sources, targets = refs[: count + 1], refs[count + 1 :]
        for source, target in zip(sources[:count], targets[:count]):
            target[...] = source[...]
        row = 0
        for target in targets[count:]:
            for part in range(target.shape[1] // width):
                rows = target.shape[0]
                target[:, width * part : width * (part + 1)] = sources[count][row : row + rows, :]
                row += rows

    results = pl.pallas_call(
        hand_out,
        out_shape=tuple(large.values()) + tuple(small.values()),
        in_specs=[vmem()] * (count + 1),
        out_specs=(vmem(),) * (count + len(small)),
        compiler_params=pltpu.CompilerParams(vmem_limit_bytes=VMEM_LIMIT),
        name="hand_out",
    )(*made.values())
    out = dict(zip(list(large) + list(small), results))
    out["d_qkv"] = jnp.swapaxes(out["d_qkv"], 1, 2)
    for name in ("d_proj_bias", "d_fc_in_bias", "d_fc_out_bias", "d_peg_bias"):
        out[name] = out[name].reshape(-1)
    order = ("output", "d_tokens", "d_qkv", "d_proj", "d_proj_bias", "d_fc_in", "d_fc_in_bias", "d_fc_out", "d_fc_out_bias",
             "d_gains", "d_shifts", "d_peg", "d_peg_bias")
    return tuple(out[name] for name in order)


def solution(mesh):
    rows = P(("img", "head"), None)
    placed = (rows, P("img", None), P(None, None, "head"), P("head", None), P(), rows, P(), rows, P(), P(), P(), P(), P(), rows)
    return jax.shard_map(
        on_device,
        mesh=mesh,
        in_specs=placed,
        out_specs=(rows, rows, P(None, None, "head"), P("head", None), P(), rows, P(), rows, P(), P(), P(), P(), P()),
        check_vma=False,
    )
```

time: 102 us -> 66.1 us (0.65)
  Pallas kernels: 88.2 us -> 65.1 us
  local copies, waits for them, and re-layouts: 12.8 us -> 0 us
    pallas_call x1, Pallas kernels: 88.2 us -> 61.8 us  [call(): pl.pallas_call(functools.partial(kernel, names), out_shape=tuple(outputs....]
    unnamed x36 -> x0, local copies, waits for them, and re-layouts: 12.8 us -> none
    pallas_call x0 -> x1, Pallas kernels: none -> 3.33 us  [on_device(): pl.pallas_call(hand_out, out_shape=tuple(large.values()) + tuple(small.va...]
where the time goes in v3:
time: 66.1 us; the launch traced here: 66 us
  Pallas kernels  65.1 us (98%)
  between operations  0.84 us (1%)
    pallas_call x1, Pallas kernels, call(): pl.pallas_call(functools.partial(kernel, names), out_shape=tuple(outputs....  61.8 us
    pallas_call x1, Pallas kernels, on_device(): pl.pallas_call(hand_out, out_shape=tuple(large.values()) + tuple(small.va...  3.33 us

profile of v3, /device:TPU:0, one launch (start us, length us, event | category | flops | bytes accessed | tf_op | source)
XLA Modules:
  0.0 66.0 jit_solution(5663964042376043588)
XLA Ops:
  0.7 61.8 %block.1 = (bf16[1568,256]{1,0:T(8,128)(2,1)}, f32[1568,256]{1,0:T(8,128)}, f32[3,64,256]{2,1,0:T(8,128)}, f32[64,256]{1,0:T(8,128)}, f32[32,256]{1,0:T(8,128)}, /*index=5*/f32[32,256]{1,0:T(8,128)}, f32[32,256]{1,0:T(8,128)}) custom-call(s32[1,32]{1,0:T(1,128)} %refs_0_.1, bf16[1568,256]{1,0:T(8,128)(2,1)} %refs_1_.1, bf16[1568,256]{1,0:T(8,128)(2,1)} %refs_2_.1, ...), custom_call_target="tpu_custom_call" | custom-call | tf_op jit(solution)/shard_map/block/pallas_call | solution.py:864
  62.5 3.3 %hand_out.1 = (bf16[1568,256]{1,0:T(8,128)(2,1)}, f32[1568,256]{1,0:T(8,128)}, f32[3,64,256]{2,1,0:T(8,128)}, f32[64,256]{1,0:T(8,128)}, f32[32,256]{1,0:T(8,128...) custom-call(bf16[1568,256]{1,0:T(8,128)(2,1)} %get-tuple-element.33., ...), custom_call_target="tpu_custom_call" | custom-call | tf_op jit(solution)/shard_map/hand_out/pallas_call | solution.py:1048

commit v4 on v3

--- a/solution.py
+++ b/solution.py
@@ -19,12 +19,12 @@
 TALL = 64
 MARGIN = 5
 HALO = 256
-EDGE = 6
+EDGE = 96
 OFFSET = 8
 BLOCK = 8
 FEED = 8
 SPAN = 4
-SMALL = 32
+SMALL = 24
 VMEM_LIMIT = 56 * 1024 * 1024
 
 
@@ -135,6 +135,20 @@
         jnp.concatenate([up * above_on, mid, down * below_on], axis=0)
         for up, mid, down in zip(above, middle, below)
     ]
+
+
+def edge_of(ext_ref, full, rest, patch_row):
+    width = ext_ref.shape[-1]
+    tiles = [ext_ref[full].reshape(SLOT, width)] + [ext_ref[window, patch_row] for window in rest]
+    rows = SLOT + 8 * len(rest)
+    return jnp.concatenate(tiles + [jnp.zeros((EDGE - rows, width), F32)], axis=0).astype(BF16)
+
+
+def edge_to(ext_ref, full, rest, patch_row, edge):
+    edge = edge.astype(F32)
+    ext_ref[full] = edge[0:SLOT].reshape(WS, 8, -1)
+    for index, window in enumerate(rest):
+        ext_ref[window, patch_row] = edge[SLOT + 8 * index : SLOT + 8 * (index + 1)]
 
 
 def valid_cells(high, wide, width):
@@ -301,15 +315,15 @@
 
 
 def qkv_weights(r):
-    halves, _, heads = r.at_w.shape[:3]
+    halves, heads = r.at_w.shape[:2]
     return jnp.concatenate(
-        [r.at_w[half, kind, z] for kind in range(3) for z in range(heads) for half in range(halves)], axis=0
+        [r.at_w[half, z, kind] for kind in range(3) for z in range(heads) for half in range(halves)], axis=0
     )
 
 
 def proj_weights(r):
-    halves, _, heads = r.at_w.shape[:3]
-    return jnp.concatenate([r.at_w[half, 3, z] for z in range(heads) for half in range(halves)], axis=0)
+    halves, heads = r.at_w.shape[:2]
+    return jnp.concatenate([r.at_w[half, z, 3] for z in range(heads) for half in range(halves)], axis=0)
 
 
 def feed_weights(r, slot, kind):
@@ -339,7 +353,7 @@
     r.result[place, :] = hidden + r.fc_out_bias[...]
 
 
-def feed_chunk(r, slot, chunk):
+def feed_chunk(r, slot, chunk, keep):
     rows = FEED * SLOT
     blocks = r.windows // FEED
     w_in, w_out = feed_weights(r, slot, 0), feed_weights(r, slot, 1)
@@ -362,15 +376,18 @@
         d_pre = d_active * slope
         d_bias = d_bias + fold(d_pre)
         d_pre = d_pre.astype(BF16)
-        r.active[place, :] = active
-        r.d_pre[place, :] = d_pre
+        r.active[keep, place, :] = active
+        r.d_pre[keep, place, :] = d_pre
         r.result[place, :] += nn(active, w_out)
         d_normed = nn(d_pre, w_in)
         r.d_two[place, :] = d_normed if slot == 0 else r.d_two[place, :] + d_normed
     r.bias[chunk] = d_bias
+
+
+def feed_gradients(r, slot, keep):
     cores, _, heads, _, own, _ = r.g_fc.shape
-    d_in = tn(r.d_pre[...], r.normed_two[...]).astype(BF16)
-    d_out = tn(r.active[...], r.dout[...].astype(BF16)).astype(BF16)
+    d_in = tn(r.d_pre[keep], r.normed_two[...]).astype(BF16)
+    d_out = tn(r.active[keep], r.dout[...].astype(BF16)).astype(BF16)
     for core in range(cores):
         for z in range(heads):
             place = own * (heads * core + z)
@@ -468,12 +485,17 @@
     lax.fori_loop(0, dense_ref.shape[0] // rows // count, body, 0)
 
 
+def share_buffers(r):
+    r.d_two = r.field
+    r.hidden = r.field
+    r.source = r.result
+
+
 def clear(r):
     for ref in (r.g_proj, r.g_qkv, r.sums):
         ref[...] = jnp.zeros_like(ref)
     tail = r.windows * SLOT
-    for ref in (r.result, r.source):
-        ref[tail:, :] = jnp.zeros((ref.shape[0] - tail, ref.shape[1]), F32)
+    r.result[tail:, :] = jnp.zeros((r.result.shape[0] - tail, r.result.shape[1]), F32)
 
 
 def mask_result(first, r):
@@ -519,15 +541,19 @@
     lax.fori_loop(start, stop, step, 0)
 
 
-COPIES = 55
+COPIES = 65
+FEED_ORDER = (0, 3, 1, 2)
+FETCHED = ("sides", "qkv_w", "proj_w", "og", "tokens", "fc_in", "fc_out", "proj_bias", "fc_in_bias", "fc_out_bias", "gain", "shift",
+           "peg", "peg_bias")
 
 
 def fused_kernel(names, *refs):
     r = SimpleNamespace(**dict(zip(names, refs)))
     r.windows = r.mixed.shape[0] - 2 * MARGIN
+    share_buffers(r)
     blocks = r.windows // BLOCK
     own_rows = r.tokens.shape[0]
-    heads = r.at_w.shape[2]
+    heads = r.at_w.shape[1]
     quads = r.fc_w.shape[1]
     piece = r.at_w.shape[3]
     z, img = lax.axis_index("head"), lax.axis_index("img")
@@ -559,12 +585,14 @@
             device_id_type=MESH,
         )
 
-    forth = copy(r.tokens.at[own_rows - HALO : own_rows], r.halo_low, (img, z + 1))
-    back = copy(r.tokens.at[0:HALO], r.halo_high, (img, z - 1))
-    at_own = r.at_w.at[core, yx]
-    at_z = [copy(at_own.at[z], at_own.at[z], z_peer[m]) for m in z_peer]
-    at_yx = [copy(at_own, at_own, yx_peer[m]) for m in yx_peer]
-    at_core = copy(r.at_w.at[core], r.at_w.at[core], sibling)
+    forth = copy(r.tok_last, r.tok_above, (img, z + 1))
+    back = copy(r.tok_first, r.tok_below, (img, z - 1))
+    at_z = [copy(r.at_w.at[core, z, yx], r.at_w.at[core, z, yx], z_peer[m]) for m in z_peer]
+    at_yx = [
+        [copy(r.at_w.at[core, flip(z, m), yx], r.at_w.at[core, flip(z, m), yx], yx_peer[n]) for n in yx_peer]
+        for m in z_peer
+    ]
+    at_core = [copy(r.at_w.at[core, flip(z, m)], r.at_w.at[core, flip(z, m)], sibling) for m in z_peer]
     fc_own = r.fc_w.at[core, 0]
     fc_z = [copy(fc_own.at[z], fc_own.at[z], z_peer[m]) for m in z_peer]
     fc_yx = [copy(fc_own, r.fc_w.at[core, m], yx_peer[m]) for m in yx_peer]
@@ -578,8 +606,8 @@
     ga_plane = [copy(r.ga_all.at[yx, core], r.ga_all.at[yx, core], peer) for peer in plane]
     sm_plane = [copy(r.small, r.small_plane.at[yx, core], peer) for peer in plane]
     sm_z = [copy(r.small_sum, r.small_z.at[z], z_peer[m]) for m in z_peer]
-    mix_forth = copy(r.edge_out.at[0], r.edge_in.at[0], (img, z + 1))
-    mix_back = copy(r.edge_out.at[1], r.edge_in.at[1], (img, z - 1))
+    mix_forth = copy(r.mix_last, r.mix_above, (img, z + 1))
+    mix_back = copy(r.mix_first, r.mix_below, (img, z - 1))
     has_next, has_last = z < heads - 1, z > 0
 
     def start(copies):
@@ -596,20 +624,34 @@
             total = total + others[index].astype(F32)
         return total
 
-    for kind in range(4):
-        rows = r.qkv_w[kind] if kind < 3 else r.proj_w[...]
-        for half in range(2):
-            r.at_own[kind, half] = rows[piece * half : piece * (half + 1)]
-    r.at_w[core, yx, z] = r.at_own[yx, core]
-    r.fc_w[core, 0, z, 0] = r.fc_in[...]
-    r.fc_w[core, 0, z, 1] = r.fc_out[...]
     barrier = pltpu.get_barrier_semaphore()
     greeted = [z_peer[m] for m in z_peer] + plane
     for peer in greeted:
         pl.semaphore_signal(barrier, inc=1, device_id=peer, device_id_type=MESH)
+    fetched = {}
+    targets = {"qkv_w": r.at_own.at[0:3], "proj_w": r.at_own.at[3], "fc_in": r.fc_w.at[core, 0, z, 0], "fc_out": r.fc_w.at[core, 0, z, 1]}
+    for index, name in enumerate(FETCHED):
+        source = getattr(r, "far_" + name)
+        target = targets[name] if name in targets else getattr(r, name)
+        fetched[name] = pltpu.make_async_copy(source, target, r.local.at[index])
+        fetched[name].start()
+    fetched["sides"].wait()
     scan_windows(r.sides, r.info, heads * r.windows)
+    fetched["qkv_w"].wait()
+    fetched["proj_w"].wait()
+    for kind in range(4):
+        for half in range(2):
+            r.at_w[half, z, kind] = r.at_own[kind, half]
     pl.semaphore_wait(barrier, len(greeted))
     start(at_z)
+    fetched["tokens"].wait()
+    take_tokens(first, r)
+    margin = (MARGIN,) + r.ext.shape[1:]
+    end = MARGIN + r.windows
+    above, below = (MARGIN - 1, range(MARGIN - 1), WS - 1), (end, range(end + 1, end + MARGIN), 0)
+    last, foremost = (end - 1, range(end - MARGIN, end - 1), WS - 1), (MARGIN, range(MARGIN + 1, 2 * MARGIN), 0)
+    r.tok_last[...] = edge_of(r.ext, *last)
+    r.tok_first[...] = edge_of(r.ext, *foremost)
 
     @pl.when(has_next)
     def _():
@@ -619,41 +661,47 @@
     def _():
         back.start()
 
+    fetched["og"].wait()
     take_cotangent(first, r)
+    for name in FETCHED:
+        if name not in ("sides", "tokens", "og", "qkv_w", "proj_w"):
+            fetched[name].wait()
+    for one, many in zip(at_z, at_yx):
+        one.wait_recv()
+        start(many)
     start(fc_z)
     clear(r)
-    take_tokens(first, r)
-    arrive(at_z)
-    start(at_yx)
     field_pass(first, r, BLOCK, r.windows - BLOCK)
-    margin = (MARGIN,) + r.ext.shape[1:]
-
-    @pl.when(has_last)
-    def _():
-        forth.wait_recv()
-        take_margin(first, r, r.halo_low, HALO - MARGIN * CELLS, 0)
-
-    @pl.when(z == 0)
-    def _():
-        r.ext[0:MARGIN] = jnp.zeros(margin, F32)
-
-    @pl.when(has_next)
-    def _():
-        back.wait_recv()
-        take_margin(first, r, r.halo_high, 0, MARGIN + r.windows)
-
-    @pl.when(z == heads - 1)
-    def _():
-        r.ext[MARGIN + r.windows :] = jnp.zeros(margin, F32)
-
+    for many, one in zip(at_yx, at_core):
+        arrive(many)
+        one.start()
+
+    def margins(ext_ref, forth, back, from_above, from_below):
+        @pl.when(has_last)
+        def _():
+            forth.wait_recv()
+            edge_to(ext_ref, *above, from_above[...])
+
+        @pl.when(z == 0)
+        def _():
+            ext_ref[0:MARGIN] = jnp.zeros(margin, F32)
+
+        @pl.when(has_next)
+        def _():
+            back.wait_recv()
+            edge_to(ext_ref, *below, from_below[...])
+
+        @pl.when(z == heads - 1)
+        def _():
+            ext_ref[end:] = jnp.zeros(margin, F32)
+
+    margins(r.ext, forth, back, r.tok_above, r.tok_below)
     arrive(fc_z)
-    start(fc_yx)
+    start([fc_yx[m - 1] for m in FEED_ORDER[1:]])
     fc_core[0].start()
     field_pass(first, r, 0, BLOCK)
     field_pass(first, r, r.windows - BLOCK, r.windows)
-    arrive(at_yx)
-    at_core.start()
-    at_core.wait_recv()
+    arrive(at_core)
     loop(0, 2, lambda step: attention_block(first, r, step))
     for one, two in zip(fc_yx, fc_core[1:]):
         one.wait_recv()
@@ -666,59 +714,62 @@
         if m > 0:
             gf_yx[m - 1].start()
 
-    for m in range(quads):
+    sent_slot = None
+    for m in FEED_ORDER:
         fc_core[m].wait_recv()
-        feed_chunk(r, m, flip(yx, m))
-        gf_core[m].start()
+        feed_chunk(r, m, flip(yx, m), min(m, 1))
         if m > 0:
-            add_cores(m - 1)
+            feed_gradients(r, m, 1)
+            gf_core[m].start()
+            if sent_slot is not None:
+                add_cores(sent_slot)
+            sent_slot = m
 
     def attention(start, stop):
         loop(start, stop, lambda step: attention_back(first, r, step))
 
     attention(0, 1)
-    add_cores(quads - 1)
-    attention(1, 3)
+    add_cores(sent_slot)
+    attention(1, blocks)
+    turn_attention_gradients(r)
+    ga_core.start()
+
+    def field(start, stop):
+        loop(start, stop, lambda step: field_back(first, r, (step + blocks - 1) % blocks))
+
+    feed_gradients(r, 0, 0)
+    gf_core[0].start()
+    ga_core.wait_recv()
+    r.ga_two[...] = (r.g_at[core].astype(F32) + r.ga_one[...].astype(F32)).astype(BF16)
+    start(ga_yx)
+    field(0, 2)
+    r.mix_last[...] = edge_of(r.mixed, *last)
+    r.mix_first[...] = edge_of(r.mixed, *foremost)
+
+    @pl.when(has_next)
+    def _():
+        mix_forth.start()
+
+    @pl.when(has_last)
+    def _():
+        mix_back.start()
+
+    add_cores(0)
     arrive(gf_yx)
     r.gf_four[...] = total_of(r.gf_two[0], r.gf_three).astype(BF16)
     start(gf_z)
-    attention(3, blocks)
-    turn_attention_gradients(r)
-    ga_core.start()
-
-    def field(start, stop):
-        loop(start, stop, lambda step: field_back(first, r, (step + blocks - 1) % blocks))
-
-    field(0, 2)
-    edge = EDGE * SLOT
-    last = r.mixed[MARGIN + r.windows - EDGE : MARGIN + r.windows]
-    r.edge_out[0] = last.reshape(edge, -1).astype(BF16)
-    r.edge_out[1] = r.mixed[MARGIN : MARGIN + EDGE].reshape(edge, -1).astype(BF16)
-
-    @pl.when(has_next)
-    def _():
-        mix_forth.start()
-
-    @pl.when(has_last)
-    def _():
-        mix_back.start()
-
-    ga_core.wait_recv()
-    r.ga_two[...] = (r.g_at[core].astype(F32) + r.ga_one[...].astype(F32)).astype(BF16)
-    start(ga_yx)
     field(2, blocks)
     collect_small(r)
+    arrive(ga_yx)
+    r.ga_four[...] = total_of(r.ga_two[yx], r.ga_three).astype(BF16)
+    start(ga_z)
     start(sm_plane)
     mask_result(first, r)
     shrink(r.result, r.output, False)
-    arrive(gf_z)
-    total = total_of(r.gf_four[z], r.gf_five)
-    r.d_fc_in[...] = total[0]
-    r.d_fc_out[...] = total[1]
     token_pass(first, r, BLOCK, r.windows - BLOCK)
-    arrive(ga_yx)
-    r.ga_four[...] = total_of(r.ga_two[yx], r.ga_three).astype(BF16)
-    start(ga_z)
+    arrive(ga_z)
+    r.ga_all[yx, core] = total_of(r.ga_four[z], r.ga_five).astype(BF16)
+    start(ga_plane)
     arrive(sm_plane)
     r.small_plane[yx, core] = r.small[...]
     total = jnp.zeros(r.small.shape, F32)
@@ -727,32 +778,14 @@
             total = total + r.small_plane[a, b]
     r.small_sum[...] = total
     start(sm_z)
-    skip = (EDGE - MARGIN) * SLOT
-
-    @pl.when(has_last)
-    def _():
-        mix_forth.wait_recv()
-        r.mixed[0:MARGIN] = r.edge_in[0].astype(F32)[skip:].reshape(margin)
-
-    @pl.when(z == 0)
-    def _():
-        r.mixed[0:MARGIN] = jnp.zeros(margin, F32)
-
-    @pl.when(has_next)
-    def _():
-        mix_back.wait_recv()
-        r.mixed[MARGIN + r.windows :] = r.edge_in[1].astype(F32)[0 : MARGIN * SLOT].reshape(margin)
-
-    @pl.when(z == heads - 1)
-    def _():
-        r.mixed[MARGIN + r.windows :] = jnp.zeros(margin, F32)
-
+    margins(r.mixed, mix_forth, mix_back, r.mix_above, r.mix_below)
     token_pass(first, r, 0, BLOCK)
     token_pass(first, r, r.windows - BLOCK, r.windows)
-    arrive(ga_z)
-    r.ga_all[yx, core] = total_of(r.ga_four[z], r.ga_five).astype(BF16)
-    start(ga_plane)
     shrink(r.source, r.d_tokens, True)
+    arrive(gf_z)
+    total = total_of(r.gf_four[z], r.gf_five)
+    r.d_fc_in[...] = total[0]
+    r.d_fc_out[...] = total[1]
     arrive(sm_z)
     r.small_z[z] = r.small_sum[...]
     total = jnp.zeros(r.small.shape, F32)
@@ -769,7 +802,7 @@
             else:
                 r.d_proj[place, :] = rows
 
-    sent = at_z + at_yx + [at_core] + fc_z + fc_yx + fc_core + gf_core + gf_yx + gf_z + [ga_core] + ga_yx + ga_z
+    sent = at_z + sum(at_yx, []) + at_core + fc_z + fc_yx + fc_core + gf_core + gf_yx + gf_z + [ga_core] + ga_yx + ga_z
     for one in sent + ga_plane + sm_plane + sm_z:
         one.wait_send()
 
@@ -787,9 +820,10 @@
 def local_kernel(names, *refs):
     r = SimpleNamespace(**dict(zip(names, refs)))
     r.windows = r.mixed.shape[0] - 2 * MARGIN
+    share_buffers(r)
     blocks = r.windows // BLOCK
     first = lax.axis_index("head") * r.windows
-    scan_windows(r.sides, r.info, r.at_w.shape[2] * r.windows)
+    scan_windows(r.sides, r.info, r.at_w.shape[1] * r.windows)
     clear(r)
     take_cotangent(first, r)
     take_tokens(first, r)
@@ -798,7 +832,8 @@
     field_pass(first, r, 0, r.windows)
     loop(0, blocks, lambda step: attention_block(first, r, step))
     for chunk in range(r.fc_w.shape[1]):
-        feed_chunk(r, chunk, chunk)
+        feed_chunk(r, chunk, chunk, 0)
+        feed_gradients(r, chunk, 0)
     loop(0, blocks, lambda step: attention_back(first, r, step))
     loop(0, blocks, lambda step: field_back(first, r, step))
     turn_attention_gradients(r)
@@ -842,15 +877,12 @@
         "qkv": pltpu.VMEM((windows, TALL, 3 * width), BF16),
         "probs": pltpu.VMEM((windows, TALL, 2 * width), F32),
         "context": pltpu.VMEM((padded, width), BF16),
-        "hidden": pltpu.VMEM((padded, width), F32),
         "result": pltpu.VMEM((extra, width), F32),
-        "source": pltpu.VMEM((extra, width), F32),
         "scaled_two": pltpu.VMEM((padded, width), F32),
         "inverse_two": pltpu.VMEM((padded, 1), F32),
         "normed_two": pltpu.VMEM((padded, width), BF16),
-        "d_two": pltpu.VMEM((padded, width), F32),
-        "active": pltpu.VMEM((padded, 256), BF16),
-        "d_pre": pltpu.VMEM((padded, 256), BF16),
+        "active": pltpu.VMEM((2, padded, 256), BF16),
+        "d_pre": pltpu.VMEM((2, padded, 256), BF16),
         "d_parts": pltpu.VMEM((padded, 3 * width), BF16),
         "g_proj": pltpu.VMEM((width, width), F32),
         "g_qkv": pltpu.VMEM((3 * width, width), F32),
@@ -859,12 +891,12 @@
     }
 
 
-def call(kernel, name, inputs, outputs, scratch, **params):
+def call(kernel, name, inputs, outputs, scratch, specs=None, **params):
     names = list(inputs) + list(outputs) + list(scratch)
     results = pl.pallas_call(
         functools.partial(kernel, names),
         out_shape=tuple(outputs.values()),
-        in_specs=[smem()] + [vmem()] * (len(inputs) - 1),
+        in_specs=specs or [smem()] + [vmem()] * (len(inputs) - 1),
         out_specs=(vmem(),) * len(outputs),
         scratch_shapes=list(scratch.values()),
         compiler_params=pltpu.CompilerParams(vmem_limit_bytes=VMEM_LIMIT, **params),
@@ -902,7 +934,7 @@
             "halo_low": halo[0],
             "halo_high": halo[1],
             "og": out_grad,
-            "at_w": at_w.reshape(4, heads, 2, piece, width).transpose(2, 0, 1, 3, 4),
+            "at_w": at_w.reshape(4, heads, 2, piece, width).transpose(2, 1, 0, 3, 4),
             "fc_w": fc_w.reshape(2, hidden // 256, 2, heads, own, width).transpose(2, 1, 3, 0, 4, 5),
             "proj_bias": proj_bias[None],
             "fc_in_bias": fc_in_bias.reshape(-1, 1, 256),
@@ -927,12 +959,13 @@
     back = lax.ppermute(mixed[start : start + MARGIN].astype(BF16), "head", [(i + 1, i) for i in range(heads - 1)])
     own = mixed[MARGIN : MARGIN + windows]
     mixed = jnp.concatenate([forth.astype(F32), own, back.astype(F32)], axis=0)
+    buffers = work_buffers(windows, heads, width, hidden)
     d_tokens = call(
         token_kernel,
         "tokens",
         {"sides": image_sides, "mixed": mixed, "peg": peg_weight},
         {"d_tokens": shape((own_rows, width), F32)},
-        {name: work_buffers(windows, heads, width, hidden)[name] for name in ("info", "source")},
+        {"info": buffers["info"], "source": buffers["result"]},
     )["d_tokens"]
     everywhere = ("img", "head")
     d_fc_in, d_fc_out = (
@@ -963,8 +996,8 @@
         "sides": image_sides,
         "tokens": tokens,
         "og": out_grad,
-        "qkv_w": jnp.swapaxes(qkv_weight, 1, 2),
-        "proj_w": proj_weight,
+        "qkv_w": jnp.swapaxes(qkv_weight, 1, 2).reshape(3, 2, piece, width),
+        "proj_w": proj_weight.reshape(2, piece, width),
         "fc_in": fc_in,
         "fc_out": fc_out,
         "proj_bias": proj_bias[None],
@@ -984,14 +1017,17 @@
         "d_fc_out": shape(fc_out.shape, F32),
     }
     scratch = work_buffers(windows, heads, width, hidden)
+    scratch["sides"] = pltpu.SMEM(image_sides.shape, jnp.int32)
+    for kind in ("tok", "mix"):
+        for place in ("last", "first", "above", "below"):
+            scratch[kind + "_" + place] = pltpu.VMEM((EDGE, width), BF16)
+    for name in FETCHED:
+        if name not in ("sides", "qkv_w", "proj_w", "fc_in", "fc_out"):
+            scratch[name] = pltpu.VMEM(inputs[name].shape, inputs[name].dtype)
     scratch.update({
-        "halo_low": pltpu.VMEM((HALO, width), BF16),
-        "halo_high": pltpu.VMEM((HALO, width), BF16),
         "ext": pltpu.VMEM((windows + 2 * MARGIN, WS, 8, width), F32),
         "mixed": pltpu.VMEM((windows + 2 * MARGIN, WS, 8, width), F32),
-        "edge_out": pltpu.VMEM((2, EDGE * SLOT, width), BF16),
-        "edge_in": pltpu.VMEM((2, EDGE * SLOT, width), BF16),
-        "at_w": pltpu.VMEM((2, 4, heads, piece, width), BF16),
+        "at_w": pltpu.VMEM((2, heads, 4, piece, width), BF16),
         "at_own": pltpu.VMEM((4, 2, piece, width), BF16),
         "fc_w": pltpu.VMEM((2, quads, heads, 2, own, width), BF16),
         "g_fc": pltpu.VMEM((2, quads, heads, 2, own, width), BF16),
@@ -1011,15 +1047,17 @@
         "small_sum": pltpu.VMEM((SMALL, width), F32),
         "small_z": pltpu.VMEM((heads, SMALL, width), F32),
         "small": pltpu.VMEM((SMALL, width), F32),
+        "local": pltpu.SemaphoreType.DMA((len(FETCHED),)),
         "send": pltpu.SemaphoreType.DMA((COPIES,)),
         "recv": pltpu.SemaphoreType.DMA((COPIES,)),
     })
     made = call(
         fused_kernel,
         "block",
-        inputs,
+        {"far_" + name: inputs[name] for name in FETCHED},
         dict(large, small_out=shape((SMALL, width), F32)),
         scratch,
+        [pl.BlockSpec(memory_space=pltpu.HBM)] * len(FETCHED),
         collective_id=0,
         has_side_effects=True,
     )

time: 66.1 us -> 63.1 us (0.955)
  Pallas kernels: 65.1 us -> 62.1 us
    pallas_call x1, Pallas kernels: 61.8 us -> 58.8 us  [call(): pl.pallas_call(functools.partial(kernel, names), out_shape=tuple(outputs....]
where the time goes in v4:
time: 63.1 us; the launch traced here: 63 us
  Pallas kernels  62.1 us (98%)
  between operations  0.84 us (1%)
    pallas_call x1, Pallas kernels, call(): pl.pallas_call(functools.partial(kernel, names), out_shape=tuple(outputs....  58.8 us
    pallas_call x1, Pallas kernels, on_device(): pl.pallas_call(hand_out, out_shape=tuple(large.values()) + tuple(small.va...  3.33 us

profile of v4, /device:TPU:0, one launch (start us, length us, event | category | flops | bytes accessed | tf_op | source)
XLA Modules:
  0.0 63.0 jit_solution(5338072716587072333)
XLA Ops:
  0.7 58.8 %block.1 = (bf16[1568,256]{1,0:T(8,128)(2,1)}, f32[1568,256]{1,0:T(8,128)}, f32[3,64,256]{2,1,0:T(8,128)}, f32[64,256]{1,0:T(8,128)}, f32[32,256]{1,0:T(8,128)}, /*index=5*/f32[32,256]{1,0:T(8,128)}, f32[24,256]{1,0:T(8,128)}) custom-call(s32[1,32]{1,0:T(1,128)} %refs_0_.1, bf16[3,2,32,256]{3,2,1,0:T(8,128)(2,1)} %bitcast.13, bf16[2,32,256]{2,1,0:T(8,128)(2,1)} %bitcast.14, ...), custom_call_target="tpu_custom_call" | custom-call | tf_op jit(solution)/shard_map/block/pallas_call | solution.py:896
  59.5 3.3 %hand_out.1 = (bf16[1568,256]{1,0:T(8,128)(2,1)}, f32[1568,256]{1,0:T(8,128)}, f32[3,64,256]{2,1,0:T(8,128)}, f32[64,256]{1,0:T(8,128)}, f32[32,256]{1,0:T(8,128...) custom-call(bf16[1568,256]{1,0:T(8,128)(2,1)} %get-tuple-element.33., ...), custom_call_target="tpu_custom_call" | custom-call | tf_op jit(solution)/shard_map/hand_out/pallas_call | solution.py:1086

commit v5 on v4

--- a/solution.py
+++ b/solution.py
@@ -22,7 +22,8 @@
 EDGE = 96
 OFFSET = 8
 BLOCK = 8
-FEED = 8
+FEED = 16
+ATTEND = 16
 SPAN = 4
 SMALL = 24
 VMEM_LIMIT = 56 * 1024 * 1024
@@ -229,11 +230,13 @@
         windows = [BLOCK * step + i for i in range(BLOCK)]
         limits = [window_of(r.info, first + window)[3:] for window in windows]
         starts = [CELLS * window for window in windows]
+        total = carry
         for window, rows in zip(windows, expand(r.og, starts, limits)):
             r.dout[rows_at(window, SLOT), :] = rows
-        return carry
-
-    lax.fori_loop(0, r.windows // BLOCK, cotangent, 0)
+            total = total + fold(rows)
+        return total
+
+    r.sums[1] = lax.fori_loop(0, r.windows // BLOCK, cotangent, jnp.zeros(r.sums.shape[1:], F32))
 
 
 def field_pass(first, r, start, stop):
@@ -334,12 +337,12 @@
 
 
 def attention_block(first, r, step):
-    rows = BLOCK * SLOT
+    rows = ATTEND * SLOT
     place = rows_at(step, rows)
-    windows = [BLOCK * step + sub for sub in range(BLOCK)]
+    windows = [ATTEND * step + sub for sub in range(ATTEND)]
     limits = [window_of(r.info, first + window)[3:] for window in windows]
     projected = nt(r.normed[place, :], qkv_weights(r))
-    qkvs = [to_tall(projected[SLOT * sub : SLOT * (sub + 1)]) for sub in range(BLOCK)]
+    qkvs = [to_tall(projected[SLOT * sub : SLOT * (sub + 1)]) for sub in range(ATTEND)]
     for window, qkv in zip(windows, qkvs):
         r.qkv[window] = qkv
     context = attend(qkvs, limits, r.probs, windows)
@@ -376,9 +379,8 @@
         d_pre = d_active * slope
         d_bias = d_bias + fold(d_pre)
         d_pre = d_pre.astype(BF16)
-        r.active[keep, place, :] = active
+        r.active[slot, place, :] = active
         r.d_pre[keep, place, :] = d_pre
-        r.result[place, :] += nn(active, w_out)
         d_normed = nn(d_pre, w_in)
         r.d_two[place, :] = d_normed if slot == 0 else r.d_two[place, :] + d_normed
     r.bias[chunk] = d_bias
@@ -387,7 +389,7 @@
 def feed_gradients(r, slot, keep):
     cores, _, heads, _, own, _ = r.g_fc.shape
     d_in = tn(r.d_pre[keep], r.normed_two[...]).astype(BF16)
-    d_out = tn(r.active[keep], r.dout[...].astype(BF16)).astype(BF16)
+    d_out = tn(r.active[slot], r.dout[...].astype(BF16)).astype(BF16)
     for core in range(cores):
         for z in range(heads):
             place = own * (heads * core + z)
@@ -396,9 +398,9 @@
 
 
 def attention_back(first, r, step):
-    rows = BLOCK * SLOT
+    rows = ATTEND * SLOT
     place = rows_at(step, rows)
-    windows = [BLOCK * step + sub for sub in range(BLOCK)]
+    windows = [ATTEND * step + sub for sub in range(ATTEND)]
     d_output = r.dout[place, :]
     scaled = r.scaled_two[place, :]
     d_normed = r.d_two[place, :]
@@ -406,10 +408,9 @@
     r.hidden[place, :] = d_hidden
     d_branch = d_hidden.astype(BF16)
     d_context = nt(d_branch, proj_weights(r))
-    d_context = [to_tall(d_context[SLOT * sub : SLOT * (sub + 1)]) for sub in range(BLOCK)]
+    d_context = [to_tall(d_context[SLOT * sub : SLOT * (sub + 1)]) for sub in range(ATTEND)]
     r.g_proj[...] += tn(r.context[place, :], d_branch)
     r.sums[0] += fold(d_branch.astype(F32))
-    r.sums[1] += fold(d_output)
     r.sums[3] += fold(d_normed * scaled)
     r.sums[5] += fold(d_normed)
     d_qkv = attend_back([r.qkv[window] for window in windows], d_context, r.probs, windows)
@@ -498,15 +499,20 @@
     r.result[tail:, :] = jnp.zeros((r.result.shape[0] - tail, r.result.shape[1]), F32)
 
 
-def mask_result(first, r):
+def finish_result(first, r):
+    weights = [feed_weights(r, slot, 1) for slot in range(r.fc_w.shape[1])]
+
     def body(step, carry):
+        place = rows_at(step, BLOCK * SLOT)
+        total = r.result[place, :]
+        for slot, w_out in enumerate(weights):
+            total = total + nn(r.active[slot, place, :], w_out)
         for sub in range(BLOCK):
             window = BLOCK * step + sub
             _, _, _, high, wide = window_of(r.info, first + window)
-            place = rows_at(window, SLOT)
-            cells = r.result[place, :].reshape(WS, 8, -1)
+            cells = total[SLOT * sub : SLOT * (sub + 1)].reshape(WS, 8, -1)
             cells = jnp.where(valid_cells(high, wide, cells.shape[-1]), cells, 0.0)
-            r.result[place, :] = cells.reshape(SLOT, -1)
+            r.result[rows_at(window, SLOT), :] = cells.reshape(SLOT, -1)
         return carry
 
     lax.fori_loop(0, r.windows // BLOCK, body, 0)
@@ -644,8 +650,11 @@
             r.at_w[half, z, kind] = r.at_own[kind, half]
     pl.semaphore_wait(barrier, len(greeted))
     start(at_z)
+    fetched["fc_in"].wait()
+    fetched["fc_out"].wait()
     fetched["tokens"].wait()
     take_tokens(first, r)
+    start(fc_z)
     margin = (MARGIN,) + r.ext.shape[1:]
     end = MARGIN + r.windows
     above, below = (MARGIN - 1, range(MARGIN - 1), WS - 1), (end, range(end + 1, end + MARGIN), 0)
@@ -662,19 +671,17 @@
         back.start()
 
     fetched["og"].wait()
+    clear(r)
     take_cotangent(first, r)
-    for name in FETCHED:
-        if name not in ("sides", "tokens", "og", "qkv_w", "proj_w"):
-            fetched[name].wait()
     for one, many in zip(at_z, at_yx):
         one.wait_recv()
         start(many)
-    start(fc_z)
-    clear(r)
+    for name in FETCHED[7:]:
+        fetched[name].wait()
     field_pass(first, r, BLOCK, r.windows - BLOCK)
-    for many, one in zip(at_yx, at_core):
-        arrive(many)
-        one.start()
+    arrive(fc_z)
+    start([fc_yx[m - 1] for m in FEED_ORDER[1:]])
+    fc_core[0].start()
 
     def margins(ext_ref, forth, back, from_above, from_below):
         @pl.when(has_last)
@@ -696,17 +703,17 @@
             ext_ref[end:] = jnp.zeros(margin, F32)
 
     margins(r.ext, forth, back, r.tok_above, r.tok_below)
-    arrive(fc_z)
-    start([fc_yx[m - 1] for m in FEED_ORDER[1:]])
-    fc_core[0].start()
     field_pass(first, r, 0, BLOCK)
     field_pass(first, r, r.windows - BLOCK, r.windows)
+    for many, one in zip(at_yx, at_core):
+        arrive(many)
+        one.start()
     arrive(at_core)
-    loop(0, 2, lambda step: attention_block(first, r, step))
-    for one, two in zip(fc_yx, fc_core[1:]):
-        one.wait_recv()
-        two.start()
-    loop(2, blocks, lambda step: attention_block(first, r, step))
+    steps = r.windows // ATTEND
+    loop(0, steps, lambda step: attention_block(first, r, step))
+    for m in FEED_ORDER[1:]:
+        fc_yx[m - 1].wait_recv()
+        fc_core[m].start()
 
     def add_cores(m):
         gf_core[m].wait_recv()
@@ -730,7 +737,7 @@
 
     attention(0, 1)
     add_cores(sent_slot)
-    attention(1, blocks)
+    attention(1, steps)
     turn_attention_gradients(r)
     ga_core.start()
 
@@ -764,8 +771,13 @@
     r.ga_four[...] = total_of(r.ga_two[yx], r.ga_three).astype(BF16)
     start(ga_z)
     start(sm_plane)
-    mask_result(first, r)
+    finish_result(first, r)
     shrink(r.result, r.output, False)
+    written = [
+        pltpu.make_async_copy(r.output, r.far_output, r.written.at[0]),
+        pltpu.make_async_copy(r.d_tokens, r.far_d_tokens, r.written.at[1]),
+    ]
+    written[0].start()
     token_pass(first, r, BLOCK, r.windows - BLOCK)
     arrive(ga_z)
     r.ga_all[yx, core] = total_of(r.ga_four[z], r.ga_five).astype(BF16)
@@ -782,6 +794,7 @@
     token_pass(first, r, 0, BLOCK)
     token_pass(first, r, r.windows - BLOCK, r.windows)
     shrink(r.source, r.d_tokens, True)
+    written[1].start()
     arrive(gf_z)
     total = total_of(r.gf_four[z], r.gf_five)
     r.d_fc_in[...] = total[0]
@@ -802,6 +815,8 @@
             else:
                 r.d_proj[place, :] = rows
 
+    for one in written:
+        one.wait()
     sent = at_z + sum(at_yx, []) + at_core + fc_z + fc_yx + fc_core + gf_core + gf_yx + gf_z + [ga_core] + ga_yx + ga_z
     for one in sent + ga_plane + sm_plane + sm_z:
         one.wait_send()
@@ -830,15 +845,15 @@
     take_margin(first, r, r.halo_low, HALO - MARGIN * CELLS, 0)
     take_margin(first, r, r.halo_high, 0, MARGIN + r.windows)
     field_pass(first, r, 0, r.windows)
-    loop(0, blocks, lambda step: attention_block(first, r, step))
+    loop(0, r.windows // ATTEND, lambda step: attention_block(first, r, step))
     for chunk in range(r.fc_w.shape[1]):
         feed_chunk(r, chunk, chunk, 0)
         feed_gradients(r, chunk, 0)
-    loop(0, blocks, lambda step: attention_back(first, r, step))
+    loop(0, r.windows // ATTEND, lambda step: attention_back(first, r, step))
     loop(0, blocks, lambda step: field_back(first, r, step))
     turn_attention_gradients(r)
     collect_small(r)
-    mask_result(first, r)
+    finish_result(first, r)
     shrink(r.result, r.output, False)
     for edge in (slice(0, MARGIN), slice(MARGIN + r.windows, 2 * MARGIN + r.windows)):
         r.mixed[edge] = jnp.zeros((MARGIN,) + r.mixed.shape[1:], F32)
@@ -881,7 +896,7 @@
         "scaled_two": pltpu.VMEM((padded, width), F32),
         "inverse_two": pltpu.VMEM((padded, 1), F32),
         "normed_two": pltpu.VMEM((padded, width), BF16),
-        "active": pltpu.VMEM((2, padded, 256), BF16),
+        "active": pltpu.VMEM((hidden // 256, padded, 256), BF16),
         "d_pre": pltpu.VMEM((2, padded, 256), BF16),
         "d_parts": pltpu.VMEM((padded, 3 * width), BF16),
         "g_proj": pltpu.VMEM((width, width), F32),
@@ -891,13 +906,13 @@
     }
 
 
-def call(kernel, name, inputs, outputs, scratch, specs=None, **params):
+def call(kernel, name, inputs, outputs, scratch, specs=None, out_specs=None, **params):
     names = list(inputs) + list(outputs) + list(scratch)
     results = pl.pallas_call(
         functools.partial(kernel, names),
         out_shape=tuple(outputs.values()),
         in_specs=specs or [smem()] + [vmem()] * (len(inputs) - 1),
-        out_specs=(vmem(),) * len(outputs),
+        out_specs=out_specs or (vmem(),) * len(outputs),
         scratch_shapes=list(scratch.values()),
         compiler_params=pltpu.CompilerParams(vmem_limit_bytes=VMEM_LIMIT, **params),
         name=name,
@@ -1047,17 +1062,24 @@
         "small_sum": pltpu.VMEM((SMALL, width), F32),
         "small_z": pltpu.VMEM((heads, SMALL, width), F32),
         "small": pltpu.VMEM((SMALL, width), F32),
+        "output": pltpu.VMEM((own_rows, width), BF16),
+        "d_tokens": pltpu.VMEM((own_rows, width), F32),
+        "written": pltpu.SemaphoreType.DMA((2,)),
         "local": pltpu.SemaphoreType.DMA((len(FETCHED),)),
         "send": pltpu.SemaphoreType.DMA((COPIES,)),
         "recv": pltpu.SemaphoreType.DMA((COPIES,)),
     })
+    far = pl.BlockSpec(memory_space=pltpu.HBM)
+    made = {"far_" + name if name in ("output", "d_tokens") else name: array for name, array in large.items()}
+    made["small_out"] = shape((SMALL, width), F32)
     made = call(
         fused_kernel,
         "block",
         {"far_" + name: inputs[name] for name in FETCHED},
-        dict(large, small_out=shape((SMALL, width), F32)),
+        made,
         scratch,
-        [pl.BlockSpec(memory_space=pltpu.HBM)] * len(FETCHED),
+        [far] * len(FETCHED),
+        tuple(far if name.startswith("far_") else vmem() for name in made),
         collective_id=0,
         has_side_effects=True,
     )
@@ -1083,11 +1105,20 @@
                 target[:, width * part : width * (part + 1)] = sources[count][row : row + rows, :]
                 row += rows
 
+    parts = 2
+
+    def spec(array, cut):
+        shape = array.shape
+        block = (shape[0] // parts,) + tuple(shape[1:]) if cut else shape
+        return pl.BlockSpec(block, lambda i: (i if cut else 0,) + (0,) * (len(shape) - 1))
+
+    cuts = {"output", "d_tokens"}
     results = pl.pallas_call(
         hand_out,
+        grid=(parts,),
         out_shape=tuple(large.values()) + tuple(small.values()),
-        in_specs=[vmem()] * (count + 1),
-        out_specs=(vmem(),) * (count + len(small)),
+        in_specs=[spec(array, name.startswith("far_")) for name, array in made.items()],
+        out_specs=tuple(spec(array, name in cuts) for name, array in {**large, **small}.items()),
         compiler_params=pltpu.CompilerParams(vmem_limit_bytes=VMEM_LIMIT),
         name="hand_out",
     )(*made.values())

time: 63.1 us -> 57.9 us (0.918)
  Pallas kernels: 62.1 us -> 56.9 us
    pallas_call x1, Pallas kernels: 58.8 us -> 53.8 us  [call(): pl.pallas_call(functools.partial(kernel, names), out_shape=tuple(outputs....]
where the time goes in v5:
time: 57.9 us; the launch traced here: 57.7 us
  Pallas kernels  56.9 us (98%)
  between operations  0.84 us (1%)
    pallas_call x1, Pallas kernels, call(): pl.pallas_call(functools.partial(kernel, names), out_shape=tuple(outputs....  53.8 us
    pallas_call x1, Pallas kernels, on_device(): pl.pallas_call(hand_out, grid=(parts,), out_shape=tuple(large.values()) +...  3.04 us

profile of v5, /device:TPU:0, one launch (start us, length us, event | category | flops | bytes accessed | tf_op | source)
XLA Modules:
  0.0 57.7 jit_solution(1338517494353642343)
XLA Ops:
  0.7 53.8 %block.1 = (bf16[1568,256]{1,0:T(8,128)(2,1)}, f32[1568,256]{1,0:T(8,128)}, f32[3,64,256]{2,1,0:T(8,128)}, f32[64,256]{1,0:T(8,128)}, f32[32,256]{1,0:T(8,128)}, /*index=5*/f32[32,256]{1,0:T(8,128)}, f32[24,256]{1,0:T(8,128)}) custom-call(s32[1,32]{1,0:T(1,128)} %refs_0_.1, bf16[3,2,32,256]{3,2,1,0:T(8,128)(2,1)} %bitcast.13, bf16[2,32,256]{2,1,0:T(8,128)(2,1)} %bitcast.14, ...), custom_call_target="tpu_custom_call" | custom-call | tf_op jit(solution)/shard_map/block/pallas_call | solution.py:911
  54.5 3.0 %hand_out.1 = (bf16[1568,256]{1,0:T(8,128)(2,1)}, f32[1568,256]{1,0:T(8,128)}, f32[3,64,256]{2,1,0:T(8,128)}, f32[64,256]{1,0:T(8,128)}, f32[32,256]{1,0:T(8,128...) custom-call(bf16[1568,256]{1,0:T(8,128)(2,1)} %get-tuple-element.33., ...), custom_call_target="tpu_custom_call" | custom-call | tf_op jit(solution)/shard_map/hand_out/pallas_call | solution.py:1116

commit v6 on v5

--- a/solution.py
+++ b/solution.py
@@ -22,8 +22,8 @@
 EDGE = 96
 OFFSET = 8
 BLOCK = 8
-FEED = 16
-ATTEND = 16
+FEED = 32
+ATTEND = 32
 SPAN = 4
 SMALL = 24
 VMEM_LIMIT = 56 * 1024 * 1024
@@ -397,7 +397,7 @@
             r.g_fc[core, slot, z, 1] = d_out[place : place + own]
 
 
-def attention_back(first, r, step):
+def attention_back(first, r, step, between=None):
     rows = ATTEND * SLOT
     place = rows_at(step, rows)
     windows = [ATTEND * step + sub for sub in range(ATTEND)]
@@ -408,6 +408,8 @@
     r.hidden[place, :] = d_hidden
     d_branch = d_hidden.astype(BF16)
     d_context = nt(d_branch, proj_weights(r))
+    if between is not None:
+        between()
     d_context = [to_tall(d_context[SLOT * sub : SLOT * (sub + 1)]) for sub in range(ATTEND)]
     r.g_proj[...] += tn(r.context[place, :], d_branch)
     r.sums[0] += fold(d_branch.astype(F32))
@@ -548,7 +550,7 @@
 
 
 COPIES = 65
-FEED_ORDER = (0, 3, 1, 2)
+FEED_ORDER = (0, 1, 2, 3)
 FETCHED = ("sides", "qkv_w", "proj_w", "og", "tokens", "fc_in", "fc_out", "proj_bias", "fc_in_bias", "fc_out_bias", "gain", "shift",
            "peg", "peg_bias")
 
@@ -641,8 +643,6 @@
         target = targets[name] if name in targets else getattr(r, name)
         fetched[name] = pltpu.make_async_copy(source, target, r.local.at[index])
         fetched[name].start()
-    fetched["sides"].wait()
-    scan_windows(r.sides, r.info, heads * r.windows)
     fetched["qkv_w"].wait()
     fetched["proj_w"].wait()
     for kind in range(4):
@@ -652,9 +652,11 @@
     start(at_z)
     fetched["fc_in"].wait()
     fetched["fc_out"].wait()
+    start(fc_z)
+    fetched["sides"].wait()
+    scan_windows(r.sides, r.info, heads * r.windows)
     fetched["tokens"].wait()
     take_tokens(first, r)
-    start(fc_z)
     margin = (MARGIN,) + r.ext.shape[1:]
     end = MARGIN + r.windows
     above, below = (MARGIN - 1, range(MARGIN - 1), WS - 1), (end, range(end + 1, end + MARGIN), 0)
@@ -710,7 +712,8 @@
         one.start()
     arrive(at_core)
     steps = r.windows // ATTEND
-    loop(0, steps, lambda step: attention_block(first, r, step))
+    for step in range(steps):
+        attention_block(first, r, step)
     for m in FEED_ORDER[1:]:
         fc_yx[m - 1].wait_recv()
         fc_core[m].start()
@@ -732,12 +735,9 @@
                 add_cores(sent_slot)
             sent_slot = m
 
-    def attention(start, stop):
-        loop(start, stop, lambda step: attention_back(first, r, step))
-
-    attention(0, 1)
-    add_cores(sent_slot)
-    attention(1, steps)
+    attention_back(first, r, 0, lambda: add_cores(sent_slot))
+    for step in range(1, steps):
+        attention_back(first, r, step)
     turn_attention_gradients(r)
     ga_core.start()
 
@@ -767,10 +767,10 @@
     start(gf_z)
     field(2, blocks)
     collect_small(r)
+    start(sm_plane)
     arrive(ga_yx)
     r.ga_four[...] = total_of(r.ga_two[yx], r.ga_three).astype(BF16)
     start(ga_z)
-    start(sm_plane)
     finish_result(first, r)
     shrink(r.result, r.output, False)
     written = [
@@ -845,11 +845,13 @@
     take_margin(first, r, r.halo_low, HALO - MARGIN * CELLS, 0)
     take_margin(first, r, r.halo_high, 0, MARGIN + r.windows)
     field_pass(first, r, 0, r.windows)
-    loop(0, r.windows // ATTEND, lambda step: attention_block(first, r, step))
+    for step in range(r.windows // ATTEND):
+        attention_block(first, r, step)
     for chunk in range(r.fc_w.shape[1]):
         feed_chunk(r, chunk, chunk, 0)
         feed_gradients(r, chunk, 0)
-    loop(0, r.windows // ATTEND, lambda step: attention_back(first, r, step))
+    for step in range(r.windows // ATTEND):
+        attention_back(first, r, step)
     loop(0, blocks, lambda step: field_back(first, r, step))
     turn_attention_gradients(r)
     collect_small(r)

time: 57.9 us -> 56.7 us (0.979)
  Pallas kernels: 56.9 us -> 55.7 us
    pallas_call x1, Pallas kernels: 53.8 us -> 52.7 us  [call(): pl.pallas_call(functools.partial(kernel, names), out_shape=tuple(outputs....]
where the time goes in v6:
time: 56.7 us; the launch traced here: 56.5 us
  Pallas kernels  55.7 us (98%)
  between operations  0.82 us (1%)
    pallas_call x1, Pallas kernels, call(): pl.pallas_call(functools.partial(kernel, names), out_shape=tuple(outputs....  52.7 us
    pallas_call x1, Pallas kernels, on_device(): pl.pallas_call(hand_out, grid=(parts,), out_shape=tuple(large.values()) +...  3.04 us

profile of v6, /device:TPU:0, one launch (start us, length us, event | category | flops | bytes accessed | tf_op | source)
XLA Modules:
  0.0 56.5 jit_solution(7872847330579462664)
XLA Ops:
  0.7 52.7 %block.1 = (bf16[1568,256]{1,0:T(8,128)(2,1)}, f32[1568,256]{1,0:T(8,128)}, f32[3,64,256]{2,1,0:T(8,128)}, f32[64,256]{1,0:T(8,128)}, f32[32,256]{1,0:T(8,128)}, /*index=5*/f32[32,256]{1,0:T(8,128)}, f32[24,256]{1,0:T(8,128)}) custom-call(s32[1,32]{1,0:T(1,128)} %refs_0_.1, bf16[3,2,32,256]{3,2,1,0:T(8,128)(2,1)} %bitcast.13, bf16[2,32,256]{2,1,0:T(8,128)(2,1)} %bitcast.14, ...), custom_call_target="tpu_custom_call" | custom-call | tf_op jit(solution)/shard_map/block/pallas_call | solution.py:913
  53.3 3.0 %hand_out.1 = (bf16[1568,256]{1,0:T(8,128)(2,1)}, f32[1568,256]{1,0:T(8,128)}, f32[3,64,256]{2,1,0:T(8,128)}, f32[64,256]{1,0:T(8,128)}, f32[32,256]{1,0:T(8,128...) custom-call(bf16[1568,256]{1,0:T(8,128)(2,1)} %get-tuple-element.33., ...), custom_call_target="tpu_custom_call" | custom-call | tf_op jit(solution)/shard_map/hand_out/pallas_call | solution.py:1118
